TPU v7x, 256 devices: a whole 4x4x8 slice. The times are simulated.
256 devices in a mesh: seq: 64 (over z, x, core), head: 4 (over y).
Axes of the slice: x: 4, y: 4, z: 8, core: 2. Of those that a mesh axis runs over, the one named last changes fastest.
Arguments:
- hidden_in: bfloat16 [65536, 2048], P('seq', 'head'), may hold values from -16 to 16
- value_weight: bfloat16 [2048, 2048], P(None, 'head'), may hold values from -0.125 to 0.125
- queries: bfloat16 [65536, 2048], P('seq', 'head'), may hold values from -6 to 6
- keys: bfloat16 [65536, 2048], P('seq', 'head'), may hold values from -6 to 6
- level_weights: bfloat16 [17, 16, 65536], P(None, 'head', 'seq'), may hold values from 0 to 1
- out_grad: bfloat16 [65536, 2048], P('seq', 'head'), may hold values from -0.0234375 to 0.0234375
Outputs:
- attended: bfloat16 [65536, 2048], P('seq', 'head')
- weight_grad: float32 [2048, 2048], P('seq', 'head')
All inputs are finite; a program needn't handle non-finite values.
Results may differ from a plain program's by a relative error of at most 0.0057.
Values may be sent and summed in bfloat16 or wider, within the bound.
No kernel may reach another device: no remote copies, remote signals or barrier semaphores. Data moves between devices by JAX's collectives and lax.ppermute only.
A program may use at most 128 MiB of HBM per device.

v0:
```python
import jax
import jax.numpy as jnp
from jax import lax
from jax.sharding import PartitionSpec as P


def from_partner(value, axis, distance):
    return lax.ppermute(value, axis, [(i, i ^ 1 << distance) for i in range(lax.axis_size(axis))])


def level_of(later, earlier, depth):
    differ = jnp.bitwise_xor(later, earlier)
    result = jnp.zeros(differ.shape, jnp.int32)
    for digit in range(depth):
        result = result + (differ >= 1 << digit).astype(jnp.int32)
    return result


def near_part(queries3, keys3, values3, grads3, near_weights, depth):
    length = queries3.shape[0]
    count = max(1, length // 512)
    span_rows = length // count
    pieces = []
    value_back = jnp.zeros(values3.shape, jnp.float32)
    for index in range(count):
        first = index * span_rows
        last = first + span_rows
        scores = jnp.einsum(
            "thd,shd->hts", queries3[first:last], keys3[:last], preferred_element_type=jnp.float32
        )
        later = first + jnp.arange(span_rows, dtype=jnp.int32)[:, None]
        earlier = jnp.arange(last, dtype=jnp.int32)[None, :]
        table = level_of(later, earlier, depth)
        weight = jnp.zeros(scores.shape, jnp.float32)
        for level_index in range(depth + 1):
            weight = weight + jnp.where(
                table == level_index, near_weights[level_index][:, first:last, None], 0.0
            )
        weight = jnp.where(earlier <= later, weight, 0.0)
        probs = (scores * weight).astype(jnp.bfloat16)
        pieces.append(
            jnp.einsum("hts,she->the", probs, values3[:last], preferred_element_type=jnp.float32)
        )
        value_back = value_back.at[:last].add(
            jnp.einsum(
                "hts,the->she", probs, grads3[first:last], preferred_element_type=jnp.float32
            )
        )
    return (jnp.concatenate(pieces, axis=0), value_back)


def local(hidden_in, value_weight, queries, keys, level_weights, out_grad):
    head_count = level_weights.shape[1]
    span_cols = value_weight.shape[1]
    head_width = span_cols // head_count
    length = queries.shape[0]
    depth = length.bit_length() - 1
    seq_count = lax.axis_size("seq")
    seq_depth = seq_count.bit_length() - 1
    position = lax.axis_index("seq")
    gathered = lax.all_gather(hidden_in, "head", axis=1, tiled=True)
    values = jnp.dot(gathered, value_weight, preferred_element_type=jnp.float32).astype(
        jnp.bfloat16
    )
    shape_three = (length, head_count, head_width)
    queries3 = queries.reshape(shape_three)
    keys3 = keys.reshape(shape_three)
    values3 = values.reshape(shape_three)
    grads3 = out_grad.reshape(shape_three)
    near_weights = level_weights[: depth + 1].astype(jnp.float32)
    far_weights = level_weights[depth + 1 :].astype(jnp.float32)
    attended, value_grad = near_part(queries3, keys3, values3, grads3, near_weights, depth)
    key_state = jnp.einsum("thd,the->hde", keys3, values3, preferred_element_type=jnp.float32)
    query_levels = []
    for digit in range(seq_depth):
        weighted = (queries3.astype(jnp.float32) * far_weights[digit].T[:, :, None]).astype(
            jnp.bfloat16
        )
        query_levels.append(
            jnp.einsum("thd,the->hde", weighted, grads3, preferred_element_type=jnp.float32)
        )
    query_stack = jnp.stack(query_levels)
    far_states = []
    back_states = []
    running = key_state
    for digit in range(seq_depth):
        got_keys = from_partner(running, "seq", digit)
        upper = position >> digit & 1 == 1
        far_states.append(jnp.where(upper, got_keys, 0.0))
        running = running + got_keys
    pending = query_stack
    for digit in range(seq_depth):
        got_queries = from_partner(pending, "seq", digit)
        upper = position >> digit & 1 == 1
        back_states.append(jnp.where(upper, 0.0, got_queries[0]))
        pending = pending[1:] + got_queries[1:]
    for digit in range(seq_depth):
        product = jnp.einsum(
            "thd,hde->the",
            queries3,
            far_states[digit].astype(jnp.bfloat16),
            preferred_element_type=jnp.float32,
        )
        attended = attended + product * far_weights[digit].T[:, :, None]
        value_grad = value_grad + jnp.einsum(
            "shd,hde->she",
            keys3,
            back_states[digit].astype(jnp.bfloat16),
            preferred_element_type=jnp.float32,
        )
    attended_out = attended.astype(jnp.bfloat16).reshape(length, span_cols)
    value_flat = value_grad.astype(jnp.bfloat16).reshape(length, span_cols)
    share_rows = gathered.shape[1] // seq_count
    local_term = lax.dot_general(
        gathered, value_flat, (((0,), (0,)), ((), ())), preferred_element_type=jnp.float32
    )
    summed = lax.psum(local_term, "seq")
    weight_grad = lax.dynamic_slice_in_dim(summed, position * share_rows, share_rows, 0)
    return (attended_out, weight_grad)


def solution(mesh):
    return jax.shard_map(
        local,
        mesh=mesh,
        in_specs=(
            P("seq", "head"),
            P(None, "head"),
            P("seq", "head"),
            P("seq", "head"),
            P(None, "head", "seq"),
            P("seq", "head"),
        ),
        out_specs=(P("seq", "head"), P("seq", "head")),
        check_vma=False,
    )
```

profile of v0, /device:TPU:30, one launch (start us, length us, event | category | flops | bytes accessed | tf_op | source)
XLA Modules:
  0.0 375.8 jit_solution(18027901408983456728)
XLA Ops:
  9.5 1.7 fusion.23
  16.6 6.2 %iota_compare_fusion = (pred[512,1024]{1,0:T(8,128)(4,1)S(1)}, pred[512,1024]{1,0:T(8,128)(4,1)S(1)}, pred[512,1024]{1,0:T(8,128)(4,1)S(1)}, pred[512,1024]{1,0:...) fusion(s32[512]{0:T(512)S(1)} %iota_add_fusion), kind=kLoop, calls=%fused_computation.48 | loop fusion | flops 22020096 | bytes 6293504 | tf_op jit(solution)/shard_map/le | solution.py:39
  24.6 13.4 %multiply_convert_fusion = bf16[4,512,1024]{2,1,0:T(8,128)(2,1)} fusion(f32[4,512]{1,0:T(4,128)S(1)} %get-tuple-element.90, f32[4,512]{1,0:T(4,128)S(1)} %get-tuple-element.111, f32[4,512]{1,0:T(4,128)S(1)} %get-tuple-element.86, f32[4,512]{1,0:T(4,128)S(1)} %get-tuple-element.109, f32[4,512]{1,0:T(4,128)S(1)} %get-tuple-element.82, ...), kind=kOutput, calls=%fused_computation | convolution fusion | flops 587202560 | bytes 12148736 | tf_op jit(solution)/shard_map/thd,shd->hts/dot_general | solution.py:28
  42.2 2.1 copy.91
  44.3 2.1 copy.55
  46.4 2.0 copy.54
  49.8 3.0 fusion.150
  52.9 18.0 %collective-permute-done.7 = f32[5,4,128,128]{3,2,1,0:T(8,128)} collective-permute-done((f32[5,4,128,128]{3,2,1,0:T(8,128)}, f32[5,4,128,128]{3,2,1,0:T(8,128)}, u32[]{:S(2)}, u32[]{:S(2)}) %collective-permute-start.7) | collective-permute-done | bytes 1310752 | tf_op jit(solution)/shard_map/ppermute | solution.py:8
  70.9 1.7 slice_add_fusion.1
  74.1 6.8 %multiply_convert_fusion.1 = bf16[4,512,512]{2,1,0:T(8,128)(2,1)S(1)} fusion(bf16[512,4,128]{0,2,1:T(8,128)(2,1)S(1)} %bitcast.276, bf16[512,4,128]{0,2,1:T(8,128)(2,1)S(1)} %bitcast.275, f32[4,512]{1,0:T(4,128)S(1)} %get-tuple-element.89, f32[4,512]{1,0:T(4,128)S(1)} %get-tuple-element.112, f32[4,512]{1,0:T(4,128)S(1)} %get-tuple-element.85, ...), kind=kOutput, calls=%fused_computation.7 | convolution fusion | flops 293601280 | bytes 6381568 | tf_op jit(solution)/shard_map/thd,shd->hts/dot_general | solution.py:28
  81.0 17.9 %collective-permute-done.8 = f32[4,4,128,128]{3,2,1,0:T(8,128)S(1)} collective-permute-done((f32[4,4,128,128]{3,2,1,0:T(8,128)S(1)}, f32[4,4,128,128]{3,2,1,0:T(8,128)S(1)}, u32[]{:S(2)}, u32[]{:S(2)}) %collective-permute-start.8) | collective-permute-done | bytes 1048608 | tf_op jit(solution)/shard_map/ppermute | solution.py:8
  99.0 2.0 collective-permute-start.9
  104.4 13.2 %collective-permute-done.9 = f32[3,4,128,128]{3,2,1,0:T(8,128)S(1)} collective-permute-done((f32[3,4,128,128]{3,2,1,0:T(8,128)S(1)}, f32[3,4,128,128]{3,2,1,0:T(8,128)S(1)}, u32[]{:S(2)}, u32[]{:S(2)}) %collective-permute-start.9) | collective-permute-done | bytes 786464 | tf_op jit(solution)/shard_map/ppermute | solution.py:8
  117.6 3.4 collective-permute-start.10
  121.9 20.4 %collective-permute-done.10 = f32[2,4,128,128]{3,2,1,0:T(8,128)S(1)} collective-permute-done((f32[2,4,128,128]{3,2,1,0:T(8,128)S(1)}, f32[2,4,128,128]{3,2,1,0:T(8,128)S(1)}, u32[]{:S(2)}, u32[]{:S(2)}) %collective-permute-start.10) | collective-permute-done | bytes 524320 | tf_op jit(solution)/shard_map/ppermute | solution.py:8
  142.4 6.5 %collective-permute-start.11 = (bf16[1,4,128,128]{3,2,1,0:T(8,128)(2,1)S(1)}, bf16[1,4,128,128]{3,2,1,0:T(8,128)(2,1)S(1)}, u32[]{:S(2)}, u32[]{:S(2)}) collective-permute-start(bf16[1,4,128,128]{3,2,1,0:T(8,128)(2,1)S(1)} %slice_add_fusion.4), channel_id=1, source_target_pairs={{0,128},{4,132},{8,136},{12,140},{16,144},{20,148},{24,152},{28,15... | collective-permute-start | bytes 393224 | tf_op jit(solution)/shard_map/ppermute | solution.py:8
  149.4 5.5 %collective-permute-done.11 = bf16[1,4,128,128]{3,2,1,0:T(8,128)(2,1)S(1)} collective-permute-done((bf16[1,4,128,128]{3,2,1,0:T(8,128)(2,1)S(1)}, bf16[1,4,128,128]{3,2,1,0:T(8,128)(2,1)S(1)}, u32[]{:S(2)}, u32[]{:S(2)}) %collective-permute-start.11) | collective-permute-done | bytes 131104 | tf_op jit(solution)/shard_map/ppermute | solution.py:8
  154.9 1.9 fusion.12
  156.8 4.7 %convolution_convert_fusion = bf16[1024,512]{0,1:T(8,128)(2,1)S(1)} fusion(bf16[1024,2048]{1,0:T(8,128)(2,1)} %all-gather.2.cloned.1.call-done, bf16[2048,512]{1,0:T(8,128)(2,1)S(1)} %copy-done), kind=kOutput, calls=%fused_computation.49 | convolution fusion | flops 2148007936 | bytes 7340032 | tf_op jit(solution)/shard_map/dot_general | solution.py:62
  162.4 2.5 convolution_bitcast_fusion.3
  166.2 4.4 %convolution_bitcast_fusion = f32[2048,512]{0,1:T(8,128)} fusion(bf16[1024,512]{0,1:T(8,128)(2,1)S(1)} %bitcast.274, bf16[1024,2048]{1,0:T(8,128)(2,1)S(1)} %copy-done.23), kind=kOutput, calls=%fused_computation.8 | convolution fusion | flops 2147483648 | bytes 9437184 | tf_op jit(solution)/shard_map/dot_general | solution.py:114
  170.6 2.6 convolution_bitcast_fusion.2
  175.4 8.3 %collective-permute-done.1 = f32[4,128,128]{1,2,0:T(8,128)S(1)} collective-permute-done((f32[4,128,128]{1,2,0:T(8,128)S(1)}, f32[4,128,128]{1,2,0:T(8,128)S(1)}, u32[]{:S(2)}, u32[]{:S(2)}) %collective-permute-start.1) | collective-permute-done | bytes 262176 | tf_op jit(solution)/shard_map/ppermute | solution.py:8
  185.8 8.0 %collective-permute-done.2 = f32[4,128,128]{1,2,0:T(8,128)S(1)} collective-permute-done((f32[4,128,128]{1,2,0:T(8,128)S(1)}, f32[4,128,128]{1,2,0:T(8,128)S(1)}, u32[]{:S(2)}, u32[]{:S(2)}) %collective-permute-start.2) | collective-permute-done | bytes 262176 | tf_op jit(solution)/shard_map/ppermute | solution.py:8
  194.4 8.6 %collective-permute-done.3 = f32[4,128,128]{1,2,0:T(8,128)S(1)} collective-permute-done((f32[4,128,128]{1,2,0:T(8,128)S(1)}, f32[4,128,128]{1,2,0:T(8,128)S(1)}, u32[]{:S(2)}, u32[]{:S(2)}) %collective-permute-start.3) | collective-permute-done | bytes 262176 | tf_op jit(solution)/shard_map/ppermute | solution.py:8
  203.0 1.8 collective-permute-start.4
  205.2 13.1 %collective-permute-done.4 = f32[4,128,128]{1,2,0:T(8,128)S(1)} collective-permute-done((f32[4,128,128]{1,2,0:T(8,128)S(1)}, f32[4,128,128]{1,2,0:T(8,128)S(1)}, u32[]{:S(2)}, u32[]{:S(2)}) %collective-permute-start.4) | collective-permute-done | bytes 262176 | tf_op jit(solution)/shard_map/ppermute | solution.py:8
  218.4 3.2 collective-permute-start.5
  222.1 9.1 %collective-permute-done.5 = bf16[4,128,128]{1,2,0:T(8,128)(2,1)S(1)} collective-permute-done((bf16[4,128,128]{1,2,0:T(8,128)(2,1)S(1)}, bf16[4,128,128]{1,2,0:T(8,128)(2,1)S(1)}, u32[]{:S(2)}, u32[]{:S(2)}) %collective-permute-start.5) | collective-permute-done | bytes 131104 | tf_op jit(solution)/shard_map/ppermute | solution.py:8
  231.2 2.4 fusion.11
  233.6 2.3 copy.74
  235.8 131.3 %all-reduce.3.cloned.1.call-done = f32[2048,512]{0,1:T(8,128)} async-done(((f32[2048,512]{0,1:T(8,128)}), f32[2048,512]{0,1:T(8,128)}) %all-reduce.3.cloned.1.call-update) | async-done | bytes 4194320 | tf_op jit(solution)/shard_map/psum | solution.py:117
  (112 shorter events, 31.1 us)
Async XLA Ops:
  7.2 149.7 %copy-start = (bf16[2048,512]{1,0:T(8,128)(2,1)S(1)}, bf16[2048,512]{1,0:T(8,128)(2,1)}, u32[]{:S(2)}) copy-start(bf16[2048,512]{1,0:T(8,128)(2,1)} %param.13) | copy-start | bytes 6291460
  7.2 149.6 %all-gather.2.cloned.1.call-start = ((), (), s32[]{:S(2)}) async-start(), calls=%async_computation | async-start | bytes 5242880 | tf_op jit(solution)/shard_map/all_gather | solution.py:61
  7.9 359.2 %all-reduce.3.cloned.1.call-start = ((), (), s32[]{:S(2)}) async-start(), calls=%async_computation.1 | async-start | bytes 8388608 | tf_op jit(solution)/shard_map/psum | solution.py:117
  13.5 24.6 %collective-permute-start.6 = (f32[6,4,128,128]{3,2,1,0:T(8,128)S(1)}, f32[6,4,128,128]{3,2,1,0:T(8,128)S(1)}, u32[]{:S(2)}, u32[]{:S(2)}) collective-permute-start(f32[6,4,128,128]{3,2,1,0:T(8,128)S(1)} %get-tuple-element.42), channel_id=1, source_target_pairs={{0,4},{4,0},{8,12},{12,8},{16,20},{20,16},{24,28},{28,24},{32,36},... | collective-permute-start | bytes 4718600 | tf_op jit(solution)/shard_map/ppermute | solution.py:8
  16.6 8.0 %copy-start.1 = (bf16[1024,512]{1,0:T(8,128)(2,1)S(1)}, bf16[1024,512]{1,0:T(8,128)(2,1)}, u32[]{:S(2)}) copy-start(bf16[1024,512]{1,0:T(8,128)(2,1)} %param.15) | copy-start | bytes 3145732
  38.1 3.3 copy-start.9
  39.4 31.5 %collective-permute-start.7 = (f32[5,4,128,128]{3,2,1,0:T(8,128)}, f32[5,4,128,128]{3,2,1,0:T(8,128)}, u32[]{:S(2)}, u32[]{:S(2)}) collective-permute-start(f32[5,4,128,128]{3,2,1,0:T(8,128)} %slice_add_fusion), channel_id=1, source_target_pairs={{0,8},{4,12},{8,0},{12,4},{16,24},{20,28},{24,16},{28,20},{32,40},... | collective-permute-start | bytes 3932168 | tf_op jit(solution)/shard_map/ppermute | solution.py:8
  52.8 21.3 %copy-start.12 = (bf16[512,512]{0,1:T(8,128)(2,1)S(1)}, bf16[512,512]{0,1:T(8,128)(2,1)}, u32[]{:S(2)}) copy-start(bf16[512,512]{0,1:T(8,128)(2,1)} %copy.91) | copy-start | bytes 1572868
  52.8 21.2 %copy-start.13 = (bf16[512,512]{0,1:T(8,128)(2,1)S(1)}, bf16[512,512]{0,1:T(8,128)(2,1)}, u32[]{:S(2)}) copy-start(bf16[512,512]{0,1:T(8,128)(2,1)} %get-tuple-element.40) | copy-start | bytes 1572868
  52.8 21.2 %copy-start.14 = (pred[512,512]{1,0:T(8,128)(4,1)S(1)}, pred[512,512]{1,0:T(8,128)(4,1)}, u32[]{:S(2)}) copy-start(pred[512,512]{1,0:T(8,128)(4,1)} %get-tuple-element.114) | copy-start | bytes 786436
  52.8 21.2 %copy-start.15 = (pred[512,512]{1,0:T(8,128)(4,1)S(1)}, pred[512,512]{1,0:T(8,128)(4,1)}, u32[]{:S(2)}) copy-start(pred[512,512]{1,0:T(8,128)(4,1)} %get-tuple-element.115) | copy-start | bytes 786436
  52.8 21.2 %copy-start.16 = (pred[512,512]{1,0:T(8,128)(4,1)S(1)}, pred[512,512]{1,0:T(8,128)(4,1)}, u32[]{:S(2)}) copy-start(pred[512,512]{1,0:T(8,128)(4,1)} %get-tuple-element.116) | copy-start | bytes 786436
  52.8 21.2 %copy-start.18 = (f32[4,512]{1,0:T(4,128)S(1)}, f32[4,512]{1,0:T(4,128)}, u32[]{:S(2)}) copy-start(f32[4,512]{1,0:T(4,128)} %get-tuple-element.108) | copy-start | bytes 24580
  52.8 21.2 %copy-start.19 = (f32[4,512]{1,0:T(4,128)S(1)}, f32[4,512]{1,0:T(4,128)}, u32[]{:S(2)}) copy-start(f32[4,512]{1,0:T(4,128)} %get-tuple-element.73) | copy-start | bytes 24580
  52.8 21.2 %copy-start.20 = (f32[4,512]{1,0:T(4,128)S(1)}, f32[4,512]{1,0:T(4,128)}, u32[]{:S(2)}) copy-start(f32[4,512]{1,0:T(4,128)} %get-tuple-element.106) | copy-start | bytes 24580
  52.9 21.2 %copy-start.21 = (f32[4,512]{1,0:T(4,128)S(1)}, f32[4,512]{1,0:T(4,128)}, u32[]{:S(2)}) copy-start(f32[4,512]{1,0:T(4,128)} %get-tuple-element.69) | copy-start | bytes 24580
  52.9 21.2 %copy-start.22 = (f32[4,512]{1,0:T(4,128)S(1)}, f32[4,512]{1,0:T(4,128)}, u32[]{:S(2)}) copy-start(f32[4,512]{1,0:T(4,128)} %get-tuple-element.104) | copy-start | bytes 24580
  72.5 26.4 %collective-permute-start.8 = (f32[4,4,128,128]{3,2,1,0:T(8,128)S(1)}, f32[4,4,128,128]{3,2,1,0:T(8,128)S(1)}, u32[]{:S(2)}, u32[]{:S(2)}) collective-permute-start(f32[4,4,128,128]{3,2,1,0:T(8,128)S(1)} %slice_add_fusion.1), channel_id=1, source_target_pairs={{0,16},{4,20},{8,24},{12,28},{16,0},{20,4},{24,8},{28,12},{32,48},... | collective-permute-start | bytes 3145736 | tf_op jit(solution)/shard_map/ppermute | solution.py:8
  80.9 20.5 %copy-start.5 = (bf16[4,512,512]{2,1,0:T(8,128)(2,1)}, bf16[4,512,512]{2,1,0:T(8,128)(2,1)S(1)}, u32[]{:S(2)}) copy-start(bf16[4,512,512]{2,1,0:T(8,128)(2,1)S(1)} %multiply_convert_fusion.1) | copy-start | bytes 6291460
  80.9 20.1 %copy-start.8 = (bf16[512,512]{0,1:T(8,128)(2,1)S(1)}, bf16[512,512]{0,1:T(8,128)(2,1)}, u32[]{:S(2)}) copy-start(bf16[512,512]{0,1:T(8,128)(2,1)} %copy.54) | copy-start | bytes 1572868
  99.0 18.5 %collective-permute-start.9 = (f32[3,4,128,128]{3,2,1,0:T(8,128)S(1)}, f32[3,4,128,128]{3,2,1,0:T(8,128)S(1)}, u32[]{:S(2)}, u32[]{:S(2)}) collective-permute-start(f32[3,4,128,128]{3,2,1,0:T(8,128)S(1)} %slice_add_fusion.2), channel_id=1, source_target_pairs={{0,32},{4,36},{8,40},{12,44},{16,48},{20,52},{24,56},{28,60},{32,0... | collective-permute-start | bytes 2359304 | tf_op jit(solution)/shard_map/ppermute | solution.py:8
  117.6 24.8 %collective-permute-start.10 = (f32[2,4,128,128]{3,2,1,0:T(8,128)S(1)}, f32[2,4,128,128]{3,2,1,0:T(8,128)S(1)}, u32[]{:S(2)}, u32[]{:S(2)}) collective-permute-start(f32[2,4,128,128]{3,2,1,0:T(8,128)S(1)} %slice_add_fusion.3), channel_id=1, source_target_pairs={{0,64},{4,68},{8,72},{12,76},{16,80},{20,84},{24,88},{28,92},{32,9... | collective-permute-start | bytes 1572872 | tf_op jit(solution)/shard_map/ppermute | solution.py:8
  142.4 12.5 %collective-permute-start.11 = (bf16[1,4,128,128]{3,2,1,0:T(8,128)(2,1)S(1)}, bf16[1,4,128,128]{3,2,1,0:T(8,128)(2,1)S(1)}, u32[]{:S(2)}, u32[]{:S(2)}) collective-permute-start(bf16[1,4,128,128]{3,2,1,0:T(8,128)(2,1)S(1)} %slice_add_fusion.4), channel_id=1, source_target_pairs={{0,128},{4,132},{8,136},{12,140},{16,144},{20,148},{24,152},{28,15... | collective-permute-start | bytes 393224 | tf_op jit(solution)/shard_map/ppermute | solution.py:8
  156.8 5.6 %copy-start.4 = (bf16[4,512,1024]{2,1,0:T(8,128)(2,1)S(1)}, bf16[4,512,1024]{2,1,0:T(8,128)(2,1)}, u32[]{:S(2)}) copy-start(bf16[4,512,1024]{2,1,0:T(8,128)(2,1)} %multiply_convert_fusion) | copy-start | bytes 12582916
  162.4 3.7 copy-start.23
  166.1 7.0 %collective-permute-start = (f32[4,128,128]{1,2,0:T(8,128)}, f32[4,128,128]{1,2,0:T(8,128)S(1)}, u32[]{:S(2)}, u32[]{:S(2)}) collective-permute-start(f32[4,128,128]{1,2,0:T(8,128)} %convolution_bitcast_fusion.10), channel_id=1, source_target_pairs={{0,4},{4,0},{8,12},{12,8},{16,20},{20,16},{24,28},{28,24},{32,36},... | collective-permute-start | bytes 786440 | tf_op jit(solution)/shard_map/ppermute | solution.py:8
  174.1 9.5 %collective-permute-start.1 = (f32[4,128,128]{1,2,0:T(8,128)S(1)}, f32[4,128,128]{1,2,0:T(8,128)S(1)}, u32[]{:S(2)}, u32[]{:S(2)}) collective-permute-start(f32[4,128,128]{1,2,0:T(8,128)S(1)} %add.637), channel_id=1, source_target_pairs={{0,8},{4,12},{8,0},{12,4},{16,24},{20,28},{24,16},{28,20},{32,40},... | collective-permute-start | bytes 786440 | tf_op jit(solution)/shard_map/ppermute | solution.py:8
  183.7 10.1 %collective-permute-start.2 = (f32[4,128,128]{1,2,0:T(8,128)S(1)}, f32[4,128,128]{1,2,0:T(8,128)S(1)}, u32[]{:S(2)}, u32[]{:S(2)}) collective-permute-start(f32[4,128,128]{1,2,0:T(8,128)S(1)} %add.639), channel_id=1, source_target_pairs={{0,16},{4,20},{8,24},{12,28},{16,0},{20,4},{24,8},{28,12},{32,48},... | collective-permute-start | bytes 786440 | tf_op jit(solution)/shard_map/ppermute | solution.py:8
  193.8 9.1 %collective-permute-start.3 = (f32[4,128,128]{1,2,0:T(8,128)S(1)}, f32[4,128,128]{1,2,0:T(8,128)S(1)}, u32[]{:S(2)}, u32[]{:S(2)}) collective-permute-start(f32[4,128,128]{1,2,0:T(8,128)S(1)} %add.641), channel_id=1, source_target_pairs={{0,32},{4,36},{8,40},{12,44},{16,48},{20,52},{24,56},{28,60},{32,0... | collective-permute-start | bytes 786440 | tf_op jit(solution)/shard_map/ppermute | solution.py:8
  203.0 15.4 %collective-permute-start.4 = (f32[4,128,128]{1,2,0:T(8,128)S(1)}, f32[4,128,128]{1,2,0:T(8,128)S(1)}, u32[]{:S(2)}, u32[]{:S(2)}) collective-permute-start(f32[4,128,128]{1,2,0:T(8,128)S(1)} %add.643), channel_id=1, source_target_pairs={{0,64},{4,68},{8,72},{12,76},{16,80},{20,84},{24,88},{28,92},{32,9... | collective-permute-start | bytes 786440 | tf_op jit(solution)/shard_map/ppermute | solution.py:8
  205.2 26.0 %copy-start.6 = (f32[512,4,128]{0,2,1:T(8,128)S(1)}, f32[512,4,128]{0,2,1:T(8,128)}, u32[]{:S(2)}) copy-start(f32[512,4,128]{0,2,1:T(8,128)} %convolution_bitcast_fusion.3) | copy-start | bytes 3145732
  218.4 12.8 %collective-permute-start.5 = (bf16[4,128,128]{1,2,0:T(8,128)(2,1)S(1)}, bf16[4,128,128]{1,2,0:T(8,128)(2,1)S(1)}, u32[]{:S(2)}, u32[]{:S(2)}) collective-permute-start(bf16[4,128,128]{1,2,0:T(8,128)(2,1)S(1)} %add.645), channel_id=1, source_target_pairs={{0,128},{4,132},{8,136},{12,140},{16,144},{20,148},{24,152},{28,15... | collective-permute-start | bytes 393224 | tf_op jit(solution)/shard_map/ppermute | solution.py:8
  (6 other events, 11.7 us)
Sparse Core Ops, SparseCore 0:
  9.8 51.8 all-gather.1
  170.7 196.3 all-reduce.2
where the time goes:
time: 378 us; the launch traced here: 376 us
  waiting for transfers between devices  254 us (67%)
  matrix products  53.6 us (14%)
  starting transfers between devices  22 us (6%)
  local copies, waits for them, and re-layouts  17.4 us (5%)
  between operations  14.6 us (4%)
  other arithmetic  14 us (4%)
    psum x1, waiting for transfers between devices, local(): summed = lax.psum(local_term, 'seq')  131 us
    ppermute x12, waiting for transfers between devices, from_partner(): lax.ppermute(value, axis, [(i, i ^ 1 << distance) for i in range(lax.axis...  122 us
    ppermute x12, starting transfers between devices, from_partner(): lax.ppermute(value, axis, [(i, i ^ 1 << distance) for i in range(lax.axis...  21.9 us
    dot_general x2, matrix products, near_part(): jnp.einsum('thd,shd->hts', queries3[first:last], keys3[:last], preferred_...  20.3 us
  transfers between devices with their start and end apart: 14, of which 11 were waited for; matrix products, arithmetic and copies ran while one was open for 20% of the time, Pallas kernels for 0%

commit v1 on v0

v1 whole, which is shorter than its diff:
```python
import functools

import jax
import jax.numpy as jnp
from jax import lax
from jax.experimental import pallas as pl
from jax.experimental.pallas import tpu as pltpu
from jax.sharding import Mesh, PartitionSpec as P

BF = jnp.bfloat16
F32 = jnp.float32
HW = 128
NH = 4
TOK = 1024
BLK = 256
DEPTH = 10
FAR = 6
PART = 512
NX, NZ = 4, 8
VMEM = 56 * 1024 * 1024

NT = (((1,), (1,)), ((), ()))
TN = (((0,), (0,)), ((), ()))
NN = (((1,), (0,)), ((), ()))


def dot(a, b, dims=NN):
    return lax.dot_general(a, b, dims, preferred_element_type=F32)


def shift(value, axis, distance, size):
    return lax.ppermute(value, axis, [(i, (i + distance) % size) for i in range(size)])


def swap(value, axis, distance, size):
    return lax.ppermute(value, axis, [(i, i ^ distance) for i in range(size)])


def params():
    return pltpu.CompilerParams(
        dimension_semantics=("arbitrary",), vmem_limit_bytes=VMEM
    )


def cost(flops, moved):
    return pl.CostEstimate(flops=int(flops), bytes_accessed=int(moved), transcendentals=0)


def query_state_kernel(place, q_ref, g_ref, lw_ref, first_ref, send_ref, keep_ref, stack):
    slot = pl.program_id(0)
    turned = q_ref[...].astype(F32).T
    for digit in range(FAR):
        row = lw_ref[0, DEPTH + 1 + digit : DEPTH + 2 + digit, :]
        stack[digit * HW : (digit + 1) * HW, :] = (turned * row).astype(BF)
    state = dot(stack[...], g_ref[...])
    first_ref[0] = state[:HW]
    rest = state[HW:].reshape(FAR - 1, HW, HW)

    @pl.when(slot < 2)
    def _():
        send_ref[0] = rest

    @pl.when(slot >= 2)
    def _():
        keep_ref[0] = rest


def query_states(place, queries, out_grad, weights):
    def head(s, place):
        return lax.rem(2 * (1 - place[0]) + s, NH)

    return pl.pallas_call(
        query_state_kernel,
        grid_spec=pltpu.PrefetchScalarGridSpec(
            num_scalar_prefetch=1,
            grid=(NH,),
            in_specs=[
                pl.BlockSpec((TOK, HW), lambda s, p: (0, head(s, p))),
                pl.BlockSpec((TOK, HW), lambda s, p: (0, head(s, p))),
                pl.BlockSpec((1, DEPTH + 1 + FAR, TOK), lambda s, p: (head(s, p), 0, 0)),
            ],
            out_specs=[
                pl.BlockSpec((1, HW, HW), lambda s, p: (s, 0, 0)),
                pl.BlockSpec((1, FAR - 1, HW, HW), lambda s, p: (jnp.minimum(s, 1), 0, 0, 0)),
                pl.BlockSpec((1, FAR - 1, HW, HW), lambda s, p: (jnp.maximum(s - 2, 0), 0, 0, 0)),
            ],
            scratch_shapes=[pltpu.VMEM((FAR * HW, TOK), BF)],
        ),
        out_shape=[
            jax.ShapeDtypeStruct((NH, HW, HW), F32),
            jax.ShapeDtypeStruct((2, FAR - 1, HW, HW), F32),
            jax.ShapeDtypeStruct((2, FAR - 1, HW, HW), F32),
        ],
        compiler_params=params(),
        cost_estimate=cost(2e9, 4e6),
        name="query_states",
    )(place, queries, out_grad, weights)


def differing():
    earlier = lax.broadcasted_iota(jnp.int32, (BLK, BLK), 0)
    later = lax.broadcasted_iota(jnp.int32, (BLK, BLK), 1)
    return earlier ^ later, earlier <= later


def near_square(k_ref, q_ref, lw_ref, high, low, differ, causal):
    scores = dot(
        k_ref[low * BLK : (low + 1) * BLK, :], q_ref[high * BLK : (high + 1) * BLK, :], NT
    )
    columns = slice(high * BLK, (high + 1) * BLK)
    if low != high:
        level = BLK.bit_length() + (high ^ low).bit_length() - 1
        weight = lw_ref[0, level : level + 1, columns]
    else:
        weight = jnp.broadcast_to(lw_ref[0, 0:1, columns], (BLK, BLK))
        for level in range(1, BLK.bit_length()):
            row = lw_ref[0, level : level + 1, columns]
            weight = jnp.where(differ >= 1 << (level - 1), row, weight)
        weight = jnp.where(causal, weight, 0.0)
    return (scores * weight).astype(BF)


def near_back_kernel(q_ref, k_ref, g_ref, lw_ref, back_ref):
    differ, causal = differing()
    for low in range(TOK // BLK):
        total = None
        for high in range(low, TOK // BLK):
            square = near_square(k_ref, q_ref, lw_ref, high, low, differ, causal)
            term = dot(square, g_ref[high * BLK : (high + 1) * BLK, :])
            total = term if total is None else total + term
        back_ref[low * BLK : (low + 1) * BLK, :] = total


def near_ahead_kernel(q_ref, k_ref, v_ref, lw_ref, ahead_ref):
    differ, causal = differing()
    for high in range(TOK // BLK):
        total = None
        for low in range(high + 1):
            square = near_square(k_ref, q_ref, lw_ref, high, low, differ, causal)
            term = dot(v_ref[low * BLK : (low + 1) * BLK, :], square, TN)
            total = term if total is None else total + term
        ahead_ref[0, :, high * BLK : (high + 1) * BLK] = total


def of_head():
    return pl.BlockSpec((TOK, HW), lambda h: (0, h))


def lw_of_head():
    return pl.BlockSpec((1, DEPTH + 1 + FAR, TOK), lambda h: (h, 0, 0))


def near_back(queries, keys, out_grad, weights):
    return pl.pallas_call(
        near_back_kernel,
        grid=(NH,),
        in_specs=[of_head(), of_head(), of_head(), lw_of_head()],
        out_specs=of_head(),
        out_shape=jax.ShapeDtypeStruct((TOK, NH * HW), F32),
        compiler_params=params(),
        cost_estimate=cost(4e9, 5e6),
        name="near_back",
    )(queries, keys, out_grad, weights)


def near_ahead(queries, keys, values, weights):
    return pl.pallas_call(
        near_ahead_kernel,
        grid=(NH,),
        in_specs=[of_head(), of_head(), of_head(), lw_of_head()],
        out_specs=pl.BlockSpec((1, HW, TOK), lambda h: (h, 0, 0)),
        out_shape=jax.ShapeDtypeStruct((NH, HW, TOK), F32),
        compiler_params=params(),
        cost_estimate=cost(4e9, 5e6),
        name="near_ahead",
    )(queries, keys, values, weights)


def values_kernel(place, own, lu, ll, ru, rl, fu, fl, w_ref, k_ref, v_ref, state_ref):
    tile = pl.program_id(0)
    core, me = place[0], place[1]
    upper = tile < 2

    def rows(part):
        at = pl.multiple_of(lax.rem(part, 4) * PART, PART)
        return w_ref[pl.ds(at, PART), :]

    total = dot(own[...], rows(me))
    for distance, (top, bottom) in ((3, (lu, ll)), (1, (ru, rl)), (2, (fu, fl))):
        part = jnp.where(upper, top[...], bottom[...])
        total = total + dot(part, rows(me + distance))
    v_ref[...] = total.astype(BF)

    @pl.when(tile == 0)
    def _():
        state_ref[...] = jnp.zeros_like(state_ref)

    for slot in range(NH):
        at = pl.multiple_of(lax.rem(2 * (1 - core) + slot, NH) * HW, HW)
        state_ref[slot] += dot(k_ref[:, pl.ds(at, HW)], v_ref[:, pl.ds(at, HW)], TN)


def values_and_states(place, parts, value_weight, keys):
    tile = pl.BlockSpec((BLK, PART), lambda i, p: (i, 0))
    top = pl.BlockSpec((BLK, PART), lambda i, p: (jnp.minimum(i, 1), 0))
    bottom = pl.BlockSpec((BLK, PART), lambda i, p: (jnp.maximum(i - 2, 0), 0))
    return pl.pallas_call(
        values_kernel,
        grid_spec=pltpu.PrefetchScalarGridSpec(
            num_scalar_prefetch=1,
            grid=(TOK // BLK,),
            in_specs=[
                tile,
                top,
                bottom,
                top,
                bottom,
                top,
                bottom,
                pl.BlockSpec((4 * PART, NH * HW), lambda i, p: (0, 0)),
                pl.BlockSpec((BLK, NH * HW), lambda i, p: (i, 0)),
            ],
            out_specs=[
                pl.BlockSpec((BLK, NH * HW), lambda i, p: (i, 0)),
                pl.BlockSpec((NH, HW, HW), lambda i, p: (0, 0, 0)),
            ],
        ),
        out_shape=[
            jax.ShapeDtypeStruct((TOK, NH * HW), BF),
            jax.ShapeDtypeStruct((NH, HW, HW), F32),
        ],
        compiler_params=params(),
        cost_estimate=cost(3e9, 8e6),
        name="values_and_states",
    )(place, *parts, value_weight, keys)


def weight_kernel(place, near_ref, k_ref, mine_ref, other_ref, own, lu, ll, ru, rl, fu, fl, send_ref, keep_ref, grad, term):
    step = pl.program_id(0)
    core, me, col = place[0], place[1], place[2]
    half = TOK // 2

    @pl.when(step == 0)
    def _():
        for slot in range(NH):
            at = pl.multiple_of(lax.rem(2 * core + slot, NH) * HW, HW)
            state = mine_ref[slot] if slot < 2 else other_ref[slot - 2]
            far = dot(k_ref[:, pl.ds(at, HW)], state)
            grad[:, pl.ds(at, HW)] = (near_ref[:, pl.ds(at, HW)] + far).astype(BF)
        term[...] = dot(own[...], grad[...], TN)

    for index, (top, bottom) in ((1, (lu, ll)), (2, (ru, rl)), (3, (fu, fl))):

        @pl.when(step == index)
        def _(top=top, bottom=bottom):
            term[...] = dot(top[...], grad[:half, :], TN) + dot(bottom[...], grad[half:, :], TN)

    distance = jnp.where(step == 0, 0, jnp.where(step == 1, 3, jnp.where(step == 2, 1, 2)))
    part = lax.rem(me + distance, 4)
    for plane in range(2):
        for x in range(NX):
            turn = lax.rem(x - col + NX, NX)
            at = plane * 256 + x * 64
            send_ref[turn, 2 * part + plane] = term[pl.ds(pl.multiple_of(at + (1 - core) * 32, 32), 32), :]
            keep_ref[turn, 2 * part + plane] = term[pl.ds(pl.multiple_of(at + core * 32, 32), 32), :]


def weight_terms(place, near, keys, mine, other, parts):
    whole = lambda *shape: pl.BlockSpec(shape, lambda i, p: (0,) * len(shape))
    half = TOK // 2
    return pl.pallas_call(
        weight_kernel,
        grid_spec=pltpu.PrefetchScalarGridSpec(
            num_scalar_prefetch=1,
            grid=(4,),
            in_specs=[
                whole(TOK, NH * HW),
                whole(TOK, NH * HW),
                whole(2, HW, HW),
                whole(2, HW, HW),
                whole(TOK, PART),
            ]
            + [whole(half, PART)] * 6,
            out_specs=[whole(NX, NZ, 32, NH * HW), whole(NX, NZ, 32, NH * HW)],
            scratch_shapes=[pltpu.VMEM((TOK, NH * HW), BF), pltpu.VMEM((PART, NH * HW), F32)],
        ),
        out_shape=[jax.ShapeDtypeStruct((NX, NZ, 32, NH * HW), F32)] * 2,
        compiler_params=params(),
        cost_estimate=cost(4e9, 12e6),
        name="weight_terms",
    )(place, near, keys, mine, other, *parts)


def attended_kernel(place, q_ref, lw_ref, near_ref, first_ref, far_ref, out_ref, stack):
    stack[:HW, :] = first_ref[0].astype(F32).T.astype(BF)
    for digit in range(1, FAR):
        stack[digit * HW : (digit + 1) * HW, :] = far_ref[0, digit - 1].astype(F32).T.astype(BF)
    product = dot(stack[...], q_ref[...], NT)
    total = near_ref[0]
    for digit in range(FAR):
        row = lw_ref[0, DEPTH + 1 + digit : DEPTH + 2 + digit, :]
        total = total + product[digit * HW : (digit + 1) * HW, :] * row
    out_ref[...] = total.T.astype(BF)


def attend(place, queries, weights, near, first, far):
    def head(s, p):
        return lax.rem(2 * p[0] + s, NH)

    return pl.pallas_call(
        attended_kernel,
        grid_spec=pltpu.PrefetchScalarGridSpec(
            num_scalar_prefetch=1,
            grid=(NH,),
            in_specs=[
                pl.BlockSpec((TOK, HW), lambda s, p: (0, head(s, p))),
                pl.BlockSpec((1, DEPTH + 1 + FAR, TOK), lambda s, p: (head(s, p), 0, 0)),
                pl.BlockSpec((1, HW, TOK), lambda s, p: (head(s, p), 0, 0)),
                pl.BlockSpec((1, HW, HW), lambda s, p: (s, 0, 0)),
                pl.BlockSpec((1, FAR - 1, HW, HW), lambda s, p: (s, 0, 0, 0)),
            ],
            out_specs=pl.BlockSpec((TOK, HW), lambda s, p: (0, head(s, p))),
            scratch_shapes=[pltpu.VMEM((FAR * HW, HW), BF)],
        ),
        out_shape=jax.ShapeDtypeStruct((TOK, NH * HW), BF),
        compiler_params=params(),
        cost_estimate=cost(2e9, 5e6),
        name="attended",
    )(place, queries, weights, near, first, far)


def back_sums(first, send, keep, x, z):
    first_got = lax.ppermute(first, "core", [(1, 0)])
    pairs = keep + swap(send, "core", 1, 2)
    pending = pairs[:, 2:]
    got = swap(pending.astype(BF), "z", 1, NZ).astype(F32)
    total = jnp.where(z & 1 == 0, got[:, 0], 0.0)
    pending = pending[:, 1:] + got[:, 1:]
    got = swap(pending.astype(BF), "z", 2, NZ).astype(F32)
    total = total + jnp.where(z & 2 == 0, got[:, 0], 0.0)
    pending = pending[:, 1] + got[:, 1]
    total = total + lax.ppermute(pending.astype(BF), "z", [(i + 4, i) for i in range(4)]).astype(F32)
    summed = total
    for distance in (1, 3, 2):
        to = (x + distance) % NX
        level = jnp.where(to ^ x == 1, pairs[:, 0], pairs[:, 1])
        message = total + jnp.where(to < x, level, 0.0)
        summed = summed + shift(message.astype(BF), "x", distance, NX).astype(F32)
    other = swap(summed, "core", 1, 2)
    return (summed + first_got[:2]).astype(BF), (other + first_got[2:]).astype(BF)


def far_states(state, core, x, z):
    got = swap(state, "core", 1, 2)
    first = jnp.where(core == 1, got, 0.0).astype(BF)
    pair = state[2:] + got[:2]
    left, far, right = (shift(pair.astype(BF), "x", d, NX).astype(F32) for d in (1, 2, 3))
    levels = [
        jnp.where(x & 1 == 1, left, 0.0),
        jnp.where(x == 2, left + far, jnp.where(x == 3, far + right, 0.0)),
    ]
    running = pair + left + far + right
    got = swap(running.astype(BF), "z", 1, NZ).astype(F32)
    levels.append(jnp.where(z & 1 == 1, got, 0.0))
    running = running + got
    got = swap(running.astype(BF), "z", 2, NZ).astype(F32)
    levels.append(jnp.where(z & 2 == 2, got, 0.0))
    running = running + got
    levels.append(lax.ppermute(running.astype(BF), "z", [(i, i + 4) for i in range(4)]).astype(F32))
    mine = jnp.stack([level.astype(BF) for level in levels], axis=1)
    other = swap(mine, "core", 1, 2)
    return first, jnp.concatenate([mine, other], axis=0)


def local(hidden_in, value_weight, queries, keys, level_weights, out_grad):
    z, x, core, me = (lax.axis_index(a) for a in ("z", "x", "core", "head"))
    place = jnp.stack([core, me, x]).astype(jnp.int32)
    weights = level_weights.astype(F32).transpose(1, 0, 2)

    half = TOK // 2
    upper, lower = hidden_in[:half], hidden_in[half:]
    lu = shift(upper, "head", 1, 4)
    rl = shift(lower, "head", 3, 4)
    ll = shift(lower, "head", 1, 4)
    ru = shift(upper, "head", 3, 4)
    fu = shift(lu, "head", 1, 4)
    fl = shift(rl, "head", 3, 4)
    parts = (hidden_in, lu, ll, ru, rl, fu, fl)

    first, send, keep = query_states(place, queries, out_grad, weights)
    mine, other = back_sums(first, send, keep, x, z)
    back = near_back(queries, keys, out_grad, weights)

    values, state = values_and_states(place, parts, value_weight, keys)
    send, keep = weight_terms(place, back, keys, mine, other, parts)

    zero, rest = far_states(state, core, x, z)
    ahead = near_ahead(queries, keys, values, weights)

    summed = keep + swap(send, "core", 1, 2)
    rows = summed[0]
    for distance in (1, 3, 2):
        rows = rows + shift(summed[distance].astype(BF), "x", distance, NX).astype(F32)
    got = lax.all_to_all(rows.astype(BF), "z", 0, 0, tiled=True)
    weight_grad = got.astype(F32).sum(axis=0)

    attended = attend(place, queries, weights, ahead, zero, rest)
    return attended, weight_grad


def solution(mesh):
    fine = Mesh(mesh.devices.reshape(NZ, NX, 2, 4), ("z", "x", "core", "head"))
    seq = ("z", "x", "core")
    return jax.shard_map(
        local,
        mesh=fine,
        in_specs=(
            P(seq, "head"),
            P(None, "head"),
            P(seq, "head"),
            P(seq, "head"),
            P(None, "head", seq),
            P(seq, "head"),
        ),
        out_specs=(P(seq, "head"), P(seq, "head")),
        check_vma=False,
    )
```

time: 378 us -> 154 us (0.41)
  waiting for transfers between devices: 254 us -> 47.9 us
  matrix products: 53.6 us -> 0 us
  Pallas kernels: 0 us -> 45.3 us
  starting transfers between devices: 22 us -> 46.6 us
  local copies, waits for them, and re-layouts: 17.4 us -> 2.93 us
  between operations: 14.6 us -> 0.94 us
  other arithmetic: 14 us -> 9.06 us
    psum x1 -> x0, waiting for transfers between devices: 131 us -> none  [local(): summed = lax.psum(local_term, 'seq')]
    ppermute x12 -> x27, waiting for transfers between devices: 122 us -> 45.2 us  [the longest x15 23.5 us: shift(): lax.ppermute(value, axis, [(i, (i + distance) % size) for i in range(size)])]
    dot_general x27 -> x0, matrix products: 53.6 us -> none  [the longest x2 20.3 us: near_part(): jnp.einsum('thd,shd->hts', queries3[first:last], keys3[:last], preferred_...]
    pallas_call x0 -> x6, Pallas kernels: none -> 45.3 us  [the longest x1 9.88 us: weight_terms(): pl.pallas_call(weight_kernel, grid_spec=pltpu.PrefetchScalarGridSpec(num_...]
    ppermute x12 -> x27, starting transfers between devices: 21.9 us -> 41.1 us  [the longest x15 18.2 us: shift(): lax.ppermute(value, axis, [(i, (i + distance) % size) for i in range(size)])]
    slice x12 -> x2, local copies, waits for them, and re-layouts: 9.53 us -> 0.1 us  [the longest x1 0.07 us: local(): upper, lower = (hidden_in[:half], hidden_in[half:])]
    le x2 -> x0, other arithmetic: 7.22 us -> none  [near_part(): weight = jnp.where(earlier <= later, weight, 0.0)]
    all_to_all x0 -> x1, starting transfers between devices: none -> 5.52 us  [local(): got = lax.all_to_all(rows.astype(BF), 'z', 0, 0, tiled=True)]
  transfers between devices with their start and end apart: 14 -> 28, of which waited for: 11 -> 14; matrix products, arithmetic and copies ran while one was open for 20% -> 3% of each run, Pallas kernels for 0% -> 26%
where the time goes in v1:
time: 154 us; the launch traced here: 153 us
  waiting for transfers between devices  47.9 us (31%)
  starting transfers between devices  46.6 us (30%)
  Pallas kernels  45.3 us (29%)
  other arithmetic  9.06 us (6%)
  local copies, waits for them, and re-layouts  2.93 us (2%)
    ppermute x15, waiting for transfers between devices, shift(): lax.ppermute(value, axis, [(i, (i + distance) % size) for i in range(size)])  23.5 us
    ppermute x15, starting transfers between devices, shift(): lax.ppermute(value, axis, [(i, (i + distance) % size) for i in range(size)])  18.2 us
    ppermute x9, waiting for transfers between devices, swap(): return lax.ppermute(value, axis, [(i, i ^ distance) for i in range(size)])  17.7 us
    ppermute x9, starting transfers between devices, swap(): return lax.ppermute(value, axis, [(i, i ^ distance) for i in range(size)])  12.5 us
    pallas_call x1, Pallas kernels, weight_terms(): pl.pallas_call(weight_kernel, grid_spec=pltpu.PrefetchScalarGridSpec(num_...  9.88 us
    pallas_call x1, Pallas kernels, values_and_states(): pl.pallas_call(values_kernel, grid_spec=pltpu.PrefetchScalarGridSpec(num_...  8.2 us
    pallas_call x1, Pallas kernels, near_back(): pl.pallas_call(near_back_kernel, grid=(NH,), in_specs=[of_head(), of_head...  7.88 us
    ppermute x1, starting transfers between devices, far_states(): lax.ppermute(running.astype(BF), 'z', [(i, i + 4) for i in range(4)])  7.83 us
  transfers between devices with their start and end apart: 28, of which 14 were waited for; matrix products, arithmetic and copies ran while one was open for 3% of the time, Pallas kernels for 26%

profile of v1, /device:TPU:30, one launch (start us, length us, event | category | flops | bytes accessed | tf_op | source)
XLA Modules:
  0.0 152.7 jit_solution(12948800530256609673)
XLA Ops:
  0.6 1.7 %convert_bitcast_fusion.lw_ref = f32[4,17,1024]{2,1,0:T(8,128)} fusion(bf16[17,4,1024]{2,1,0:T(4,128)(2,1)} %param.10), kind=kLoop, calls=%fused_computation.9 | loop fusion | flops 69632 | bytes 417792 | tf_op jit(solution)/shard_map/transpose | solution.py:378
  2.9 5.9 %query_states.1 = (f32[4,128,128]{2,1,0:T(8,128)}, f32[2,5,128,128]{3,2,1,0:T(8,128)}, f32[2,5,128,128]{3,2,1,0:T(8,128)}) custom-call(s32[3]{0:T(128)} %pad_add_fusion.place, bf16[1024,512]{1,0:T(8,128)(2,1)} %q_ref.7, bf16[1024,512]{1,0:T(8,128)(2,1)} %g_ref.3, f32[4,17,1024]{2,1,0:T(8,128)} %convert_bitcast_fusion.lw_ref), custom_call_target="tpu_custom_call" | custom-call | flops 2000000000 | bytes 4000000 | tf_op jit(solution)/shard_map/query_states/pallas_call | solution.py:72
  10.1 2.1 %collective-permute-done.14 = f32[2,5,128,128]{3,2,0,1:T(8,128)S(1)} collective-permute-done((f32[2,5,128,128]{3,2,0,1:T(8,128)S(1)}, f32[2,5,128,128]{3,2,0,1:T(8,128)S(1)}, u32[]{:S(2)}, u32[]{:S(2)}) %collective-permute-start.14) | collective-permute-done | bytes 655392 | tf_op jit(solution)/shard_map/ppermute | solution.py:36
  13.4 2.0 %collective-permute-start.15 = (bf16[2,3,128,128]{3,2,0,1:T(8,128)(2,1)S(1)}, bf16[2,3,128,128]{3,2,0,1:T(8,128)(2,1)S(1)}, u32[]{:S(2)}, u32[]{:S(2)}) collective-permute-start(bf16[2,3,128,128]{3,2,0,1:T(8,128)(2,1)S(1)} %slice.156), channel_id=1, source_target_pairs={{0,32},{32,0},{64,96},{96,64},{128,160},{160,128},{192,224},{224,1... | collective-permute-start | bytes 589832 | tf_op jit(solution)/shard_map/ppermute | solution.py:36
  15.4 5.2 %collective-permute-done.15 = bf16[2,3,128,128]{3,2,0,1:T(8,128)(2,1)S(1)} collective-permute-done((bf16[2,3,128,128]{3,2,0,1:T(8,128)(2,1)S(1)}, bf16[2,3,128,128]{3,2,0,1:T(8,128)(2,1)S(1)}, u32[]{:S(2)}, u32[]{:S(2)}) %collective-permute-start.15) | collective-permute-done | bytes 196640 | tf_op jit(solution)/shard_map/ppermute | solution.py:36
  20.7 3.4 %collective-permute-start.16 = (bf16[2,2,128,128]{3,2,0,1:T(8,128)(2,1)S(1)}, bf16[2,2,128,128]{3,2,0,1:T(8,128)(2,1)S(1)}, u32[]{:S(2)}, u32[]{:S(2)}) collective-permute-start(bf16[2,2,128,128]{3,2,0,1:T(8,128)(2,1)S(1)} %get-tuple-element.22), channel_id=1, source_target_pairs={{0,64},{32,96},{64,0},{96,32},{128,192},{160,224},{192,128},{224,1... | collective-permute-start | bytes 393224 | tf_op jit(solution)/shard_map/ppermute | solution.py:36
  24.1 6.0 %collective-permute-done.16 = bf16[2,2,128,128]{3,2,0,1:T(8,128)(2,1)S(1)} collective-permute-done((bf16[2,2,128,128]{3,2,0,1:T(8,128)(2,1)S(1)}, bf16[2,2,128,128]{3,2,0,1:T(8,128)(2,1)S(1)}, u32[]{:S(2)}, u32[]{:S(2)}) %collective-permute-start.16) | collective-permute-done | bytes 131104 | tf_op jit(solution)/shard_map/ppermute | solution.py:36
  32.3 2.5 %collective-permute-start = (bf16[512,512]{1,0:T(8,128)(2,1)S(1)}, bf16[512,512]{1,0:T(8,128)(2,1)}, u32[]{:S(2)}, u32[]{:S(2)}) collective-permute-start(bf16[512,512]{1,0:T(8,128)(2,1)S(1)} %get-tuple-element.30), channel_id=1, source_target_pairs={{0,1},{1,2},{2,3},{3,0},{4,5},{5,6},{6,7},{7,4},{8,9},{9,10},{10,1... | collective-permute-start | bytes 1572872 | tf_op jit(solution)/shard_map/ppermute | solution.py:32
  36.2 4.0 %collective-permute-done.17 = bf16[2,128,128]{2,1,0:T(8,128)(2,1)S(1)} collective-permute-done((bf16[2,128,128]{2,1,0:T(8,128)(2,1)S(1)}, bf16[2,128,128]{2,1,0:T(8,128)(2,1)S(1)}, u32[]{:S(2)}, u32[]{:S(2)}) %collective-permute-start.17) | collective-permute-done | bytes 65568 | tf_op jit(solution)/shard_map/ppermute | solution.py:342
  43.2 2.5 %collective-permute-done.3.rl = bf16[512,512]{1,0:T(8,128)(2,1)} collective-permute-done((bf16[512,512]{1,0:T(8,128)(2,1)S(1)}, bf16[512,512]{1,0:T(8,128)(2,1)}, u32[]{:S(2)}, u32[]{:S(2)}) %collective-permute-start.3) | collective-permute-done | bytes 524320 | tf_op jit(solution)/shard_map/ppermute | solution.py:32
  45.7 1.5 %collective-permute-done.lu = bf16[512,512]{1,0:T(8,128)(2,1)} collective-permute-done((bf16[512,512]{1,0:T(8,128)(2,1)S(1)}, bf16[512,512]{1,0:T(8,128)(2,1)}, u32[]{:S(2)}, u32[]{:S(2)}) %collective-permute-start) | collective-permute-done | bytes 524320 | tf_op jit(solution)/shard_map/ppermute | solution.py:32
  47.3 3.7 %collective-permute-start.4 = (bf16[512,512]{1,0:T(8,128)(2,1)}, bf16[512,512]{1,0:T(8,128)(2,1)S(1)}, u32[]{:S(2)}, u32[]{:S(2)}) collective-permute-start(bf16[512,512]{1,0:T(8,128)(2,1)} %collective-permute-done.lu), channel_id=1, source_target_pairs={{0,1},{1,2},{2,3},{3,0},{4,5},{5,6},{6,7},{7,4},{8,9},{9,10},{10,1... | collective-permute-start | bytes 1572872 | tf_op jit(solution)/shard_map/ppermute | solution.py:32
  51.5 7.9 %near_back.1.near_ref = f32[1024,512]{1,0:T(8,128)} custom-call(bf16[1024,512]{1,0:T(8,128)(2,1)} %q_ref.7, bf16[1024,512]{1,0:T(8,128)(2,1)} %k_ref.7, bf16[1024,512]{1,0:T(8,128)(2,1)} %g_ref.3, f32[4,17,1024]{2,1,0:T(8,128)} %convert_bitcast_fusion.lw_ref), custom_call_target="tpu_custom_call" | custom-call | flops 4000000000 | bytes 5000000 | tf_op jit(solution)/shard_map/near_back/pallas_call | solution.py:154
  60.0 1.8 %collective-permute-done.2.ru = bf16[512,512]{1,0:T(8,128)(2,1)S(1)} collective-permute-done((bf16[512,512]{1,0:T(8,128)(2,1)S(1)}, bf16[512,512]{1,0:T(8,128)(2,1)S(1)}, u32[]{:S(2)}, u32[]{:S(2)}) %collective-permute-start.2) | collective-permute-done | bytes 524320 | tf_op jit(solution)/shard_map/ppermute | solution.py:32
  61.8 8.3 %collective-permute-done.5.fl = bf16[512,512]{1,0:T(8,128)(2,1)S(1)} collective-permute-done((bf16[512,512]{1,0:T(8,128)(2,1)}, bf16[512,512]{1,0:T(8,128)(2,1)S(1)}, u32[]{:S(2)}, u32[]{:S(2)}) %collective-permute-start.5) | collective-permute-done | bytes 524320 | tf_op jit(solution)/shard_map/ppermute | solution.py:32
  71.8 8.2 %values_and_states.1 = (bf16[1024,512]{1,0:T(8,128)(2,1)}, f32[4,128,128]{2,1,0:T(8,128)}) custom-call(s32[3]{0:T(128)} %pad_add_fusion.place, bf16[1024,512]{1,0:T(8,128)(2,1)} %own.3, bf16[512,512]{1,0:T(8,128)(2,1)} %collective-permute-done.lu, bf16[512,512]{1,0:T(8,128)(2,1)} %copy-done.3, bf16[512,512]{1,0:T(8,128)(2,1)} %copy-done.4, ...), custom_call_target="tpu_custom_call" | custom-call | flops 3000000000 | bytes 8000000 | tf_op jit(solution)/shard_map/values_and_states/pallas_call | solution.py:207
  80.7 9.9 %weight_terms.1 = (f32[4,8,32,512]{3,2,1,0:T(8,128)}, f32[4,8,32,512]{3,2,1,0:T(8,128)}) custom-call(s32[3]{0:T(128)} %pad_add_fusion.place, f32[1024,512]{1,0:T(8,128)} %near_back.1.near_ref, bf16[1024,512]{1,0:T(8,128)(2,1)} %k_ref.7, bf16[2,128,128]{2,1,0:T(8,128)(2,1)} %get-tuple-element.18.mine_ref, bf16[2,128,128]{2,1,0:T(8,128)(2,1)} %fusion.11.other_ref, ...), custom_call_target="tpu_custom_call" | custom-call | flops 4000000000 | bytes 12000000 | tf_op jit(solution)/shard_map/weight_terms/pallas_call | solution.py:271
  93.1 2.1 %collective-permute-start.7 = (bf16[2,128,128]{2,1,0:T(8,128)(2,1)S(1)}, bf16[2,128,128]{2,1,0:T(8,128)(2,1)S(1)}, u32[]{:S(2)}, u32[]{:S(2)}) collective-permute-start(bf16[2,128,128]{2,1,0:T(8,128)(2,1)S(1)} %fusion.30), channel_id=1, source_target_pairs={{0,8},{8,16},{16,24},{24,0},{1,9},{9,17},{17,25},{25,1},{2,10},{10... | collective-permute-start | bytes 196616 | tf_op jit(solution)/shard_map/ppermute | solution.py:32
  95.2 7.2 %near_ahead.1.near_ref = f32[4,128,1024]{2,1,0:T(8,128)} custom-call(bf16[1024,512]{1,0:T(8,128)(2,1)} %q_ref.7, bf16[1024,512]{1,0:T(8,128)(2,1)} %k_ref.7, bf16[1024,512]{1,0:T(8,128)(2,1)} %get-tuple-element.9.v_ref, f32[4,17,1024]{2,1,0:T(8,128)} %convert_bitcast_fusion.lw_ref), custom_call_target="tpu_custom_call" | custom-call | flops 4000000000 | bytes 5000000 | tf_op jit(solution)/shard_map/near_ahead/pallas_call | solution.py:167
  102.5 2.9 %collective-permute-start.10 = (bf16[2,128,128]{2,1,0:T(8,128)(2,1)S(1)}, bf16[2,128,128]{2,1,0:T(8,128)(2,1)S(1)}, u32[]{:S(2)}, u32[]{:S(2)}) collective-permute-start(bf16[2,128,128]{2,1,0:T(8,128)(2,1)S(1)} %get-tuple-element.24), channel_id=1, source_target_pairs={{0,32},{32,0},{64,96},{96,64},{128,160},{160,128},{192,224},{224,1... | collective-permute-start | bytes 196616 | tf_op jit(solution)/shard_map/ppermute | solution.py:36
  105.5 2.2 %collective-permute-done.10 = bf16[2,128,128]{2,1,0:T(8,128)(2,1)S(1)} collective-permute-done((bf16[2,128,128]{2,1,0:T(8,128)(2,1)S(1)}, bf16[2,128,128]{2,1,0:T(8,128)(2,1)S(1)}, u32[]{:S(2)}, u32[]{:S(2)}) %collective-permute-start.10) | collective-permute-done | bytes 65568 | tf_op jit(solution)/shard_map/ppermute | solution.py:36
  107.7 3.5 %collective-permute-start.11 = (bf16[2,128,128]{2,1,0:T(8,128)(2,1)S(1)}, bf16[2,128,128]{2,1,0:T(8,128)(2,1)S(1)}, u32[]{:S(2)}, u32[]{:S(2)}) collective-permute-start(bf16[2,128,128]{2,1,0:T(8,128)(2,1)S(1)} %fusion.20), channel_id=1, source_target_pairs={{0,64},{32,96},{64,0},{96,32},{128,192},{160,224},{192,128},{224,1... | collective-permute-start | bytes 196616 | tf_op jit(solution)/shard_map/ppermute | solution.py:36
  111.2 2.2 %collective-permute-done.11 = bf16[2,128,128]{2,1,0:T(8,128)(2,1)S(1)} collective-permute-done((bf16[2,128,128]{2,1,0:T(8,128)(2,1)S(1)}, bf16[2,128,128]{2,1,0:T(8,128)(2,1)S(1)}, u32[]{:S(2)}, u32[]{:S(2)}) %collective-permute-start.11) | collective-permute-done | bytes 65568 | tf_op jit(solution)/shard_map/ppermute | solution.py:36
  113.4 7.8 %collective-permute-start.12 = (bf16[2,128,128]{2,1,0:T(8,128)(2,1)S(1)}, bf16[2,128,128]{2,1,0:T(8,128)(2,1)S(1)}, u32[]{:S(2)}, u32[]{:S(2)}) collective-permute-start(bf16[2,128,128]{2,1,0:T(8,128)(2,1)S(1)} %fusion.6), channel_id=1, source_target_pairs={{0,128},{32,160},{64,192},{96,224},{1,129},{33,161},{65,193},{97,2... | collective-permute-start | bytes 196616 | tf_op jit(solution)/shard_map/ppermute | solution.py:369
  122.9 1.4 collective-permute-start.26
  124.3 1.3 collective-permute-start.25
  125.8 4.5 %collective-permute-done.24 = bf16[8,32,512]{2,1,0:T(8,128)(2,1)S(1)} collective-permute-done((bf16[8,32,512]{2,1,0:T(8,128)(2,1)S(1)}, bf16[8,32,512]{2,1,0:T(8,128)(2,1)S(1)}, u32[]{:S(2)}, u32[]{:S(2)}) %collective-permute-start.24) | collective-permute-done | bytes 262176 | tf_op jit(solution)/shard_map/ppermute | solution.py:32
  130.3 2.2 %collective-permute-done.26 = bf16[8,32,512]{2,1,0:T(8,128)(2,1)S(1)} collective-permute-done((bf16[8,32,512]{2,1,0:T(8,128)(2,1)S(1)}, bf16[8,32,512]{2,1,0:T(8,128)(2,1)S(1)}, u32[]{:S(2)}, u32[]{:S(2)}) %collective-permute-start.26) | collective-permute-done | bytes 262176 | tf_op jit(solution)/shard_map/ppermute | solution.py:32
  132.5 2.7 %collective-permute-done.25 = bf16[8,32,512]{2,1,0:T(8,128)(2,1)S(1)} collective-permute-done((bf16[8,32,512]{2,1,0:T(8,128)(2,1)S(1)}, bf16[8,32,512]{2,1,0:T(8,128)(2,1)S(1)}, u32[]{:S(2)}, u32[]{:S(2)}) %collective-permute-start.25) | collective-permute-done | bytes 262176 | tf_op jit(solution)/shard_map/ppermute | solution.py:32
  136.1 5.5 %all-to-all-start = ((bf16[8,32,512]{2,1,0:T(8,128)(2,1)}), bf16[8,32,512]{2,1,0:T(8,128)(2,1)S(1)}, u32[]{:S(2)}, u32[]{:S(2)}) async-start(bf16[8,32,512]{2,1,0:T(8,128)(2,1)} %fusion.3), calls=%async_computation | async-start | bytes 524288 | tf_op jit(solution)/shard_map/all_to_all | solution.py:404
  143.1 6.2 %attended.1 = bf16[1024,512]{1,0:T(8,128)(2,1)} custom-call(s32[3]{0:T(128)} %pad_add_fusion.place, bf16[1024,512]{1,0:T(8,128)(2,1)} %q_ref.7, f32[4,17,1024]{2,1,0:T(8,128)} %convert_bitcast_fusion.lw_ref, f32[4,128,1024]{2,1,0:T(8,128)} %near_ahead.1.near_ref, bf16[4,128,128]{2,1,0:T(8,128)(2,1)} %select_convert_fusion.first_ref, ...), custom_call_target="tpu_custom_call" | custom-call | flops 2000000000 | bytes 5000000 | tf_op jit(solution)/shard_map/attended/pallas_call | solution.py:310
  149.4 2.7 %all-to-all-done = bf16[8,32,512]{2,1,0:T(8,128)(2,1)S(1)} async-done(((bf16[8,32,512]{2,1,0:T(8,128)(2,1)}), bf16[8,32,512]{2,1,0:T(8,128)(2,1)S(1)}, u32[]{:S(2)}, u32[]{:S(2)}) %all-to-all-start) | async-done | bytes 262176 | tf_op jit(solution)/shard_map/all_to_all | solution.py:404
  (73 shorter events, 20.9 us)
Async XLA Ops:
  10.0 2.2 %collective-permute-start.14 = (f32[2,5,128,128]{3,2,0,1:T(8,128)S(1)}, f32[2,5,128,128]{3,2,0,1:T(8,128)S(1)}, u32[]{:S(2)}, u32[]{:S(2)}) collective-permute-start(f32[2,5,128,128]{3,2,0,1:T(8,128)S(1)} %copy.13), channel_id=1, source_target_pairs={{0,4},{4,0},{1,5},{5,1},{2,6},{6,2},{3,7},{7,3},{8,12},{12,8},{9,1... | collective-permute-start | bytes 1966088 | tf_op jit(solution)/shard_map/ppermute | solution.py:36
  12.2 19.3 %copy-start.1 = (bf16[1024,512]{1,0:T(8,128)(2,1)S(1)}, bf16[1024,512]{1,0:T(8,128)(2,1)}, u32[]{:S(2)}) copy-start(bf16[1024,512]{1,0:T(8,128)(2,1)} %own.3) | copy-start | bytes 3145732
  13.4 7.2 %collective-permute-start.15 = (bf16[2,3,128,128]{3,2,0,1:T(8,128)(2,1)S(1)}, bf16[2,3,128,128]{3,2,0,1:T(8,128)(2,1)S(1)}, u32[]{:S(2)}, u32[]{:S(2)}) collective-permute-start(bf16[2,3,128,128]{3,2,0,1:T(8,128)(2,1)S(1)} %slice.156), channel_id=1, source_target_pairs={{0,32},{32,0},{64,96},{96,64},{128,160},{160,128},{192,224},{224,1... | collective-permute-start | bytes 589832 | tf_op jit(solution)/shard_map/ppermute | solution.py:36
  20.7 9.3 %collective-permute-start.16 = (bf16[2,2,128,128]{3,2,0,1:T(8,128)(2,1)S(1)}, bf16[2,2,128,128]{3,2,0,1:T(8,128)(2,1)S(1)}, u32[]{:S(2)}, u32[]{:S(2)}) collective-permute-start(bf16[2,2,128,128]{3,2,0,1:T(8,128)(2,1)S(1)} %get-tuple-element.22), channel_id=1, source_target_pairs={{0,64},{32,96},{64,0},{96,32},{128,192},{160,224},{192,128},{224,1... | collective-permute-start | bytes 393224 | tf_op jit(solution)/shard_map/ppermute | solution.py:36
  30.1 10.1 %collective-permute-start.17 = (bf16[2,128,128]{2,1,0:T(8,128)(2,1)S(1)}, bf16[2,128,128]{2,1,0:T(8,128)(2,1)S(1)}, u32[]{:S(2)}, u32[]{:S(2)}) collective-permute-start(bf16[2,128,128]{2,1,0:T(8,128)(2,1)S(1)} %fusion.21), channel_id=1, source_target_pairs={{128,0},{160,32},{192,64},{224,96},{129,1},{161,33},{193,65},{225,... | collective-permute-start | bytes 196616 | tf_op jit(solution)/shard_map/ppermute | solution.py:342
  31.5 14.2 %collective-permute-start.3 = (bf16[512,512]{1,0:T(8,128)(2,1)S(1)}, bf16[512,512]{1,0:T(8,128)(2,1)}, u32[]{:S(2)}, u32[]{:S(2)}) collective-permute-start(bf16[512,512]{1,0:T(8,128)(2,1)S(1)} %get-tuple-element.29), channel_id=1, source_target_pairs={{0,3},{1,0},{2,1},{3,2},{4,7},{5,4},{6,5},{7,6},{8,11},{9,8},{10,9... | collective-permute-start | bytes 1572872 | tf_op jit(solution)/shard_map/ppermute | solution.py:32
  32.3 15.0 %collective-permute-start = (bf16[512,512]{1,0:T(8,128)(2,1)S(1)}, bf16[512,512]{1,0:T(8,128)(2,1)}, u32[]{:S(2)}, u32[]{:S(2)}) collective-permute-start(bf16[512,512]{1,0:T(8,128)(2,1)S(1)} %get-tuple-element.30), channel_id=1, source_target_pairs={{0,1},{1,2},{2,3},{3,0},{4,5},{5,6},{6,7},{7,4},{8,9},{9,10},{10,1... | collective-permute-start | bytes 1572872 | tf_op jit(solution)/shard_map/ppermute | solution.py:32
  34.8 7.5 %collective-permute-start.21 = (f32[4,128,128]{2,1,0:T(8,128)}, f32[4,128,128]{2,1,0:T(8,128)S(1)}, u32[]{:S(2)}, u32[]{:S(2)}) collective-permute-start(f32[4,128,128]{2,1,0:T(8,128)} %get-tuple-element.13), channel_id=1, source_target_pairs={{4,0},{5,1},{6,2},{7,3},{12,8},{13,9},{14,10},{15,11},{20,16},{21,... | collective-permute-start | bytes 786440 | tf_op jit(solution)/shard_map/ppermute | solution.py:333
  40.3 7.0 %collective-permute-start.19 = (bf16[2,128,128]{2,1,0:T(8,128)(2,1)S(1)}, bf16[2,128,128]{2,1,0:T(8,128)(2,1)S(1)}, u32[]{:S(2)}, u32[]{:S(2)}) collective-permute-start(bf16[2,128,128]{2,1,0:T(8,128)(2,1)S(1)} %get-tuple-element.31), channel_id=1, source_target_pairs={{0,24},{8,0},{16,8},{24,16},{1,25},{9,1},{17,9},{25,17},{2,26},{10... | collective-permute-start | bytes 196616 | tf_op jit(solution)/shard_map/ppermute | solution.py:32
  41.2 9.8 %collective-permute-start.20 = (bf16[2,128,128]{2,1,0:T(8,128)(2,1)S(1)}, bf16[2,128,128]{2,1,0:T(8,128)(2,1)S(1)}, u32[]{:S(2)}, u32[]{:S(2)}) collective-permute-start(bf16[2,128,128]{2,1,0:T(8,128)(2,1)S(1)} %get-tuple-element.32), channel_id=1, source_target_pairs={{0,16},{8,24},{16,0},{24,8},{1,17},{9,25},{17,1},{25,9},{2,18},{10... | collective-permute-start | bytes 196616 | tf_op jit(solution)/shard_map/ppermute | solution.py:32
  42.3 17.7 %collective-permute-start.1 = (bf16[512,512]{1,0:T(8,128)(2,1)S(1)}, bf16[512,512]{1,0:T(8,128)(2,1)S(1)}, u32[]{:S(2)}, u32[]{:S(2)}) collective-permute-start(bf16[512,512]{1,0:T(8,128)(2,1)S(1)} %get-tuple-element.29), channel_id=1, source_target_pairs={{0,1},{1,2},{2,3},{3,0},{4,5},{5,6},{6,7},{7,4},{8,9},{9,10},{10,1... | collective-permute-start | bytes 1572872 | tf_op jit(solution)/shard_map/ppermute | solution.py:32
  45.7 16.1 %collective-permute-start.2 = (bf16[512,512]{1,0:T(8,128)(2,1)S(1)}, bf16[512,512]{1,0:T(8,128)(2,1)S(1)}, u32[]{:S(2)}, u32[]{:S(2)}) collective-permute-start(bf16[512,512]{1,0:T(8,128)(2,1)S(1)} %get-tuple-element.30), channel_id=1, source_target_pairs={{0,3},{1,0},{2,1},{3,2},{4,7},{5,4},{6,5},{7,6},{8,11},{9,8},{10,9... | collective-permute-start | bytes 1572872 | tf_op jit(solution)/shard_map/ppermute | solution.py:32
  47.3 22.8 %collective-permute-start.5 = (bf16[512,512]{1,0:T(8,128)(2,1)}, bf16[512,512]{1,0:T(8,128)(2,1)S(1)}, u32[]{:S(2)}, u32[]{:S(2)}) collective-permute-start(bf16[512,512]{1,0:T(8,128)(2,1)} %collective-permute-done.3.rl), channel_id=1, source_target_pairs={{0,3},{1,0},{2,1},{3,2},{4,7},{5,4},{6,5},{7,6},{8,11},{9,8},{10,9... | collective-permute-start | bytes 1572872 | tf_op jit(solution)/shard_map/ppermute | solution.py:32
  47.3 22.8 %collective-permute-start.4 = (bf16[512,512]{1,0:T(8,128)(2,1)}, bf16[512,512]{1,0:T(8,128)(2,1)S(1)}, u32[]{:S(2)}, u32[]{:S(2)}) collective-permute-start(bf16[512,512]{1,0:T(8,128)(2,1)} %collective-permute-done.lu), channel_id=1, source_target_pairs={{0,1},{1,2},{2,3},{3,0},{4,5},{5,6},{6,7},{7,4},{8,9},{9,10},{10,1... | collective-permute-start | bytes 1572872 | tf_op jit(solution)/shard_map/ppermute | solution.py:32
  51.0 8.3 %collective-permute-start.18 = (bf16[2,128,128]{2,1,0:T(8,128)(2,1)S(1)}, bf16[2,128,128]{2,1,0:T(8,128)(2,1)S(1)}, u32[]{:S(2)}, u32[]{:S(2)}) collective-permute-start(bf16[2,128,128]{2,1,0:T(8,128)(2,1)S(1)} %get-tuple-element.20), channel_id=1, source_target_pairs={{0,8},{8,16},{16,24},{24,0},{1,9},{9,17},{17,25},{25,1},{2,10},{10... | collective-permute-start | bytes 196616 | tf_op jit(solution)/shard_map/ppermute | solution.py:32
  60.0 20.0 %collective-permute-start.22 = (f32[2,128,128]{2,1,0:T(8,128)S(1)}, f32[2,128,128]{2,1,0:T(8,128)S(1)}, u32[]{:S(2)}, u32[]{:S(2)}) collective-permute-start(f32[2,128,128]{2,1,0:T(8,128)S(1)} %get-tuple-element.19), channel_id=1, source_target_pairs={{0,4},{4,0},{1,5},{5,1},{2,6},{6,2},{3,7},{7,3},{8,12},{12,8},{9,1... | collective-permute-start | bytes 393224 | tf_op jit(solution)/shard_map/ppermute | solution.py:36
  60.0 10.1 %copy-start.3 = (bf16[512,512]{1,0:T(8,128)(2,1)}, bf16[512,512]{1,0:T(8,128)(2,1)S(1)}, u32[]{:S(2)}) copy-start(bf16[512,512]{1,0:T(8,128)(2,1)S(1)} %collective-permute-done.1.ll) | copy-start | bytes 1572868
  80.0 11.2 %collective-permute-start.6 = (f32[4,128,128]{2,1,0:T(8,128)}, f32[4,128,128]{2,1,0:T(8,128)S(1)}, u32[]{:S(2)}, u32[]{:S(2)}) collective-permute-start(f32[4,128,128]{2,1,0:T(8,128)} %get-tuple-element.10), channel_id=1, source_target_pairs={{0,4},{4,0},{1,5},{5,1},{2,6},{6,2},{3,7},{7,3},{8,12},{12,8},{9,1... | collective-permute-start | bytes 786440 | tf_op jit(solution)/shard_map/ppermute | solution.py:36
  80.7 10.4 %copy-start.2 = (f32[4,128,128]{2,1,0:T(8,128)S(1)}, f32[4,128,128]{2,1,0:T(8,128)}, u32[]{:S(2)}) copy-start(f32[4,128,128]{2,1,0:T(8,128)} %get-tuple-element.10) | copy-start | bytes 786436
  90.6 30.7 %collective-permute-start.23 = (f32[4,8,32,512]{3,2,1,0:T(8,128)}, f32[4,8,32,512]{3,2,1,0:T(8,128)S(1)}, u32[]{:S(2)}, u32[]{:S(2)}) collective-permute-start(f32[4,8,32,512]{3,2,1,0:T(8,128)} %get-tuple-element.15), channel_id=1, source_target_pairs={{0,4},{4,0},{1,5},{5,1},{2,6},{6,2},{3,7},{7,3},{8,12},{12,8},{9,1... | collective-permute-start | bytes 6291464 | tf_op jit(solution)/shard_map/ppermute | solution.py:36
  91.1 11.3 %collective-permute-start.9 = (bf16[2,128,128]{2,1,0:T(8,128)(2,1)S(1)}, bf16[2,128,128]{2,1,0:T(8,128)(2,1)S(1)}, u32[]{:S(2)}, u32[]{:S(2)}) collective-permute-start(bf16[2,128,128]{2,1,0:T(8,128)(2,1)S(1)} %fusion.30), channel_id=1, source_target_pairs={{0,24},{8,0},{16,8},{24,16},{1,25},{9,1},{17,9},{25,17},{2,26},{10... | collective-permute-start | bytes 196616 | tf_op jit(solution)/shard_map/ppermute | solution.py:32
  92.0 10.4 %collective-permute-start.8 = (bf16[2,128,128]{2,1,0:T(8,128)(2,1)S(1)}, bf16[2,128,128]{2,1,0:T(8,128)(2,1)S(1)}, u32[]{:S(2)}, u32[]{:S(2)}) collective-permute-start(bf16[2,128,128]{2,1,0:T(8,128)(2,1)S(1)} %fusion.30), channel_id=1, source_target_pairs={{0,16},{8,24},{16,0},{24,8},{1,17},{9,25},{17,1},{25,9},{2,18},{10... | collective-permute-start | bytes 196616 | tf_op jit(solution)/shard_map/ppermute | solution.py:32
  93.1 9.3 %collective-permute-start.7 = (bf16[2,128,128]{2,1,0:T(8,128)(2,1)S(1)}, bf16[2,128,128]{2,1,0:T(8,128)(2,1)S(1)}, u32[]{:S(2)}, u32[]{:S(2)}) collective-permute-start(bf16[2,128,128]{2,1,0:T(8,128)(2,1)S(1)} %fusion.30), channel_id=1, source_target_pairs={{0,8},{8,16},{16,24},{24,0},{1,9},{9,17},{17,25},{25,1},{2,10},{10... | collective-permute-start | bytes 196616 | tf_op jit(solution)/shard_map/ppermute | solution.py:32
  95.2 26.1 %copy-start = (f32[4,8,32,512]{3,2,1,0:T(8,128)S(1)}, f32[4,8,32,512]{3,2,1,0:T(8,128)}, u32[]{:S(2)}) copy-start(f32[4,8,32,512]{3,2,1,0:T(8,128)} %get-tuple-element.14) | copy-start | bytes 6291460
  102.5 5.1 %collective-permute-start.10 = (bf16[2,128,128]{2,1,0:T(8,128)(2,1)S(1)}, bf16[2,128,128]{2,1,0:T(8,128)(2,1)S(1)}, u32[]{:S(2)}, u32[]{:S(2)}) collective-permute-start(bf16[2,128,128]{2,1,0:T(8,128)(2,1)S(1)} %get-tuple-element.24), channel_id=1, source_target_pairs={{0,32},{32,0},{64,96},{96,64},{128,160},{160,128},{192,224},{224,1... | collective-permute-start | bytes 196616 | tf_op jit(solution)/shard_map/ppermute | solution.py:36
  107.7 5.7 %collective-permute-start.11 = (bf16[2,128,128]{2,1,0:T(8,128)(2,1)S(1)}, bf16[2,128,128]{2,1,0:T(8,128)(2,1)S(1)}, u32[]{:S(2)}, u32[]{:S(2)}) collective-permute-start(bf16[2,128,128]{2,1,0:T(8,128)(2,1)S(1)} %fusion.20), channel_id=1, source_target_pairs={{0,64},{32,96},{64,0},{96,32},{128,192},{160,224},{192,128},{224,1... | collective-permute-start | bytes 196616 | tf_op jit(solution)/shard_map/ppermute | solution.py:36
  113.4 12.2 %collective-permute-start.12 = (bf16[2,128,128]{2,1,0:T(8,128)(2,1)S(1)}, bf16[2,128,128]{2,1,0:T(8,128)(2,1)S(1)}, u32[]{:S(2)}, u32[]{:S(2)}) collective-permute-start(bf16[2,128,128]{2,1,0:T(8,128)(2,1)S(1)} %fusion.6), channel_id=1, source_target_pairs={{0,128},{32,160},{64,192},{96,224},{1,129},{33,161},{65,193},{97,2... | collective-permute-start | bytes 196616 | tf_op jit(solution)/shard_map/ppermute | solution.py:369
  122.0 8.3 %collective-permute-start.24 = (bf16[8,32,512]{2,1,0:T(8,128)(2,1)S(1)}, bf16[8,32,512]{2,1,0:T(8,128)(2,1)S(1)}, u32[]{:S(2)}, u32[]{:S(2)}) collective-permute-start(bf16[8,32,512]{2,1,0:T(8,128)(2,1)S(1)} %get-tuple-element.26), channel_id=1, source_target_pairs={{0,8},{8,16},{16,24},{24,0},{1,9},{9,17},{17,25},{25,1},{2,10},{10... | collective-permute-start | bytes 786440 | tf_op jit(solution)/shard_map/ppermute | solution.py:32
  122.9 9.5 %collective-permute-start.26 = (bf16[8,32,512]{2,1,0:T(8,128)(2,1)S(1)}, bf16[8,32,512]{2,1,0:T(8,128)(2,1)S(1)}, u32[]{:S(2)}, u32[]{:S(2)}) collective-permute-start(bf16[8,32,512]{2,1,0:T(8,128)(2,1)S(1)} %get-tuple-element.27), channel_id=1, source_target_pairs={{0,16},{8,24},{16,0},{24,8},{1,17},{9,25},{17,1},{25,9},{2,18},{10... | collective-permute-start | bytes 786440 | tf_op jit(solution)/shard_map/ppermute | solution.py:32
  124.3 10.8 %collective-permute-start.25 = (bf16[8,32,512]{2,1,0:T(8,128)(2,1)S(1)}, bf16[8,32,512]{2,1,0:T(8,128)(2,1)S(1)}, u32[]{:S(2)}, u32[]{:S(2)}) collective-permute-start(bf16[8,32,512]{2,1,0:T(8,128)(2,1)S(1)} %get-tuple-element.28), channel_id=1, source_target_pairs={{0,24},{8,0},{16,8},{24,16},{1,25},{9,1},{17,9},{25,17},{2,26},{10... | collective-permute-start | bytes 786440 | tf_op jit(solution)/shard_map/ppermute | solution.py:32
  125.7 16.6 %collective-permute-start.13 = (bf16[2,5,128,128]{3,2,1,0:T(8,128)(2,1)S(1)}, bf16[2,5,128,128]{3,2,1,0:T(8,128)(2,1)S(1)}, u32[]{:S(2)}, u32[]{:S(2)}) collective-permute-start(bf16[2,5,128,128]{3,2,1,0:T(8,128)(2,1)S(1)} %bitcast_dynamic-update-slice_fusion), channel_id=1, source_target_pairs={{0,4},{4,0},{1,5},{5,1},{2,6},{6,2},{3,7},{7,3},{8,12},{12,8},{9,1... | collective-permute-start | bytes 983048 | tf_op jit(solution)/shard_map/ppermute | solution.py:36
  136.1 16.0 %all-to-all-start = ((bf16[8,32,512]{2,1,0:T(8,128)(2,1)}), bf16[8,32,512]{2,1,0:T(8,128)(2,1)S(1)}, u32[]{:S(2)}, u32[]{:S(2)}) async-start(bf16[8,32,512]{2,1,0:T(8,128)(2,1)} %fusion.3), calls=%async_computation | async-start | bytes 524288 | tf_op jit(solution)/shard_map/all_to_all | solution.py:404
  (3 other events, 10.0 us)

commit v2 on v0

v2 whole, which is shorter than its diff:
```python
import functools

import jax
import jax.numpy as jnp
from jax import lax
from jax.experimental import pallas as pl
from jax.experimental.pallas import tpu as pltpu
from jax.sharding import Mesh, PartitionSpec as P

BF = jnp.bfloat16
F32 = jnp.float32
HW = 128
NH = 4
TOK = 1024
BLK = 256
DEPTH = 10
FAR = 6
PART = 512
NX, NZ = 4, 8
VMEM = 24 * 1024 * 1024

NT = (((1,), (1,)), ((), ()))
TN = (((0,), (0,)), ((), ()))
NN = (((1,), (0,)), ((), ()))


def dot(a, b, dims=NN):
    return lax.dot_general(a, b, dims, preferred_element_type=F32)


def shift(value, axis, distance, size):
    return lax.ppermute(value, axis, [(i, (i + distance) % size) for i in range(size)])


def swap(value, axis, distance, size):
    return lax.ppermute(value, axis, [(i, i ^ distance) for i in range(size)])


def rows_of(lw_ref, first, count, head):
    rows = []
    for level in range(first, first + count):
        every = lw_ref[level].astype(F32)
        index = lax.broadcasted_iota(jnp.int32, every.shape, 0)
        rows.append(jnp.sum(jnp.where(index == head, every, 0.0), axis=0, keepdims=True))
    return rows


def whole(*shape):
    return pl.BlockSpec(shape, lambda *_: (0,) * len(shape))


LEVELS = whole(DEPTH + 1 + FAR, NH, TOK)


def params():
    return pltpu.CompilerParams(
        dimension_semantics=("arbitrary",), vmem_limit_bytes=VMEM
    )


def cost(us):
    return pl.CostEstimate(flops=int(us * 1.15e9), bytes_accessed=1000, transcendentals=0)


ANY = pl.BlockSpec(memory_space=pl.ANY)


def streamed(*values):
    return [pltpu.with_memory_space_constraint(value, pltpu.HBM) for value in values]


def turn_kernel(in_ref, *rest):
    turned = in_ref[...].T
    at = 0
    for out_ref in rest[1:]:
        out_ref[...] = turned[at : at + out_ref.shape[0], :]
        at += out_ref.shape[0]


def turned(value, side, count, name, after):
    rows, columns = value.shape
    part = columns // count
    return pl.pallas_call(
        turn_kernel,
        grid=(rows // side,),
        in_specs=[pl.BlockSpec((side, columns), lambda i: (i, 0)), ANY],
        out_specs=[pl.BlockSpec((part, side), lambda i: (0, i))] * count,
        out_shape=[jax.ShapeDtypeStruct((part, rows), value.dtype)] * count,
        compiler_params=params(),
        cost_estimate=cost(1.5),
        name=name,
    )(value, after)


def query_state_kernel(place, q_u, q_l, g_u, g_l, lw_ref, *rest):
    first_ref, send_ref, keep_ref, turned_ref, stack = rest[-5:]
    slot = pl.program_id(0)
    half = TOK // 2
    turned_ref[0, :, :half] = q_u[...].T
    turned_ref[0, :, half:] = q_l[...].T
    turned = turned_ref[0]
    head = lax.rem(2 * (1 - place[0]) + slot, NH)
    for digit, row in enumerate(rows_of(lw_ref, DEPTH + 1, FAR, head)):
        stack[digit * HW : (digit + 1) * HW, :] = turned * row.astype(BF)
    state = dot(stack[:, :half], g_u[...]) + dot(stack[:, half:], g_l[...])
    first_ref[0] = state[:HW]
    rest = state[HW:].reshape(FAR - 1, HW, HW)

    @pl.when(slot < 2)
    def _():
        send_ref[:, 0] = rest

    @pl.when(slot >= 2)
    def _():
        keep_ref[:, 0] = rest


def query_states(place, queries, out_grad, weights, *after):
    def head(s, place):
        return lax.rem(2 * (1 - place[0]) + s, NH)

    return pl.pallas_call(
        query_state_kernel,
        grid_spec=pltpu.PrefetchScalarGridSpec(
            num_scalar_prefetch=1,
            grid=(NH,),
            in_specs=[
                pl.BlockSpec((TOK // 2, HW), lambda s, p: (0, head(s, p))),
                pl.BlockSpec((TOK // 2, HW), lambda s, p: (1, head(s, p))),
                pl.BlockSpec((TOK // 2, HW), lambda s, p: (0, head(s, p))),
                pl.BlockSpec((TOK // 2, HW), lambda s, p: (1, head(s, p))),
                LEVELS,
            ]
            + [ANY] * len(after),
            out_specs=[
                pl.BlockSpec((1, HW, HW), lambda s, p: (s, 0, 0)),
                pl.BlockSpec((FAR - 1, 1, HW, HW), lambda s, p: (0, jnp.minimum(s, 1), 0, 0)),
                pl.BlockSpec((FAR - 1, 1, HW, HW), lambda s, p: (0, jnp.maximum(s - 2, 0), 0, 0)),
                pl.BlockSpec((1, HW, TOK), lambda s, p: (head(s, p), 0, 0)),
            ],
            scratch_shapes=[pltpu.VMEM((FAR * HW, TOK), BF)],
        ),
        out_shape=[
            jax.ShapeDtypeStruct((NH, HW, HW), F32),
            jax.ShapeDtypeStruct((FAR - 1, 2, HW, HW), F32),
            jax.ShapeDtypeStruct((FAR - 1, 2, HW, HW), F32),
            pltpu.HBM((NH, HW, TOK), BF),
        ],
        compiler_params=params(),
        cost_estimate=cost(4),
        name="query_states",
    )(place, *streamed(queries, queries, out_grad, out_grad, weights), *after)


SIDES = TOK // BLK
SQUARES = [(low, high) for low in range(SIDES) for high in range(low, SIDES)]


def diagonal(levels, start, differ, causal):
    columns = slice(start, start + HW)
    weight = jnp.broadcast_to(levels[0][:, columns], (HW, HW))
    for level in range(1, HW.bit_length()):
        weight = jnp.where(differ >= 1 << (level - 1), levels[level][:, columns], weight)
    return jnp.where(causal, weight, 0.0)


def near_kernel(base, k_ref, turned_ref, g_ref, lw_ref, *rest):
    back_ref, *near_refs = rest[-3:]
    levels = rows_of(lw_ref, 0, DEPTH + 1, base + pl.program_id(0))
    earlier = lax.broadcasted_iota(jnp.int32, (HW, HW), 0)
    later = lax.broadcasted_iota(jnp.int32, (HW, HW), 1)
    differ, causal = earlier ^ later, earlier <= later
    zero = jnp.zeros((HW, HW), BF)
    middle = HW.bit_length()
    total = None
    for index, (low, high) in enumerate(SQUARES):
        columns = slice(high * BLK, (high + 1) * BLK)
        scores = dot(k_ref[low * BLK : (low + 1) * BLK, :], turned_ref[0, :, columns])
        if low != high:
            level = BLK.bit_length() + (high ^ low).bit_length() - 1
            square = (scores * levels[level][:, columns]).astype(BF)
        else:
            start = high * BLK
            across = levels[middle][:, start + HW : start + BLK]
            upper = scores[:HW, :HW] * diagonal(levels, start, differ, causal)
            lower = scores[HW:, HW:] * diagonal(levels, start + HW, differ, causal)
            top = jnp.concatenate([upper, scores[:HW, HW:] * across], axis=1).astype(BF)
            square = jnp.concatenate(
                [top, jnp.concatenate([zero, lower.astype(BF)], axis=1)], axis=0
            )
        near_refs[index // 5][0, index % 5] = square
        term = dot(square, g_ref[columns, :])
        total = term if low == high else total + term
        if high == SIDES - 1:
            back_ref[low * BLK : (low + 1) * BLK, :] = total


def near(base, keys, turned, out_grad, weights, *after):
    head = pl.BlockSpec((TOK, HW), lambda h: (0, base + h))
    return pl.pallas_call(
        functools.partial(near_kernel, base),
        grid=(2,),
        in_specs=[head, pl.BlockSpec((1, HW, TOK), lambda h: (base + h, 0, 0)), head, LEVELS]
        + [ANY] * len(after),
        out_specs=[
            pl.BlockSpec((TOK, HW), lambda h: (0, h)),
            pl.BlockSpec((1, 5, BLK, BLK), lambda h: (h, 0, 0, 0)),
            pl.BlockSpec((1, 5, BLK, BLK), lambda h: (h, 0, 0, 0)),
        ],
        out_shape=[
            jax.ShapeDtypeStruct((TOK, 2 * HW), F32),
            pltpu.HBM((2, 5, BLK, BLK), BF),
            pltpu.HBM((2, 5, BLK, BLK), BF),
        ],
        compiler_params=params(),
        cost_estimate=cost(3.2),
        name="near",
    )(keys, *streamed(turned), out_grad, weights, *after)


HALF = PART // 2


def begin_values_kernel(place, own, left, right, w_ref, *rest):
    me = place[1]
    total = None
    for distance, part in ((0, own), (3, left), (1, right)):
        at = pl.multiple_of(lax.rem(me + distance, 4) * PART, PART)
        term = dot(w_ref[:, pl.ds(at, PART)], part[...])
        total = term if total is None else total + term
    rest[-1][...] = total


def end_values_kernel(place, total_ref, fu, fl, w_upper, w_lower, k_ref, *rest):
    v_ref, state_ref = rest[-2:]
    tile = pl.program_id(0)
    core = place[0]
    far = dot(w_upper[...], fu[...]) + dot(w_lower[...], fl[...])
    v_ref[...] = (total_ref[...] + far).astype(BF)

    @pl.when(tile == 0)
    def _():
        state_ref[...] = jnp.zeros_like(state_ref)

    for slot in range(NH):
        at = pl.multiple_of(lax.rem(2 * (1 - core) + slot, NH) * HW, HW)
        state_ref[slot] += dot(v_ref[pl.ds(at, HW), :], k_ref[:, pl.ds(at, HW)])


def begin_values(place, parts, turned_weight, *after):
    wide = pl.BlockSpec((PART, BLK), lambda i, p: (0, i))
    return pl.pallas_call(
        begin_values_kernel,
        grid_spec=pltpu.PrefetchScalarGridSpec(
            num_scalar_prefetch=1,
            grid=(TOK // BLK,),
            in_specs=[wide] * 3 + [whole(NH * HW, 4 * PART)] + [ANY] * len(after),
            out_specs=wide,
        ),
        out_shape=jax.ShapeDtypeStruct((NH * HW, TOK), F32),
        compiler_params=params(),
        cost_estimate=cost(3.5),
        name="begin_values",
    )(place, *parts, turned_weight, *after)


def end_values(place, total, parts, turned_weight, keys, *after):
    tile = pl.BlockSpec((HALF, BLK), lambda i, p: (0, i))
    wide = pl.BlockSpec((PART, BLK), lambda i, p: (0, i))

    def weight(offset):
        return pl.BlockSpec((NH * HW, HALF), lambda i, p: (0, lax.rem(p[1] + 2, 4) * 2 + offset))

    return pl.pallas_call(
        end_values_kernel,
        grid_spec=pltpu.PrefetchScalarGridSpec(
            num_scalar_prefetch=1,
            grid=(TOK // BLK,),
            in_specs=[
                wide,
                tile,
                tile,
                weight(0),
                weight(1),
                pl.BlockSpec((BLK, NH * HW), lambda i, p: (i, 0)),
            ]
            + [ANY] * len(after),
            out_specs=[wide, pl.BlockSpec((NH, HW, HW), lambda i, p: (0, 0, 0))],
        ),
        out_shape=[
            pltpu.HBM((NH * HW, TOK), BF),
            jax.ShapeDtypeStruct((NH, HW, HW), F32),
        ],
        compiler_params=params(),
        cost_estimate=cost(3.7),
        name="end_values",
    )(place, total, *parts, turned_weight, turned_weight, keys, *after)


def share_out(place, term, plane, send_ref, keep_ref):
    core, col = place[0], place[2]
    for x in range(NX):
        turn = lax.rem(x - col + NX, NX)
        theirs = pl.multiple_of(x * 64 + (1 - core) * 32, 32)
        ours = pl.multiple_of(x * 64 + core * 32, 32)
        send_ref[turn, plane] = term[pl.ds(theirs, 32), :]
        keep_ref[turn, plane] = term[pl.ds(ours, 32), :]


def distance_of(step):
    return jnp.where(step == 0, 0, jnp.where(step == 1, 3, jnp.where(step == 2, 1, 2)))


def terms_kernel(place, near_a, near_b, k_ref, mine_ref, other_ref, *rest):
    own, left, right, fu, fl = rest[:5]
    send_ref, keep_ref, grad, term = rest[-4:]
    core = place[0]
    step = pl.program_id(0)

    @pl.when(step == 0)
    def _():
        for slot in range(NH):
            at = pl.multiple_of(lax.rem(2 * core + slot, NH) * HW, HW)
            state = mine_ref[slot] if slot < 2 else other_ref[slot - 2]
            far = dot(k_ref[:, pl.ds(at, HW)], state)
            columns = slice(slot % 2 * HW, (slot % 2 + 1) * HW)
            lower_heads = (core == 0) == (slot < 2)
            near = jnp.where(lower_heads, near_a[:, columns], near_b[:, columns])
            grad[:, pl.ds(at, HW)] = (near + far).astype(BF)

    halves = [(part.at[:HALF, :], part.at[HALF:, :]) for part in (own, left, right)]
    for index, pair in enumerate((*halves, (fu, fl))):

        @pl.when(step == index)
        def _(pair=pair):
            for plane in range(2):
                term[plane] = dot(pair[plane][...], grad[...])
                share_out(place, term.at[plane], plane, send_ref, keep_ref)


def shares():
    return pl.BlockSpec(
        (NX, 2, 32, NH * HW), lambda i, p: (0, lax.rem(p[1] + distance_of(i), 4), 0, 0)
    )


def weight_terms(place, near, keys, mine, other, parts, *after):
    return pl.pallas_call(
        terms_kernel,
        grid_spec=pltpu.PrefetchScalarGridSpec(
            num_scalar_prefetch=1,
            grid=(4,),
            in_specs=[
                whole(TOK, 2 * HW),
                whole(TOK, 2 * HW),
                whole(TOK, NH * HW),
                whole(2, HW, HW),
                whole(2, HW, HW),
            ]
            + [whole(PART, TOK)] * 3
            + [whole(HALF, TOK)] * 2
            + [ANY] * len(after),
            out_specs=[shares(), shares()],
            scratch_shapes=[
                pltpu.VMEM((TOK, NH * HW), BF),
                pltpu.VMEM((2, HALF, NH * HW), F32),
            ],
        ),
        out_shape=[
            jax.ShapeDtypeStruct((NX, NZ, 32, NH * HW), F32),
            pltpu.HBM((NX, NZ, 32, NH * HW), F32),
        ],
        compiler_params=params(),
        cost_estimate=cost(5),
        name="weight_terms",
    )(place, *near, keys, mine, other, *parts, *after)


def pair_kernel(place, kept_u, kept_l, got, own_ref, *messages):
    for plane, kept in enumerate((kept_u, kept_l)):
        own_ref[plane] = kept[0, 0] + got[0, plane]
        for turn in range(1, NX):
            messages[turn - 1][plane] = (kept[turn, 0] + got[turn, plane]).astype(BF)


def pair_sums(place, kept, got):
    def plane(offset):
        return pl.BlockSpec(
            (NX, 1, 32, NH * HW),
            lambda i, p: (0, 2 * lax.rem(p[1] + distance_of(i), 4) + offset, 0, 0),
        )

    return pl.pallas_call(
        pair_kernel,
        grid_spec=pltpu.PrefetchScalarGridSpec(
            num_scalar_prefetch=1,
            grid=(4,),
            in_specs=[plane(0), plane(1), shares()],
            out_specs=[
                pl.BlockSpec((2, 32, NH * HW), lambda i, p: (lax.rem(p[1] + distance_of(i), 4), 0, 0))
            ]
            * 4,
        ),
        out_shape=[jax.ShapeDtypeStruct((NZ, 32, NH * HW), F32)]
        + [jax.ShapeDtypeStruct((NZ, 32, NH * HW), BF)] * 3,
        compiler_params=params(),
        cost_estimate=cost(1.1),
        name="pair_sums",
    )(place, *streamed(kept, kept), got)


def far_product(levels, first, turned_ref, lw_ref, place, total, stack):
    head = lax.rem(2 * place[0] + pl.program_id(0), NH)
    rows = rows_of(lw_ref, DEPTH + 1 + first, 3, head)
    for index, level in enumerate(levels):
        stack[index * HW : (index + 1) * HW, :] = level
    product = dot(stack[...], turned_ref[0])
    for index in range(3):
        total = total + product[index * HW : (index + 1) * HW, :] * rows[index]
    return total


def begin_attended_kernel(place, turned_ref, lw_ref, v_ref, *rest):
    near_a, near_b, zero_ref, far_ref = rest[:2], rest[2:4], rest[4], rest[5]
    out_ref, stack = rest[-2:]
    lower_heads = (place[0] == 0) == (pl.program_id(0) < 2)

    def add(near_refs):
        for high in range(SIDES):
            columns = slice(high * BLK, (high + 1) * BLK)
            total = None
            for index, (low, other) in enumerate(SQUARES):
                if other == high:
                    term = dot(v_ref[:, low * BLK : (low + 1) * BLK], near_refs[index // 5][0, index % 5])
                    total = term if total is None else total + term
            out_ref[0, :, columns] = total

    pl.when(lower_heads)(lambda: add(near_a))
    pl.when(jnp.logical_not(lower_heads))(lambda: add(near_b))
    levels = (zero_ref[0], far_ref[0, 0], far_ref[1, 0])
    out_ref[0] = far_product(levels, 0, turned_ref, lw_ref, place, out_ref[0], stack)


def end_attended_kernel(place, turned_ref, lw_ref, total_u, total_l, far_ref, out_ref, stack):
    levels = (far_ref[0, 0], far_ref[1, 0], far_ref[2, 0])
    total = jnp.concatenate([total_u[0], total_l[0]], axis=0)
    total = far_product(levels, 3, turned_ref, lw_ref, place, total, stack)
    out_ref[...] = total.astype(BF).T


def begin_attended(place, turned, weights, values, near, zero, far, *after):
    def head(s, p):
        return lax.rem(2 * p[0] + s, NH)

    def pair(lower):
        def block(s, p):
            reads = (p[0] == 0) == (s < 2) if lower else (p[0] == 0) != (s < 2)
            idle = jnp.where(s < 2, 0, 1)
            return (jnp.where(reads, lax.rem(s, 2), idle), 0, 0, 0)

        return pl.BlockSpec((1, 5, BLK, BLK), block)

    return pl.pallas_call(
        begin_attended_kernel,
        grid_spec=pltpu.PrefetchScalarGridSpec(
            num_scalar_prefetch=1,
            grid=(NH,),
            in_specs=[
                pl.BlockSpec((1, HW, TOK), lambda s, p: (head(s, p), 0, 0)),
                LEVELS,
                pl.BlockSpec((HW, TOK), lambda s, p: (head(s, p), 0)),
                pair(True),
                pair(True),
                pair(False),
                pair(False),
                pl.BlockSpec((1, HW, HW), lambda s, p: (s, 0, 0)),
                pl.BlockSpec((2, 1, HW, HW), lambda s, p: (0, s, 0, 0)),
            ]
            + [ANY] * len(after),
            out_specs=pl.BlockSpec((1, HW, TOK), lambda s, p: (s, 0, 0)),
            scratch_shapes=[pltpu.VMEM((3 * HW, HW), BF)],
        ),
        out_shape=pltpu.HBM((NH, HW, TOK), F32),
        compiler_params=params(),
        cost_estimate=cost(0.3),
        name="begin_attended",
    )(
        place,
        *streamed(turned),
        weights,
        *streamed(values, *near),
        zero,
        far,
        *after,
    )


def end_attended(place, turned, weights, total, far):
    def head(s, p):
        return lax.rem(2 * p[0] + s, NH)

    return pl.pallas_call(
        end_attended_kernel,
        grid_spec=pltpu.PrefetchScalarGridSpec(
            num_scalar_prefetch=1,
            grid=(NH,),
            in_specs=[
                pl.BlockSpec((1, HW, TOK), lambda s, p: (head(s, p), 0, 0)),
                LEVELS,
                pl.BlockSpec((1, HW // 2, TOK), lambda s, p: (s, 0, 0)),
                pl.BlockSpec((1, HW // 2, TOK), lambda s, p: (s, 1, 0)),
                pl.BlockSpec((3, 1, HW, HW), lambda s, p: (0, s, 0, 0)),
            ],
            out_specs=pl.BlockSpec((TOK, HW), lambda s, p: (0, head(s, p))),
            scratch_shapes=[pltpu.VMEM((3 * HW, HW), BF)],
        ),
        out_shape=jax.ShapeDtypeStruct((TOK, NH * HW), BF),
        compiler_params=params(),
        cost_estimate=cost(0.3),
        name="end_attended",
    )(place, *streamed(turned), weights, *streamed(total, total), far)


def behind(value, *made):
    return lax.optimization_barrier((value, *made))[0]


def both(mine):
    return jnp.concatenate([mine, swap(mine, "core", 1, 2)], axis=1)


def local(hidden_in, value_weight, queries, keys, level_weights, out_grad):
    z, x, core, me = (lax.axis_index(a) for a in ("z", "x", "core", "head"))
    place = jnp.stack([core, me, x]).astype(jnp.int32)

    first, send, keep, turned_queries = query_states(place, queries, out_grad, level_weights)
    send_got = swap(send, "core", 1, 2)

    pairs = keep + send_got
    message = pairs[2:].astype(BF)

    (own,) = turned(hidden_in, BLK, 1, "turn_features", message)
    left = shift(own, "head", 1, 4)
    right = shift(own, "head", 3, 4)
    fu = shift(left[:HALF], "head", 1, 4)
    fl = shift(right[HALF:], "head", 3, 4)

    got = swap(message, "z", 1, NZ)
    total = jnp.where(z & 1 == 0, got[0].astype(F32), 0.0)
    level_4, level_5 = pairs[3] + got[1].astype(F32), pairs[4] + got[2].astype(F32)
    message = behind(jnp.stack([level_4, level_5]).astype(BF), own)
    got = swap(message, "z", 2, NZ)
    first_got = lax.ppermute(first, "core", [(1, 0)])
    back_a, *near_a = near(0, keys, turned_queries, out_grad, level_weights, message)
    (turned_weight,) = turned(value_weight, PART, 1, "turn_weight", message)
    total = total + jnp.where(z & 2 == 0, got[0].astype(F32), 0.0)
    message = behind((level_5 + got[1].astype(F32)).astype(BF), back_a, turned_weight)
    got = lax.ppermute(message, "z", [(i + 4, i) for i in range(4)])
    back_b, *near_b = near(2, keys, turned_queries, out_grad, level_weights, message)
    total = total + behind(got, back_b, left, right).astype(F32)
    summed = total
    for distance in (1, 3, 2):
        to = (x + distance) % NX
        level = jnp.where(to ^ x == 1, pairs[0], pairs[1])
        message = (total + jnp.where(to < x, level, 0.0)).astype(BF)
        summed = summed + shift(message, "x", distance, NX).astype(F32)
    begun = begin_values(place, (own, left, right), turned_weight, message)
    values, state = end_values(place, begun, (fu, fl), turned_weight, keys, message)
    other = swap(behind(summed, state), "core", 1, 2)
    mine = (summed + first_got[:2]).astype(BF)
    other = (other + first_got[2:]).astype(BF)

    got = swap(state, "core", 1, 2)
    zero = jnp.where(core == 1, got, 0.0).astype(BF)
    pair = state[2:] + got[:2]
    message = pair.astype(BF)
    parts = (own, left, right, fu, fl)
    send, keep = weight_terms(place, (back_a, back_b), keys, mine, other, parts, message)
    send_got = swap(send, "core", 1, 2)

    by_one, by_two, by_three = (shift(message, "x", d, NX).astype(F32) for d in (1, 2, 3))
    level_1 = jnp.where(x & 1 == 1, by_one, 0.0)
    level_2 = jnp.where(x == 2, by_one + by_two, jnp.where(x == 3, by_two + by_three, 0.0))
    running = pair + by_one + by_two + by_three
    rows, *messages = pair_sums(place, keep, send_got)
    message = behind(running.astype(BF), rows)
    first, second, third = (shift(messages[d - 1], "x", d, NX) for d in (1, 3, 2))
    rows = rows + first.astype(F32) + second.astype(F32) + third.astype(F32)
    got = swap(message, "z", 1, NZ).astype(F32)
    level_3 = jnp.where(z & 1 == 1, got, 0.0)
    running = running + got
    lower_levels = both(jnp.stack([level_1, level_2]).astype(BF))
    message = behind(running.astype(BF), first)
    got = swap(message, "z", 2, NZ).astype(F32)
    begun = begin_attended(
        place, turned_queries, level_weights, values, (*near_a, *near_b), zero, lower_levels, message
    )
    level_4 = jnp.where(z & 2 == 2, got, 0.0)
    running = running + got
    rows = rows.astype(BF)
    message = behind(running.astype(BF), begun)
    level_5 = lax.ppermute(message, "z", [(i, i + 4) for i in range(4)])
    rows = lax.all_to_all(rows, "z", 0, 0, tiled=True)
    weight_grad = rows.astype(F32).sum(axis=0)
    upper_levels = behind(jnp.stack([level_3.astype(BF), level_4.astype(BF), level_5]), rows)
    attended = end_attended(place, turned_queries, level_weights, begun, both(upper_levels))
    return attended, weight_grad


def solution(mesh):
    fine = Mesh(mesh.devices.reshape(NZ, NX, 2, 4), ("z", "x", "core", "head"))
    seq = ("z", "x", "core")
    return jax.shard_map(
        local,
        mesh=fine,
        in_specs=(
            P(seq, "head"),
            P(None, "head"),
            P(seq, "head"),
            P(seq, "head"),
            P(None, "head", seq),
            P(seq, "head"),
        ),
        out_specs=(P(seq, "head"), P(seq, "head")),
        check_vma=False,
    )
```

time: 378 us -> 132 us (0.35)
  waiting for transfers between devices: 254 us -> 37 us
  matrix products: 53.6 us -> 0 us
  Pallas kernels: 0 us -> 46.2 us
  starting transfers between devices: 22 us -> 44.1 us
  local copies, waits for them, and re-layouts: 17.4 us -> 0.12 us
  between operations: 14.6 us -> 0.96 us
  other arithmetic: 14 us -> 2.29 us
    psum x1 -> x0, waiting for transfers between devices: 131 us -> none  [local(): summed = lax.psum(local_term, 'seq')]
    ppermute x12 -> x26, waiting for transfers between devices: 122 us -> 37 us  [the longest x13 23 us: shift(): lax.ppermute(value, axis, [(i, (i + distance) % size) for i in range(size)])]
    dot_general x27 -> x0, matrix products: 53.6 us -> none  [the longest x2 20.3 us: near_part(): jnp.einsum('thd,shd->hts', queries3[first:last], keys3[:last], preferred_...]
    pallas_call x0 -> x11, Pallas kernels: none -> 46.2 us  [the longest x2 10.3 us: near(): pl.pallas_call(functools.partial(near_kernel, base), grid=(2,), in_specs=...]
    ppermute x12 -> x26, starting transfers between devices: 21.9 us -> 36.5 us  [the longest x13 18.3 us: shift(): lax.ppermute(value, axis, [(i, (i + distance) % size) for i in range(size)])]
    slice x12 -> x3, local copies, waits for them, and re-layouts: 9.53 us -> 0.1 us  [the longest x1 0.03 us: local(): fl = shift(right[HALF:], 'head', 3, 4)]
    all_to_all x0 -> x1, starting transfers between devices: none -> 7.58 us  [local(): rows = lax.all_to_all(rows, 'z', 0, 0, tiled=True)]
    le x2 -> x0, other arithmetic: 7.22 us -> none  [near_part(): weight = jnp.where(earlier <= later, weight, 0.0)]
  transfers between devices with their start and end apart: 14 -> 27, of which waited for: 11 -> 16; matrix products, arithmetic and copies ran while one was open for 20% -> 2% of each run, Pallas kernels for 0% -> 17%
where the time goes in v2:
time: 132 us; the launch traced here: 131 us
  Pallas kernels  46.2 us (35%)
  starting transfers between devices  44.1 us (33%)
  waiting for transfers between devices  37 us (28%)
  other arithmetic  2.29 us (2%)
    ppermute x13, waiting for transfers between devices, shift(): lax.ppermute(value, axis, [(i, (i + distance) % size) for i in range(size)])  23 us
    ppermute x13, starting transfers between devices, shift(): lax.ppermute(value, axis, [(i, (i + distance) % size) for i in range(size)])  18.3 us
    pallas_call x2, Pallas kernels, near(): pl.pallas_call(functools.partial(near_kernel, base), grid=(2,), in_specs=...  10.3 us
    ppermute x10, starting transfers between devices, swap(): return lax.ppermute(value, axis, [(i, i ^ distance) for i in range(size)])  10.1 us
    ppermute x10, waiting for transfers between devices, swap(): return lax.ppermute(value, axis, [(i, i ^ distance) for i in range(size)])  8.44 us
    all_to_all x1, starting transfers between devices, local(): rows = lax.all_to_all(rows, 'z', 0, 0, tiled=True)  7.58 us
    pallas_call x1, Pallas kernels, begin_attended(): pl.pallas_call(begin_attended_kernel, grid_spec=pltpu.PrefetchScalarGridS...  7.21 us
    pallas_call x1, Pallas kernels, query_states(): pl.pallas_call(query_state_kernel, grid_spec=pltpu.PrefetchScalarGridSpec...  5.85 us
  transfers between devices with their start and end apart: 27, of which 16 were waited for; matrix products, arithmetic and copies ran while one was open for 2% of the time, Pallas kernels for 17%

profile of v2, /device:TPU:30, one launch (start us, length us, event | category | flops | bytes accessed | tf_op | source)
XLA Modules:
  0.0 130.7 jit_solution(12879525660654842028)
XLA Ops:
  0.7 5.9 %query_states.1 = (f32[4,128,128]{2,1,0:T(8,128)S(1)}, f32[5,2,128,128]{3,2,1,0:T(8,128)S(1)}, f32[5,2,128,128]{3,2,1,0:T(8,128)S(1)}, bf16[4,128,1024]{2,1,0:T(8,128)(2,1)}) custom-call(s32[3]{0:T(128)S(1)} %pad_add_fusion.place, bf16[1024,512]{1,0:T(8,128)(2,1)} %q_l.1, bf16[1024,512]{1,0:T(8,128)(2,1)} %q_l.1, bf16[1024,512]{1,0:T(8,128)(2,1)} %g_ref.3, ...), custom_call_target="tpu_custom_call" | custom-call | flops 4600000000 | bytes 1000 | tf_op jit(solution)/shard_map/query_states/pallas_call | solution.py:122
  6.6 2.1 %collective-permute-done = f32[5,2,128,128]{3,2,1,0:T(8,128)S(1)} collective-permute-done((f32[5,2,128,128]{3,2,1,0:T(8,128)S(1)}, f32[5,2,128,128]{3,2,1,0:T(8,128)S(1)}, u32[]{:S(2)}, u32[]{:S(2)}) %collective-permute-start) | collective-permute-done | bytes 655392 | tf_op jit(solution)/shard_map/ppermute | solution.py:36
  8.8 2.0 %collective-permute-start.3 = (bf16[3,2,128,128]{3,2,1,0:T(8,128)(2,1)S(1)}, bf16[3,2,128,128]{3,2,1,0:T(8,128)(2,1)S(1)}, u32[]{:S(2)}, u32[]{:S(2)}) collective-permute-start(bf16[3,2,128,128]{3,2,1,0:T(8,128)(2,1)S(1)} %slice.139.rest_0_), channel_id=1, source_target_pairs={{0,32},{32,0},{64,96},{96,64},{128,160},{160,128},{192,224},{224,1... | collective-permute-start | bytes 589832 | tf_op jit(solution)/shard_map/ppermute | solution.py:36
  13.1 1.8 %collective-permute-start.2 = (bf16[512,1024]{1,0:T(8,128)(2,1)S(1)}, bf16[512,1024]{1,0:T(8,128)(2,1)S(1)}, u32[]{:S(2)}, u32[]{:S(2)}) collective-permute-start(bf16[512,1024]{1,0:T(8,128)(2,1)S(1)} %turn_features.1.own.rest_0_), channel_id=1, source_target_pairs={{0,3},{1,0},{2,1},{3,2},{4,7},{5,4},{6,5},{7,6},{8,11},{9,8},{10,9... | collective-permute-start | bytes 3145736 | tf_op jit(solution)/shard_map/ppermute | solution.py:32
  16.1 3.4 %collective-permute-start.4 = (bf16[2,2,128,128]{3,2,1,0:T(8,128)(2,1)S(1)}, bf16[2,2,128,128]{3,2,1,0:T(8,128)(2,1)S(1)}, u32[]{:S(2)}, u32[]{:S(2)}) collective-permute-start(bf16[2,2,128,128]{3,2,1,0:T(8,128)(2,1)S(1)} %pad_maximum_fusion.3.rest_0_), channel_id=1, source_target_pairs={{0,64},{32,96},{64,0},{96,32},{128,192},{160,224},{192,128},{224,1... | collective-permute-start | bytes 393224 | tf_op jit(solution)/shard_map/ppermute | solution.py:36
  19.4 5.2 %near.2 = (f32[1024,256]{1,0:T(8,128)S(1)}, bf16[2,5,256,256]{3,2,1,0:T(8,128)(2,1)}, bf16[2,5,256,256]{3,2,1,0:T(8,128)(2,1)}) custom-call(bf16[1024,512]{1,0:T(8,128)(2,1)S(1)} %copy-done.4, bf16[4,128,1024]{2,1,0:T(8,128)(2,1)} %get-tuple-element.28.turned_ref, bf16[1024,512]{1,0:T(8,128)(2,1)S(1)} %copy-done.3, bf16[17,4,1024]{2,1,0:T(4,128)(2,1)S(1)} %copy-done, ...), custom_call_target="tpu_custom_call" | custom-call | flops 3680000000 | bytes 1000 | tf_op jit(solution)/shard_map/near/pallas_call | solution.py:200
  26.9 5.1 %near.3 = (f32[1024,256]{1,0:T(8,128)S(1)}, bf16[2,5,256,256]{3,2,1,0:T(8,128)(2,1)}, bf16[2,5,256,256]{3,2,1,0:T(8,128)(2,1)}) custom-call(bf16[1024,512]{1,0:T(8,128)(2,1)S(1)} %copy-done.4, bf16[4,128,1024]{2,1,0:T(8,128)(2,1)} %get-tuple-element.28.turned_ref, bf16[1024,512]{1,0:T(8,128)(2,1)S(1)} %copy-done.3, bf16[17,4,1024]{2,1,0:T(4,128)(2,1)S(1)} %copy-done, ...), custom_call_target="tpu_custom_call" | custom-call | flops 3680000000 | bytes 1000 | tf_op jit(solution)/shard_map/near/pallas_call | solution.py:200
  32.1 3.6 %collective-permute-done.5 = bf16[2,128,128]{2,1,0:T(8,128)(2,1)S(1)} collective-permute-done((bf16[2,128,128]{2,1,0:T(8,128)(2,1)S(1)}, bf16[2,128,128]{2,1,0:T(8,128)(2,1)S(1)}, u32[]{:S(2)}, u32[]{:S(2)}) %collective-permute-start.5) | collective-permute-done | bytes 65568 | tf_op jit(solution)/shard_map/ppermute | solution.py:558
  35.7 3.1 %collective-permute-done.1.left.rest_1_ = bf16[512,1024]{1,0:T(8,128)(2,1)S(1)} collective-permute-done((bf16[512,1024]{1,0:T(8,128)(2,1)S(1)}, bf16[512,1024]{1,0:T(8,128)(2,1)S(1)}, u32[]{:S(2)}, u32[]{:S(2)}) %collective-permute-start.1) | collective-permute-done | bytes 1048608 | tf_op jit(solution)/shard_map/ppermute | solution.py:32
  38.8 1.6 %collective-permute-done.2.right.rest_2_ = bf16[512,1024]{1,0:T(8,128)(2,1)S(1)} collective-permute-done((bf16[512,1024]{1,0:T(8,128)(2,1)S(1)}, bf16[512,1024]{1,0:T(8,128)(2,1)S(1)}, u32[]{:S(2)}, u32[]{:S(2)}) %collective-permute-start.2) | collective-permute-done | bytes 1048608 | tf_op jit(solution)/shard_map/ppermute | solution.py:32
  41.0 1.5 %collective-permute-start.14 = (bf16[2,128,128]{2,1,0:T(8,128)(2,1)S(1)}, bf16[2,128,128]{2,1,0:T(8,128)(2,1)S(1)}, u32[]{:S(2)}, u32[]{:S(2)}) collective-permute-start(bf16[2,128,128]{2,1,0:T(8,128)(2,1)S(1)} %get-tuple-element.59), channel_id=1, source_target_pairs={{0,24},{8,0},{16,8},{24,16},{1,25},{9,1},{17,9},{25,17},{2,26},{10... | collective-permute-start | bytes 196616 | tf_op jit(solution)/shard_map/ppermute | solution.py:32
  44.5 2.0 %collective-permute-start.7 = (bf16[256,1024]{1,0:T(8,128)(2,1)S(1)}, bf16[256,1024]{1,0:T(8,128)(2,1)S(1)}, u32[]{:S(2)}, u32[]{:S(2)}) collective-permute-start(bf16[256,1024]{1,0:T(8,128)(2,1)S(1)} %slice.80), channel_id=1, source_target_pairs={{0,3},{1,0},{2,1},{3,2},{4,7},{5,4},{6,5},{7,6},{8,11},{9,8},{10,9... | collective-permute-start | bytes 1572872 | tf_op jit(solution)/shard_map/ppermute | solution.py:32
  46.5 3.4 %begin_values.1.total_ref = f32[512,1024]{1,0:T(8,128)S(1)} custom-call(s32[3]{0:T(128)S(1)} %pad_add_fusion.place, bf16[512,1024]{1,0:T(8,128)(2,1)S(1)} %turn_features.1.own.rest_0_, bf16[512,1024]{1,0:T(8,128)(2,1)S(1)} %collective-permute-done.1.left.rest_1_, bf16[512,1024]{1,0:T(8,128)(2,1)S(1)} %collective-permute-done.2.right.rest_2_, ...), custom_call_target="tpu_custom_call" | custom-call | flops 4024999936 | bytes 1000 | tf_op jit(solution)/shard_map/begin_values/pallas_call | solution.py:252
  50.0 7.2 %collective-permute-done.6.fu.rest_3_ = bf16[256,1024]{1,0:T(8,128)(2,1)S(1)} collective-permute-done((bf16[256,1024]{1,0:T(8,128)(2,1)S(1)}, bf16[256,1024]{1,0:T(8,128)(2,1)S(1)}, u32[]{:S(2)}, u32[]{:S(2)}) %collective-permute-start.6) | collective-permute-done | bytes 524320 | tf_op jit(solution)/shard_map/ppermute | solution.py:32
  57.3 1.5 %collective-permute-done.7.fl.rest_4_ = bf16[256,1024]{1,0:T(8,128)(2,1)S(1)} collective-permute-done((bf16[256,1024]{1,0:T(8,128)(2,1)S(1)}, bf16[256,1024]{1,0:T(8,128)(2,1)S(1)}, u32[]{:S(2)}, u32[]{:S(2)}) %collective-permute-start.7) | collective-permute-done | bytes 524320 | tf_op jit(solution)/shard_map/ppermute | solution.py:32
  58.8 4.1 %end_values.1 = (bf16[512,1024]{1,0:T(8,128)(2,1)}, f32[4,128,128]{2,1,0:T(8,128)S(1)}) custom-call(s32[3]{0:T(128)S(1)} %pad_add_fusion.place, f32[512,1024]{1,0:T(8,128)S(1)} %begin_values.1.total_ref, bf16[256,1024]{1,0:T(8,128)(2,1)S(1)} %collective-permute-done.6.fu.rest_3_, bf16[256,1024]{1,0:T(8,128)(2,1)S(1)} %collective-permute-done.7.fl.rest_4_, ...), custom_call_target="tpu_custom_call" | custom-call | flops 4255000064 | bytes 1000 | tf_op jit(solution)/shard_map/end_values/pallas_call | solution.py:274
  64.7 5.6 %weight_terms.1 = (f32[4,8,32,512]{3,2,1,0:T(8,128)}, f32[4,8,32,512]{3,2,1,0:T(8,128)}) custom-call(s32[3]{0:T(128)S(1)} %pad_add_fusion.place, f32[1024,256]{1,0:T(8,128)S(1)} %get-tuple-element.32.near_a, f32[1024,256]{1,0:T(8,128)S(1)} %get-tuple-element.34.near_b, bf16[1024,512]{1,0:T(8,128)(2,1)S(1)} %copy-done.4, ...), custom_call_target="tpu_custom_call" | custom-call | flops 5750000128 | bytes 1000 | tf_op jit(solution)/shard_map/weight_terms/pallas_call | solution.py:348
  70.6 2.1 %collective-permute-start.10 = (bf16[2,128,128]{2,1,0:T(8,128)(2,1)S(1)}, bf16[2,128,128]{2,1,0:T(8,128)(2,1)S(1)}, u32[]{:S(2)}, u32[]{:S(2)}) collective-permute-start(bf16[2,128,128]{2,1,0:T(8,128)(2,1)S(1)} %fusion.20.rest_5_), channel_id=1, source_target_pairs={{0,16},{8,24},{16,0},{24,8},{1,17},{9,25},{17,1},{25,9},{2,18},{10... | collective-permute-start | bytes 196616 | tf_op jit(solution)/shard_map/ppermute | solution.py:32
  73.6 2.4 %collective-permute-start.9 = (bf16[2,128,128]{2,1,0:T(8,128)(2,1)S(1)}, bf16[2,128,128]{2,1,0:T(8,128)(2,1)S(1)}, u32[]{:S(2)}, u32[]{:S(2)}) collective-permute-start(bf16[2,128,128]{2,1,0:T(8,128)(2,1)S(1)} %fusion.20.rest_5_), channel_id=1, source_target_pairs={{0,8},{8,16},{16,24},{24,0},{1,9},{9,17},{17,25},{25,1},{2,10},{10... | collective-permute-start | bytes 196616 | tf_op jit(solution)/shard_map/ppermute | solution.py:32
  76.5 1.8 %collective-permute-done.11 = bf16[2,128,128]{2,1,0:T(8,128)(2,1)S(1)} collective-permute-done((bf16[2,128,128]{2,1,0:T(8,128)(2,1)S(1)}, bf16[2,128,128]{2,1,0:T(8,128)(2,1)S(1)}, u32[]{:S(2)}, u32[]{:S(2)}) %collective-permute-start.11) | collective-permute-done | bytes 65568 | tf_op jit(solution)/shard_map/ppermute | solution.py:32
  78.3 3.0 %pair_sums.1 = (f32[8,32,512]{2,1,0:T(8,128)S(1)}, bf16[8,32,512]{2,1,0:T(8,128)(2,1)S(1)}, bf16[8,32,512]{2,1,0:T(8,128)(2,1)S(1)}, bf16[8,32,512]{2,1,0:T(8,128)(2,1)S(1)}) custom-call(s32[3]{0:T(128)S(1)} %pad_add_fusion.place, f32[4,8,32,512]{3,2,1,0:T(8,128)} %get-tuple-element.44.kept_u.kept_l, f32[4,8,32,512]{3,2,1,0:T(8,128)} %get-tuple-element.44.kept_u.kept_l, ...), custom_call_target="tpu_custom_call" | custom-call | flops 1264999936 | bytes 1000 | tf_op jit(solution)/shard_map/pair_sums/pallas_call | solution.py:393
  81.3 3.3 %collective-permute-start.20 = (bf16[8,32,512]{2,1,0:T(8,128)(2,1)S(1)}, bf16[8,32,512]{2,1,0:T(8,128)(2,1)S(1)}, u32[]{:S(2)}, u32[]{:S(2)}) collective-permute-start(bf16[8,32,512]{2,1,0:T(8,128)(2,1)S(1)} %get-tuple-element.48), channel_id=1, source_target_pairs={{0,8},{8,16},{16,24},{24,0},{1,9},{9,17},{17,25},{25,1},{2,10},{10... | collective-permute-start | bytes 786440 | tf_op jit(solution)/shard_map/ppermute | solution.py:32
  84.7 1.6 %collective-permute-start.24 = (bf16[8,32,512]{2,1,0:T(8,128)(2,1)S(1)}, bf16[8,32,512]{2,1,0:T(8,128)(2,1)S(1)}, u32[]{:S(2)}, u32[]{:S(2)}) collective-permute-start(bf16[8,32,512]{2,1,0:T(8,128)(2,1)S(1)} %get-tuple-element.52), channel_id=1, source_target_pairs={{0,16},{8,24},{16,0},{24,8},{1,17},{9,25},{17,1},{25,9},{2,18},{10... | collective-permute-start | bytes 786440 | tf_op jit(solution)/shard_map/ppermute | solution.py:32
  87.2 3.3 %collective-permute-done.19 = bf16[2,128,128]{2,1,0:T(8,128)(2,1)S(1)} collective-permute-done((bf16[2,128,128]{2,1,0:T(8,128)(2,1)S(1)}, bf16[2,128,128]{2,1,0:T(8,128)(2,1)S(1)}, u32[]{:S(2)}, u32[]{:S(2)}) %collective-permute-start.19) | collective-permute-done | bytes 65568 | tf_op jit(solution)/shard_map/ppermute | solution.py:36
  90.5 4.0 %collective-permute-done.20 = bf16[8,32,512]{2,1,0:T(8,128)(2,1)S(1)} collective-permute-done((bf16[8,32,512]{2,1,0:T(8,128)(2,1)S(1)}, bf16[8,32,512]{2,1,0:T(8,128)(2,1)S(1)}, u32[]{:S(2)}, u32[]{:S(2)}) %collective-permute-start.20) | collective-permute-done | bytes 262176 | tf_op jit(solution)/shard_map/ppermute | solution.py:32
  94.5 3.4 %collective-permute-done.23 = bf16[8,32,512]{2,1,0:T(8,128)(2,1)S(1)} collective-permute-done((bf16[8,32,512]{2,1,0:T(8,128)(2,1)S(1)}, bf16[8,32,512]{2,1,0:T(8,128)(2,1)S(1)}, u32[]{:S(2)}, u32[]{:S(2)}) %collective-permute-start.23) | collective-permute-done | bytes 262176 | tf_op jit(solution)/shard_map/ppermute | solution.py:32
  98.8 7.6 %all-to-all-start = ((bf16[8,32,512]{2,1,0:T(8,128)(2,1)}), bf16[8,32,512]{2,1,0:T(8,128)(2,1)S(1)}, u32[]{:S(2)}, u32[]{:S(2)}) async-start(bf16[8,32,512]{2,1,0:T(8,128)(2,1)} %add_convert_fusion), calls=%async_computation | async-start | bytes 524288 | tf_op jit(solution)/shard_map/all_to_all | solution.py:603
  106.3 2.9 %collective-permute-start.21 = (bf16[2,128,128]{2,1,0:T(8,128)(2,1)S(1)}, bf16[2,128,128]{2,1,0:T(8,128)(2,1)S(1)}, u32[]{:S(2)}, u32[]{:S(2)}) collective-permute-start(bf16[2,128,128]{2,1,0:T(8,128)(2,1)S(1)} %fusion.13.rest_6_), channel_id=1, source_target_pairs={{0,64},{32,96},{64,0},{96,32},{128,192},{160,224},{192,128},{224,1... | collective-permute-start | bytes 196616 | tf_op jit(solution)/shard_map/ppermute | solution.py:36
  109.3 7.2 %begin_attended.1.total_u.total_l = f32[4,128,1024]{2,1,0:T(8,128)} custom-call(s32[3]{0:T(128)S(1)} %pad_add_fusion.place, bf16[4,128,1024]{2,1,0:T(8,128)(2,1)} %get-tuple-element.28.turned_ref, bf16[17,4,1024]{2,1,0:T(4,128)(2,1)S(1)} %copy-done, bf16[512,1024]{1,0:T(8,128)(2,1)} %get-tuple-element.36.v_ref, ...), custom_call_target="tpu_custom_call" | custom-call | flops 345000000 | bytes 1000 | tf_op jit(solution)/shard_map/begin_attended/pallas_call | solution.py:463
  116.6 5.5 %collective-permute-start.22 = (bf16[2,128,128]{2,1,0:T(8,128)(2,1)S(1)}, bf16[2,128,128]{2,1,0:T(8,128)(2,1)S(1)}, u32[]{:S(2)}, u32[]{:S(2)}) collective-permute-start(bf16[2,128,128]{2,1,0:T(8,128)(2,1)S(1)} %get-tuple-element.50), channel_id=1, source_target_pairs={{0,128},{32,160},{64,192},{96,224},{1,129},{33,161},{65,193},{97,2... | collective-permute-start | bytes 196616 | tf_op jit(solution)/shard_map/ppermute | solution.py:602
  122.1 1.9 %collective-permute-done.22 = bf16[2,128,128]{2,1,0:T(8,128)(2,1)S(1)} collective-permute-done((bf16[2,128,128]{2,1,0:T(8,128)(2,1)S(1)}, bf16[2,128,128]{2,1,0:T(8,128)(2,1)S(1)}, u32[]{:S(2)}, u32[]{:S(2)}) %collective-permute-start.22) | collective-permute-done | bytes 65568 | tf_op jit(solution)/shard_map/ppermute | solution.py:602
  125.5 5.1 %end_attended.1 = bf16[1024,512]{1,0:T(8,128)(2,1)} custom-call(s32[3]{0:T(128)S(1)} %pad_add_fusion.place, bf16[4,128,1024]{2,1,0:T(8,128)(2,1)} %get-tuple-element.28.turned_ref, bf16[17,4,1024]{2,1,0:T(4,128)(2,1)S(1)} %copy-done, f32[4,128,1024]{2,1,0:T(8,128)} %begin_attended.1.total_u.total_l, f32[4,128,1024]{2,1,0:T(8,128)} %begin_attended.1.total_u.total_l, ...), custom_call_target="tpu_custom_call" | custom-call | flops 345000000 | bytes 1000 | tf_op jit(solution)/shard_map/end_attended/pallas_call | solution.py:502
  (66 shorter events, 15.5 us)
Async XLA Ops:
  6.6 5.6 %copy-start.2 = (bf16[1024,512]{1,0:T(8,128)(2,1)S(1)}, bf16[1024,512]{1,0:T(8,128)(2,1)}, u32[]{:S(2)}) copy-start(bf16[1024,512]{1,0:T(8,128)(2,1)} %in_ref.2) | copy-start | bytes 3145732
  6.6 2.1 %collective-permute-start = (f32[5,2,128,128]{3,2,1,0:T(8,128)S(1)}, f32[5,2,128,128]{3,2,1,0:T(8,128)S(1)}, u32[]{:S(2)}, u32[]{:S(2)}) collective-permute-start(f32[5,2,128,128]{3,2,1,0:T(8,128)S(1)} %get-tuple-element.30), channel_id=1, source_target_pairs={{0,4},{4,0},{1,5},{5,1},{2,6},{6,2},{3,7},{7,3},{8,12},{12,8},{9,1... | collective-permute-start | bytes 1966088 | tf_op jit(solution)/shard_map/ppermute | solution.py:36
  8.8 7.2 %collective-permute-start.3 = (bf16[3,2,128,128]{3,2,1,0:T(8,128)(2,1)S(1)}, bf16[3,2,128,128]{3,2,1,0:T(8,128)(2,1)S(1)}, u32[]{:S(2)}, u32[]{:S(2)}) collective-permute-start(bf16[3,2,128,128]{3,2,1,0:T(8,128)(2,1)S(1)} %slice.139.rest_0_), channel_id=1, source_target_pairs={{0,32},{32,0},{64,96},{96,64},{128,160},{160,128},{192,224},{224,1... | collective-permute-start | bytes 589832 | tf_op jit(solution)/shard_map/ppermute | solution.py:36
  10.8 33.7 %collective-permute-start.16 = (f32[4,128,128]{2,1,0:T(8,128)S(1)}, f32[4,128,128]{2,1,0:T(8,128)S(1)}, u32[]{:S(2)}, u32[]{:S(2)}) collective-permute-start(f32[4,128,128]{2,1,0:T(8,128)S(1)} %get-tuple-element.42), channel_id=1, source_target_pairs={{4,0},{5,1},{6,2},{7,3},{12,8},{13,9},{14,10},{15,11},{20,16},{21,... | collective-permute-start | bytes 786440 | tf_op jit(solution)/shard_map/ppermute | solution.py:553
  12.2 7.3 %copy-start = (bf16[17,4,1024]{2,1,0:T(4,128)(2,1)S(1)}, bf16[17,4,1024]{2,1,0:T(4,128)(2,1)}, u32[]{:S(2)}) copy-start(bf16[17,4,1024]{2,1,0:T(4,128)(2,1)} %lw_ref.9) | copy-start | bytes 417796
  12.2 7.3 %copy-start.3 = (bf16[1024,512]{1,0:T(8,128)(2,1)S(1)}, bf16[1024,512]{1,0:T(8,128)(2,1)}, u32[]{:S(2)}) copy-start(bf16[1024,512]{1,0:T(8,128)(2,1)} %g_ref.3) | copy-start | bytes 3145732
  12.2 7.3 %copy-start.4 = (bf16[1024,512]{1,0:T(8,128)(2,1)S(1)}, bf16[1024,512]{1,0:T(8,128)(2,1)}, u32[]{:S(2)}) copy-start(bf16[1024,512]{1,0:T(8,128)(2,1)} %k_ref.7) | copy-start | bytes 3145732
  12.8 25.9 %collective-permute-start.1 = (bf16[512,1024]{1,0:T(8,128)(2,1)S(1)}, bf16[512,1024]{1,0:T(8,128)(2,1)S(1)}, u32[]{:S(2)}, u32[]{:S(2)}) collective-permute-start(bf16[512,1024]{1,0:T(8,128)(2,1)S(1)} %turn_features.1.own.rest_0_), channel_id=1, source_target_pairs={{0,1},{1,2},{2,3},{3,0},{4,5},{5,6},{6,7},{7,4},{8,9},{9,10},{10,1... | collective-permute-start | bytes 3145736 | tf_op jit(solution)/shard_map/ppermute | solution.py:32
  13.1 27.2 %collective-permute-start.2 = (bf16[512,1024]{1,0:T(8,128)(2,1)S(1)}, bf16[512,1024]{1,0:T(8,128)(2,1)S(1)}, u32[]{:S(2)}, u32[]{:S(2)}) collective-permute-start(bf16[512,1024]{1,0:T(8,128)(2,1)S(1)} %turn_features.1.own.rest_0_), channel_id=1, source_target_pairs={{0,3},{1,0},{2,1},{3,2},{4,7},{5,4},{6,5},{7,6},{8,11},{9,8},{10,9... | collective-permute-start | bytes 3145736 | tf_op jit(solution)/shard_map/ppermute | solution.py:32
  16.1 9.5 %collective-permute-start.4 = (bf16[2,2,128,128]{3,2,1,0:T(8,128)(2,1)S(1)}, bf16[2,2,128,128]{3,2,1,0:T(8,128)(2,1)S(1)}, u32[]{:S(2)}, u32[]{:S(2)}) collective-permute-start(bf16[2,2,128,128]{3,2,1,0:T(8,128)(2,1)S(1)} %pad_maximum_fusion.3.rest_0_), channel_id=1, source_target_pairs={{0,64},{32,96},{64,0},{96,32},{128,192},{160,224},{192,128},{224,1... | collective-permute-start | bytes 393224 | tf_op jit(solution)/shard_map/ppermute | solution.py:36
  19.4 5.2 %copy-start.1 = (bf16[2048,512]{1,0:T(8,128)(2,1)S(1)}, bf16[2048,512]{1,0:T(8,128)(2,1)}, u32[]{:S(2)}) copy-start(bf16[2048,512]{1,0:T(8,128)(2,1)} %in_ref.3) | copy-start | bytes 6291460
  25.6 10.1 %collective-permute-start.5 = (bf16[2,128,128]{2,1,0:T(8,128)(2,1)S(1)}, bf16[2,128,128]{2,1,0:T(8,128)(2,1)S(1)}, u32[]{:S(2)}, u32[]{:S(2)}) collective-permute-start(bf16[2,128,128]{2,1,0:T(8,128)(2,1)S(1)} %fusion.15.rest_0_), channel_id=1, source_target_pairs={{128,0},{160,32},{192,64},{224,96},{129,1},{161,33},{193,65},{225,... | collective-permute-start | bytes 196616 | tf_op jit(solution)/shard_map/ppermute | solution.py:558
  40.4 9.5 %collective-permute-start.13 = (bf16[2,128,128]{2,1,0:T(8,128)(2,1)S(1)}, bf16[2,128,128]{2,1,0:T(8,128)(2,1)S(1)}, u32[]{:S(2)}, u32[]{:S(2)}) collective-permute-start(bf16[2,128,128]{2,1,0:T(8,128)(2,1)S(1)} %get-tuple-element.58), channel_id=1, source_target_pairs={{0,8},{8,16},{16,24},{24,0},{1,9},{9,17},{17,25},{25,1},{2,10},{10... | collective-permute-start | bytes 196616 | tf_op jit(solution)/shard_map/ppermute | solution.py:32
  41.0 9.0 %collective-permute-start.14 = (bf16[2,128,128]{2,1,0:T(8,128)(2,1)S(1)}, bf16[2,128,128]{2,1,0:T(8,128)(2,1)S(1)}, u32[]{:S(2)}, u32[]{:S(2)}) collective-permute-start(bf16[2,128,128]{2,1,0:T(8,128)(2,1)S(1)} %get-tuple-element.59), channel_id=1, source_target_pairs={{0,24},{8,0},{16,8},{24,16},{1,25},{9,1},{17,9},{25,17},{2,26},{10... | collective-permute-start | bytes 196616 | tf_op jit(solution)/shard_map/ppermute | solution.py:32
  42.6 7.4 %collective-permute-start.15 = (bf16[2,128,128]{2,1,0:T(8,128)(2,1)S(1)}, bf16[2,128,128]{2,1,0:T(8,128)(2,1)S(1)}, u32[]{:S(2)}, u32[]{:S(2)}) collective-permute-start(bf16[2,128,128]{2,1,0:T(8,128)(2,1)S(1)} %fusion.12.rest_0_), channel_id=1, source_target_pairs={{0,16},{8,24},{16,0},{24,8},{1,17},{9,25},{17,1},{25,9},{2,18},{10... | collective-permute-start | bytes 196616 | tf_op jit(solution)/shard_map/ppermute | solution.py:32
  44.1 13.2 %collective-permute-start.6 = (bf16[256,1024]{1,0:T(8,128)(2,1)S(1)}, bf16[256,1024]{1,0:T(8,128)(2,1)S(1)}, u32[]{:S(2)}, u32[]{:S(2)}) collective-permute-start(bf16[256,1024]{1,0:T(8,128)(2,1)S(1)} %slice.79), channel_id=1, source_target_pairs={{0,1},{1,2},{2,3},{3,0},{4,5},{5,6},{6,7},{7,4},{8,9},{9,10},{10,1... | collective-permute-start | bytes 1572872 | tf_op jit(solution)/shard_map/ppermute | solution.py:32
  44.5 14.3 %collective-permute-start.7 = (bf16[256,1024]{1,0:T(8,128)(2,1)S(1)}, bf16[256,1024]{1,0:T(8,128)(2,1)S(1)}, u32[]{:S(2)}, u32[]{:S(2)}) collective-permute-start(bf16[256,1024]{1,0:T(8,128)(2,1)S(1)} %slice.80), channel_id=1, source_target_pairs={{0,3},{1,0},{2,1},{3,2},{4,7},{5,4},{6,5},{7,6},{8,11},{9,8},{10,9... | collective-permute-start | bytes 1572872 | tf_op jit(solution)/shard_map/ppermute | solution.py:32
  62.9 1.3 %collective-permute-start.17 = (f32[2,128,128]{2,1,0:T(8,128)S(1)}, f32[2,128,128]{2,1,0:T(8,128)S(1)}, u32[]{:S(2)}, u32[]{:S(2)}) collective-permute-start(f32[2,128,128]{2,1,0:T(8,128)S(1)} %get-tuple-element.43), channel_id=1, source_target_pairs={{0,4},{4,0},{1,5},{5,1},{2,6},{6,2},{3,7},{7,3},{8,12},{12,8},{9,1... | collective-permute-start | bytes 393224 | tf_op jit(solution)/shard_map/ppermute | solution.py:36
  62.9 1.7 %collective-permute-start.8 = (f32[4,128,128]{2,1,0:T(8,128)S(1)}, f32[4,128,128]{2,1,0:T(8,128)S(1)}, u32[]{:S(2)}, u32[]{:S(2)}) collective-permute-start(f32[4,128,128]{2,1,0:T(8,128)S(1)} %get-tuple-element.41), channel_id=1, source_target_pairs={{0,4},{4,0},{1,5},{5,1},{2,6},{6,2},{3,7},{7,3},{8,12},{12,8},{9,1... | collective-permute-start | bytes 786440 | tf_op jit(solution)/shard_map/ppermute | solution.py:36
  70.3 8.0 %collective-permute-start.18 = (f32[4,8,32,512]{3,2,1,0:T(8,128)}, f32[4,8,32,512]{3,2,1,0:T(8,128)S(1)}, u32[]{:S(2)}, u32[]{:S(2)}) collective-permute-start(f32[4,8,32,512]{3,2,1,0:T(8,128)} %get-tuple-element.45), channel_id=1, source_target_pairs={{0,4},{4,0},{1,5},{5,1},{2,6},{6,2},{3,7},{7,3},{8,12},{12,8},{9,1... | collective-permute-start | bytes 6291464 | tf_op jit(solution)/shard_map/ppermute | solution.py:36
  70.6 5.8 %collective-permute-start.10 = (bf16[2,128,128]{2,1,0:T(8,128)(2,1)S(1)}, bf16[2,128,128]{2,1,0:T(8,128)(2,1)S(1)}, u32[]{:S(2)}, u32[]{:S(2)}) collective-permute-start(bf16[2,128,128]{2,1,0:T(8,128)(2,1)S(1)} %fusion.20.rest_5_), channel_id=1, source_target_pairs={{0,16},{8,24},{16,0},{24,8},{1,17},{9,25},{17,1},{25,9},{2,18},{10... | collective-permute-start | bytes 196616 | tf_op jit(solution)/shard_map/ppermute | solution.py:32
  72.7 5.5 %collective-permute-start.11 = (bf16[2,128,128]{2,1,0:T(8,128)(2,1)S(1)}, bf16[2,128,128]{2,1,0:T(8,128)(2,1)S(1)}, u32[]{:S(2)}, u32[]{:S(2)}) collective-permute-start(bf16[2,128,128]{2,1,0:T(8,128)(2,1)S(1)} %fusion.20.rest_5_), channel_id=1, source_target_pairs={{0,24},{8,0},{16,8},{24,16},{1,25},{9,1},{17,9},{25,17},{2,26},{10... | collective-permute-start | bytes 196616 | tf_op jit(solution)/shard_map/ppermute | solution.py:32
  73.6 4.6 %collective-permute-start.9 = (bf16[2,128,128]{2,1,0:T(8,128)(2,1)S(1)}, bf16[2,128,128]{2,1,0:T(8,128)(2,1)S(1)}, u32[]{:S(2)}, u32[]{:S(2)}) collective-permute-start(bf16[2,128,128]{2,1,0:T(8,128)(2,1)S(1)} %fusion.20.rest_5_), channel_id=1, source_target_pairs={{0,8},{8,16},{16,24},{24,0},{1,9},{9,17},{17,25},{25,1},{2,10},{10... | collective-permute-start | bytes 196616 | tf_op jit(solution)/shard_map/ppermute | solution.py:32
  81.3 13.1 %collective-permute-start.20 = (bf16[8,32,512]{2,1,0:T(8,128)(2,1)S(1)}, bf16[8,32,512]{2,1,0:T(8,128)(2,1)S(1)}, u32[]{:S(2)}, u32[]{:S(2)}) collective-permute-start(bf16[8,32,512]{2,1,0:T(8,128)(2,1)S(1)} %get-tuple-element.48), channel_id=1, source_target_pairs={{0,8},{8,16},{16,24},{24,0},{1,9},{9,17},{17,25},{25,1},{2,10},{10... | collective-permute-start | bytes 786440 | tf_op jit(solution)/shard_map/ppermute | solution.py:32
  84.7 13.2 %collective-permute-start.23 = (bf16[8,32,512]{2,1,0:T(8,128)(2,1)S(1)}, bf16[8,32,512]{2,1,0:T(8,128)(2,1)S(1)}, u32[]{:S(2)}, u32[]{:S(2)}) collective-permute-start(bf16[8,32,512]{2,1,0:T(8,128)(2,1)S(1)} %get-tuple-element.51), channel_id=1, source_target_pairs={{0,24},{8,0},{16,8},{24,16},{1,25},{9,1},{17,9},{25,17},{2,26},{10... | collective-permute-start | bytes 786440 | tf_op jit(solution)/shard_map/ppermute | solution.py:32
  84.7 13.2 %collective-permute-start.24 = (bf16[8,32,512]{2,1,0:T(8,128)(2,1)S(1)}, bf16[8,32,512]{2,1,0:T(8,128)(2,1)S(1)}, u32[]{:S(2)}, u32[]{:S(2)}) collective-permute-start(bf16[8,32,512]{2,1,0:T(8,128)(2,1)S(1)} %get-tuple-element.52), channel_id=1, source_target_pairs={{0,16},{8,24},{16,0},{24,8},{1,17},{9,25},{17,1},{25,9},{2,18},{10... | collective-permute-start | bytes 786440 | tf_op jit(solution)/shard_map/ppermute | solution.py:32
  86.2 4.3 %collective-permute-start.19 = (bf16[2,128,128]{2,1,0:T(8,128)(2,1)S(1)}, bf16[2,128,128]{2,1,0:T(8,128)(2,1)S(1)}, u32[]{:S(2)}, u32[]{:S(2)}) collective-permute-start(bf16[2,128,128]{2,1,0:T(8,128)(2,1)S(1)} %get-tuple-element.47), channel_id=1, source_target_pairs={{0,32},{32,0},{64,96},{96,64},{128,160},{160,128},{192,224},{224,1... | collective-permute-start | bytes 196616 | tf_op jit(solution)/shard_map/ppermute | solution.py:36
  87.1 22.2 %collective-permute-start.12 = (bf16[2,2,128,128]{3,2,1,0:T(8,128)(2,1)S(1)}, bf16[2,2,128,128]{3,2,1,0:T(8,128)(2,1)S(1)}, u32[]{:S(2)}, u32[]{:S(2)}) collective-permute-start(bf16[2,2,128,128]{3,2,1,0:T(8,128)(2,1)S(1)} %pad_maximum_fusion.4), channel_id=1, source_target_pairs={{0,4},{4,0},{1,5},{5,1},{2,6},{6,2},{3,7},{7,3},{8,12},{12,8},{9,1... | collective-permute-start | bytes 393224 | tf_op jit(solution)/shard_map/ppermute | solution.py:36
  98.8 25.2 %all-to-all-start = ((bf16[8,32,512]{2,1,0:T(8,128)(2,1)}), bf16[8,32,512]{2,1,0:T(8,128)(2,1)S(1)}, u32[]{:S(2)}, u32[]{:S(2)}) async-start(bf16[8,32,512]{2,1,0:T(8,128)(2,1)} %add_convert_fusion), calls=%async_computation | async-start | bytes 524288 | tf_op jit(solution)/shard_map/all_to_all | solution.py:603
  106.3 10.2 %collective-permute-start.21 = (bf16[2,128,128]{2,1,0:T(8,128)(2,1)S(1)}, bf16[2,128,128]{2,1,0:T(8,128)(2,1)S(1)}, u32[]{:S(2)}, u32[]{:S(2)}) collective-permute-start(bf16[2,128,128]{2,1,0:T(8,128)(2,1)S(1)} %fusion.13.rest_6_), channel_id=1, source_target_pairs={{0,64},{32,96},{64,0},{96,32},{128,192},{160,224},{192,128},{224,1... | collective-permute-start | bytes 196616 | tf_op jit(solution)/shard_map/ppermute | solution.py:36
  116.6 7.4 %collective-permute-start.22 = (bf16[2,128,128]{2,1,0:T(8,128)(2,1)S(1)}, bf16[2,128,128]{2,1,0:T(8,128)(2,1)S(1)}, u32[]{:S(2)}, u32[]{:S(2)}) collective-permute-start(bf16[2,128,128]{2,1,0:T(8,128)(2,1)S(1)} %get-tuple-element.50), channel_id=1, source_target_pairs={{0,128},{32,160},{64,192},{96,224},{1,129},{33,161},{65,193},{97,2... | collective-permute-start | bytes 196616 | tf_op jit(solution)/shard_map/ppermute | solution.py:602
  124.0 1.5 %collective-permute-start.25 = (bf16[3,2,128,128]{3,2,1,0:T(8,128)(2,1)S(1)}, bf16[3,2,128,128]{3,2,1,0:T(8,128)(2,1)S(1)}, u32[]{:S(2)}, u32[]{:S(2)}) collective-permute-start(bf16[3,2,128,128]{3,2,1,0:T(8,128)(2,1)S(1)} %pad_maximum_fusion.2), channel_id=1, source_target_pairs={{0,4},{4,0},{1,5},{5,1},{2,6},{6,2},{3,7},{7,3},{8,12},{12,8},{9,1... | collective-permute-start | bytes 589832 | tf_op jit(solution)/shard_map/ppermute | solution.py:36

commit v3 on v2

--- a/solution.py
+++ b/solution.py
@@ -586,23 +586,23 @@
     message = behind(running.astype(BF), rows)
     first, second, third = (shift(messages[d - 1], "x", d, NX) for d in (1, 3, 2))
     rows = rows + first.astype(F32) + second.astype(F32) + third.astype(F32)
+    lower_levels = both(jnp.stack([level_1, level_2]).astype(BF))
+    begun = begin_attended(
+        place, turned_queries, level_weights, values, (*near_a, *near_b), zero, lower_levels, message
+    )
     got = swap(message, "z", 1, NZ).astype(F32)
     level_3 = jnp.where(z & 1 == 1, got, 0.0)
     running = running + got
-    lower_levels = both(jnp.stack([level_1, level_2]).astype(BF))
-    message = behind(running.astype(BF), first)
+    rows = rows.astype(BF)
+    message = behind(running.astype(BF), begun, rows)
     got = swap(message, "z", 2, NZ).astype(F32)
-    begun = begin_attended(
-        place, turned_queries, level_weights, values, (*near_a, *near_b), zero, lower_levels, message
-    )
     level_4 = jnp.where(z & 2 == 2, got, 0.0)
     running = running + got
-    rows = rows.astype(BF)
-    message = behind(running.astype(BF), begun)
+    message = running.astype(BF)
     level_5 = lax.ppermute(message, "z", [(i, i + 4) for i in range(4)])
     rows = lax.all_to_all(rows, "z", 0, 0, tiled=True)
     weight_grad = rows.astype(F32).sum(axis=0)
-    upper_levels = behind(jnp.stack([level_3.astype(BF), level_4.astype(BF), level_5]), rows)
+    upper_levels = jnp.stack([level_3.astype(BF), level_4.astype(BF), level_5])
     attended = end_attended(place, turned_queries, level_weights, begun, both(upper_levels))
     return attended, weight_grad
 

time: 132 us -> 131 us (level)
    all_to_all x1, starting transfers between devices: 7.58 us -> 3.42 us  [local(): rows = lax.all_to_all(rows, 'z', 0, 0, tiled=True)]
    all_to_all x1, waiting for transfers between devices: 0.01 us -> 3.67 us  [local(): rows = lax.all_to_all(rows, 'z', 0, 0, tiled=True)]
    ppermute x1, starting transfers between devices: 5.48 us -> 9.02 us  [local(): level_5 = lax.ppermute(message, 'z', [(i, i + 4) for i in range(4)])]
    ppermute x1, waiting for transfers between devices: 1.88 us -> 0.01 us  [local(): level_5 = lax.ppermute(message, 'z', [(i, i + 4) for i in range(4)])]
    ppermute x13, waiting for transfers between devices: 23 us -> 21.4 us  [shift(): lax.ppermute(value, axis, [(i, (i + distance) % size) for i in range(size)])]
  transfers between devices with their start and end apart: 27 -> 27, of which waited for: 16 -> 16; matrix products, arithmetic and copies ran while one was open for 2% -> 0% of each run, Pallas kernels for 17% -> 24%
where the time goes in v3:
time: 131 us; the launch traced here: 130 us
  Pallas kernels  46.2 us (35%)
  starting transfers between devices  43.8 us (33%)
  waiting for transfers between devices  37 us (28%)
  other arithmetic  2.27 us (2%)
    ppermute x13, waiting for transfers between devices, shift(): lax.ppermute(value, axis, [(i, (i + distance) % size) for i in range(size)])  21.4 us
    ppermute x13, starting transfers between devices, shift(): lax.ppermute(value, axis, [(i, (i + distance) % size) for i in range(size)])  18.7 us
    pallas_call x2, Pallas kernels, near(): pl.pallas_call(functools.partial(near_kernel, base), grid=(2,), in_specs=...  10.3 us
    ppermute x10, starting transfers between devices, swap(): return lax.ppermute(value, axis, [(i, i ^ distance) for i in range(size)])  10.1 us
    ppermute x1, starting transfers between devices, local(): level_5 = lax.ppermute(message, 'z', [(i, i + 4) for i in range(4)])  9.02 us
    ppermute x10, waiting for transfers between devices, swap(): return lax.ppermute(value, axis, [(i, i ^ distance) for i in range(size)])  8.26 us
    pallas_call x1, Pallas kernels, begin_attended(): pl.pallas_call(begin_attended_kernel, grid_spec=pltpu.PrefetchScalarGridS...  7.21 us
    pallas_call x1, Pallas kernels, query_states(): pl.pallas_call(query_state_kernel, grid_spec=pltpu.PrefetchScalarGridSpec...  5.85 us
  transfers between devices with their start and end apart: 27, of which 16 were waited for; matrix products, arithmetic and copies ran while one was open for 0% of the time, Pallas kernels for 24%

profile of v3, /device:TPU:30, one launch (start us, length us, event | category | flops | bytes accessed | tf_op | source)
XLA Modules:
  0.0 130.4 jit_solution(3024474681905621626)
XLA Ops:
  0.7 5.9 %query_states.1 = (f32[4,128,128]{2,1,0:T(8,128)S(1)}, f32[5,2,128,128]{3,2,1,0:T(8,128)S(1)}, f32[5,2,128,128]{3,2,1,0:T(8,128)S(1)}, bf16[4,128,1024]{2,1,0:T(8,128)(2,1)}) custom-call(s32[3]{0:T(128)S(1)} %pad_add_fusion.place, bf16[1024,512]{1,0:T(8,128)(2,1)} %q_l.1, bf16[1024,512]{1,0:T(8,128)(2,1)} %q_l.1, bf16[1024,512]{1,0:T(8,128)(2,1)} %g_ref.3, ...), custom_call_target="tpu_custom_call" | custom-call | flops 4600000000 | bytes 1000 | tf_op jit(solution)/shard_map/query_states/pallas_call | solution.py:122
  6.6 2.1 %collective-permute-done = f32[5,2,128,128]{3,2,1,0:T(8,128)S(1)} collective-permute-done((f32[5,2,128,128]{3,2,1,0:T(8,128)S(1)}, f32[5,2,128,128]{3,2,1,0:T(8,128)S(1)}, u32[]{:S(2)}, u32[]{:S(2)}) %collective-permute-start) | collective-permute-done | bytes 655392 | tf_op jit(solution)/shard_map/ppermute | solution.py:36
  8.8 2.0 %collective-permute-start.3 = (bf16[3,2,128,128]{3,2,1,0:T(8,128)(2,1)S(1)}, bf16[3,2,128,128]{3,2,1,0:T(8,128)(2,1)S(1)}, u32[]{:S(2)}, u32[]{:S(2)}) collective-permute-start(bf16[3,2,128,128]{3,2,1,0:T(8,128)(2,1)S(1)} %slice.139.rest_0_), channel_id=1, source_target_pairs={{0,32},{32,0},{64,96},{96,64},{128,160},{160,128},{192,224},{224,1... | collective-permute-start | bytes 589832 | tf_op jit(solution)/shard_map/ppermute | solution.py:36
  13.1 1.8 %collective-permute-start.2 = (bf16[512,1024]{1,0:T(8,128)(2,1)S(1)}, bf16[512,1024]{1,0:T(8,128)(2,1)S(1)}, u32[]{:S(2)}, u32[]{:S(2)}) collective-permute-start(bf16[512,1024]{1,0:T(8,128)(2,1)S(1)} %turn_features.1.own.rest_0_), channel_id=1, source_target_pairs={{0,3},{1,0},{2,1},{3,2},{4,7},{5,4},{6,5},{7,6},{8,11},{9,8},{10,9... | collective-permute-start | bytes 3145736 | tf_op jit(solution)/shard_map/ppermute | solution.py:32
  16.1 3.4 %collective-permute-start.4 = (bf16[2,2,128,128]{3,2,1,0:T(8,128)(2,1)S(1)}, bf16[2,2,128,128]{3,2,1,0:T(8,128)(2,1)S(1)}, u32[]{:S(2)}, u32[]{:S(2)}) collective-permute-start(bf16[2,2,128,128]{3,2,1,0:T(8,128)(2,1)S(1)} %pad_maximum_fusion.3.rest_0_), channel_id=1, source_target_pairs={{0,64},{32,96},{64,0},{96,32},{128,192},{160,224},{192,128},{224,1... | collective-permute-start | bytes 393224 | tf_op jit(solution)/shard_map/ppermute | solution.py:36
  19.4 5.2 %near.2 = (f32[1024,256]{1,0:T(8,128)S(1)}, bf16[2,5,256,256]{3,2,1,0:T(8,128)(2,1)}, bf16[2,5,256,256]{3,2,1,0:T(8,128)(2,1)}) custom-call(bf16[1024,512]{1,0:T(8,128)(2,1)S(1)} %copy-done.4, bf16[4,128,1024]{2,1,0:T(8,128)(2,1)} %get-tuple-element.26.turned_ref, bf16[1024,512]{1,0:T(8,128)(2,1)S(1)} %copy-done.3, bf16[17,4,1024]{2,1,0:T(4,128)(2,1)S(1)} %copy-done, ...), custom_call_target="tpu_custom_call" | custom-call | flops 3680000000 | bytes 1000 | tf_op jit(solution)/shard_map/near/pallas_call | solution.py:200
  26.9 5.1 %near.3 = (f32[1024,256]{1,0:T(8,128)S(1)}, bf16[2,5,256,256]{3,2,1,0:T(8,128)(2,1)}, bf16[2,5,256,256]{3,2,1,0:T(8,128)(2,1)}) custom-call(bf16[1024,512]{1,0:T(8,128)(2,1)S(1)} %copy-done.4, bf16[4,128,1024]{2,1,0:T(8,128)(2,1)} %get-tuple-element.26.turned_ref, bf16[1024,512]{1,0:T(8,128)(2,1)S(1)} %copy-done.3, bf16[17,4,1024]{2,1,0:T(4,128)(2,1)S(1)} %copy-done, ...), custom_call_target="tpu_custom_call" | custom-call | flops 3680000000 | bytes 1000 | tf_op jit(solution)/shard_map/near/pallas_call | solution.py:200
  32.1 3.6 %collective-permute-done.5 = bf16[2,128,128]{2,1,0:T(8,128)(2,1)S(1)} collective-permute-done((bf16[2,128,128]{2,1,0:T(8,128)(2,1)S(1)}, bf16[2,128,128]{2,1,0:T(8,128)(2,1)S(1)}, u32[]{:S(2)}, u32[]{:S(2)}) %collective-permute-start.5) | collective-permute-done | bytes 65568 | tf_op jit(solution)/shard_map/ppermute | solution.py:558
  35.7 3.1 %collective-permute-done.1.left.rest_1_ = bf16[512,1024]{1,0:T(8,128)(2,1)S(1)} collective-permute-done((bf16[512,1024]{1,0:T(8,128)(2,1)S(1)}, bf16[512,1024]{1,0:T(8,128)(2,1)S(1)}, u32[]{:S(2)}, u32[]{:S(2)}) %collective-permute-start.1) | collective-permute-done | bytes 1048608 | tf_op jit(solution)/shard_map/ppermute | solution.py:32
  38.8 1.6 %collective-permute-done.2.right.rest_2_ = bf16[512,1024]{1,0:T(8,128)(2,1)S(1)} collective-permute-done((bf16[512,1024]{1,0:T(8,128)(2,1)S(1)}, bf16[512,1024]{1,0:T(8,128)(2,1)S(1)}, u32[]{:S(2)}, u32[]{:S(2)}) %collective-permute-start.2) | collective-permute-done | bytes 1048608 | tf_op jit(solution)/shard_map/ppermute | solution.py:32
  41.0 1.5 %collective-permute-start.14 = (bf16[2,128,128]{2,1,0:T(8,128)(2,1)S(1)}, bf16[2,128,128]{2,1,0:T(8,128)(2,1)S(1)}, u32[]{:S(2)}, u32[]{:S(2)}) collective-permute-start(bf16[2,128,128]{2,1,0:T(8,128)(2,1)S(1)} %get-tuple-element.55), channel_id=1, source_target_pairs={{0,24},{8,0},{16,8},{24,16},{1,25},{9,1},{17,9},{25,17},{2,26},{10... | collective-permute-start | bytes 196616 | tf_op jit(solution)/shard_map/ppermute | solution.py:32
  44.5 2.0 %collective-permute-start.7 = (bf16[256,1024]{1,0:T(8,128)(2,1)S(1)}, bf16[256,1024]{1,0:T(8,128)(2,1)S(1)}, u32[]{:S(2)}, u32[]{:S(2)}) collective-permute-start(bf16[256,1024]{1,0:T(8,128)(2,1)S(1)} %slice.80), channel_id=1, source_target_pairs={{0,3},{1,0},{2,1},{3,2},{4,7},{5,4},{6,5},{7,6},{8,11},{9,8},{10,9... | collective-permute-start | bytes 1572872 | tf_op jit(solution)/shard_map/ppermute | solution.py:32
  46.5 3.4 %begin_values.1.total_ref = f32[512,1024]{1,0:T(8,128)S(1)} custom-call(s32[3]{0:T(128)S(1)} %pad_add_fusion.place, bf16[512,1024]{1,0:T(8,128)(2,1)S(1)} %turn_features.1.own.rest_0_, bf16[512,1024]{1,0:T(8,128)(2,1)S(1)} %collective-permute-done.1.left.rest_1_, bf16[512,1024]{1,0:T(8,128)(2,1)S(1)} %collective-permute-done.2.right.rest_2_, ...), custom_call_target="tpu_custom_call" | custom-call | flops 4024999936 | bytes 1000 | tf_op jit(solution)/shard_map/begin_values/pallas_call | solution.py:252
  50.0 7.2 %collective-permute-done.6.fu.rest_3_ = bf16[256,1024]{1,0:T(8,128)(2,1)S(1)} collective-permute-done((bf16[256,1024]{1,0:T(8,128)(2,1)S(1)}, bf16[256,1024]{1,0:T(8,128)(2,1)S(1)}, u32[]{:S(2)}, u32[]{:S(2)}) %collective-permute-start.6) | collective-permute-done | bytes 524320 | tf_op jit(solution)/shard_map/ppermute | solution.py:32
  57.3 1.5 %collective-permute-done.7.fl.rest_4_ = bf16[256,1024]{1,0:T(8,128)(2,1)S(1)} collective-permute-done((bf16[256,1024]{1,0:T(8,128)(2,1)S(1)}, bf16[256,1024]{1,0:T(8,128)(2,1)S(1)}, u32[]{:S(2)}, u32[]{:S(2)}) %collective-permute-start.7) | collective-permute-done | bytes 524320 | tf_op jit(solution)/shard_map/ppermute | solution.py:32
  58.8 4.1 %end_values.1 = (bf16[512,1024]{1,0:T(8,128)(2,1)}, f32[4,128,128]{2,1,0:T(8,128)S(1)}) custom-call(s32[3]{0:T(128)S(1)} %pad_add_fusion.place, f32[512,1024]{1,0:T(8,128)S(1)} %begin_values.1.total_ref, bf16[256,1024]{1,0:T(8,128)(2,1)S(1)} %collective-permute-done.6.fu.rest_3_, bf16[256,1024]{1,0:T(8,128)(2,1)S(1)} %collective-permute-done.7.fl.rest_4_, ...), custom_call_target="tpu_custom_call" | custom-call | flops 4255000064 | bytes 1000 | tf_op jit(solution)/shard_map/end_values/pallas_call | solution.py:274
  64.7 5.6 %weight_terms.1 = (f32[4,8,32,512]{3,2,1,0:T(8,128)}, f32[4,8,32,512]{3,2,1,0:T(8,128)}) custom-call(s32[3]{0:T(128)S(1)} %pad_add_fusion.place, f32[1024,256]{1,0:T(8,128)S(1)} %get-tuple-element.30.near_a, f32[1024,256]{1,0:T(8,128)S(1)} %get-tuple-element.32.near_b, bf16[1024,512]{1,0:T(8,128)(2,1)S(1)} %copy-done.4, ...), custom_call_target="tpu_custom_call" | custom-call | flops 5750000128 | bytes 1000 | tf_op jit(solution)/shard_map/weight_terms/pallas_call | solution.py:348
  70.6 2.1 %collective-permute-start.10 = (bf16[2,128,128]{2,1,0:T(8,128)(2,1)S(1)}, bf16[2,128,128]{2,1,0:T(8,128)(2,1)S(1)}, u32[]{:S(2)}, u32[]{:S(2)}) collective-permute-start(bf16[2,128,128]{2,1,0:T(8,128)(2,1)S(1)} %fusion.20.rest_5_), channel_id=1, source_target_pairs={{0,16},{8,24},{16,0},{24,8},{1,17},{9,25},{17,1},{25,9},{2,18},{10... | collective-permute-start | bytes 196616 | tf_op jit(solution)/shard_map/ppermute | solution.py:32
  73.6 2.4 %collective-permute-start.9 = (bf16[2,128,128]{2,1,0:T(8,128)(2,1)S(1)}, bf16[2,128,128]{2,1,0:T(8,128)(2,1)S(1)}, u32[]{:S(2)}, u32[]{:S(2)}) collective-permute-start(bf16[2,128,128]{2,1,0:T(8,128)(2,1)S(1)} %fusion.20.rest_5_), channel_id=1, source_target_pairs={{0,8},{8,16},{16,24},{24,0},{1,9},{9,17},{17,25},{25,1},{2,10},{10... | collective-permute-start | bytes 196616 | tf_op jit(solution)/shard_map/ppermute | solution.py:32
  76.5 1.8 %collective-permute-done.11 = bf16[2,128,128]{2,1,0:T(8,128)(2,1)S(1)} collective-permute-done((bf16[2,128,128]{2,1,0:T(8,128)(2,1)S(1)}, bf16[2,128,128]{2,1,0:T(8,128)(2,1)S(1)}, u32[]{:S(2)}, u32[]{:S(2)}) %collective-permute-start.11) | collective-permute-done | bytes 65568 | tf_op jit(solution)/shard_map/ppermute | solution.py:32
  78.5 3.0 %pair_sums.1 = (f32[8,32,512]{2,1,0:T(8,128)S(1)}, bf16[8,32,512]{2,1,0:T(8,128)(2,1)S(1)}, bf16[8,32,512]{2,1,0:T(8,128)(2,1)S(1)}, bf16[8,32,512]{2,1,0:T(8,128)(2,1)S(1)}) custom-call(s32[3]{0:T(128)S(1)} %pad_add_fusion.place, f32[4,8,32,512]{3,2,1,0:T(8,128)} %get-tuple-element.42.kept_u.kept_l, f32[4,8,32,512]{3,2,1,0:T(8,128)} %get-tuple-element.42.kept_u.kept_l, ...), custom_call_target="tpu_custom_call" | custom-call | flops 1264999936 | bytes 1000 | tf_op jit(solution)/shard_map/pair_sums/pallas_call | solution.py:393
  82.0 3.3 %collective-permute-start.20 = (bf16[8,32,512]{2,1,0:T(8,128)(2,1)S(1)}, bf16[8,32,512]{2,1,0:T(8,128)(2,1)S(1)}, u32[]{:S(2)}, u32[]{:S(2)}) collective-permute-start(bf16[8,32,512]{2,1,0:T(8,128)(2,1)S(1)} %get-tuple-element.46), channel_id=1, source_target_pairs={{0,8},{8,16},{16,24},{24,0},{1,9},{9,17},{17,25},{25,1},{2,10},{10... | collective-permute-start | bytes 786440 | tf_op jit(solution)/shard_map/ppermute | solution.py:32
  85.3 2.0 %collective-permute-start.22 = (bf16[8,32,512]{2,1,0:T(8,128)(2,1)S(1)}, bf16[8,32,512]{2,1,0:T(8,128)(2,1)S(1)}, u32[]{:S(2)}, u32[]{:S(2)}) collective-permute-start(bf16[8,32,512]{2,1,0:T(8,128)(2,1)S(1)} %get-tuple-element.48), channel_id=1, source_target_pairs={{0,16},{8,24},{16,0},{24,8},{1,17},{9,25},{17,1},{25,9},{2,18},{10... | collective-permute-start | bytes 786440 | tf_op jit(solution)/shard_map/ppermute | solution.py:32
  87.3 7.2 %begin_attended.1.total_u.total_l = f32[4,128,1024]{2,1,0:T(8,128)} custom-call(s32[3]{0:T(128)S(1)} %pad_add_fusion.place, bf16[4,128,1024]{2,1,0:T(8,128)(2,1)} %get-tuple-element.26.turned_ref, bf16[17,4,1024]{2,1,0:T(4,128)(2,1)S(1)} %copy-done, bf16[512,1024]{1,0:T(8,128)(2,1)} %get-tuple-element.34.v_ref, ...), custom_call_target="tpu_custom_call" | custom-call | flops 345000000 | bytes 1000 | tf_op jit(solution)/shard_map/begin_attended/pallas_call | solution.py:463
  94.6 2.3 %collective-permute-done.20 = bf16[8,32,512]{2,1,0:T(8,128)(2,1)S(1)} collective-permute-done((bf16[8,32,512]{2,1,0:T(8,128)(2,1)S(1)}, bf16[8,32,512]{2,1,0:T(8,128)(2,1)S(1)}, u32[]{:S(2)}, u32[]{:S(2)}) %collective-permute-start.20) | collective-permute-done | bytes 262176 | tf_op jit(solution)/shard_map/ppermute | solution.py:32
  96.9 3.4 %collective-permute-done.21 = bf16[8,32,512]{2,1,0:T(8,128)(2,1)S(1)} collective-permute-done((bf16[8,32,512]{2,1,0:T(8,128)(2,1)S(1)}, bf16[8,32,512]{2,1,0:T(8,128)(2,1)S(1)}, u32[]{:S(2)}, u32[]{:S(2)}) %collective-permute-start.21) | collective-permute-done | bytes 262176 | tf_op jit(solution)/shard_map/ppermute | solution.py:32
  101.2 3.2 %collective-permute-start.23 = (bf16[2,128,128]{2,1,0:T(8,128)(2,1)S(1)}, bf16[2,128,128]{2,1,0:T(8,128)(2,1)S(1)}, u32[]{:S(2)}, u32[]{:S(2)}) collective-permute-start(bf16[2,128,128]{2,1,0:T(8,128)(2,1)S(1)} %fusion.13), channel_id=1, source_target_pairs={{0,64},{32,96},{64,0},{96,32},{128,192},{160,224},{192,128},{224,1... | collective-permute-start | bytes 196616 | tf_op jit(solution)/shard_map/ppermute | solution.py:36
  104.4 2.5 %collective-permute-done.23 = bf16[2,128,128]{2,1,0:T(8,128)(2,1)S(1)} collective-permute-done((bf16[2,128,128]{2,1,0:T(8,128)(2,1)S(1)}, bf16[2,128,128]{2,1,0:T(8,128)(2,1)S(1)}, u32[]{:S(2)}, u32[]{:S(2)}) %collective-permute-start.23) | collective-permute-done | bytes 65568 | tf_op jit(solution)/shard_map/ppermute | solution.py:36
  106.9 9.0 %collective-permute-start.24 = (bf16[2,128,128]{2,1,0:T(8,128)(2,1)S(1)}, bf16[2,128,128]{2,1,0:T(8,128)(2,1)S(1)}, u32[]{:S(2)}, u32[]{:S(2)}) collective-permute-start(bf16[2,128,128]{2,1,0:T(8,128)(2,1)S(1)} %get-tuple-element.60), channel_id=1, source_target_pairs={{0,128},{32,160},{64,192},{96,224},{1,129},{33,161},{65,193},{97,2... | collective-permute-start | bytes 196616 | tf_op jit(solution)/shard_map/ppermute | solution.py:602
  115.9 3.4 %all-to-all-start = ((bf16[8,32,512]{2,1,0:T(8,128)(2,1)}), bf16[8,32,512]{2,1,0:T(8,128)(2,1)S(1)}, u32[]{:S(2)}, u32[]{:S(2)}) async-start(bf16[8,32,512]{2,1,0:T(8,128)(2,1)} %add_convert_fusion), calls=%async_computation | async-start | bytes 524288 | tf_op jit(solution)/shard_map/all_to_all | solution.py:603
  120.9 5.1 %end_attended.1 = bf16[1024,512]{1,0:T(8,128)(2,1)} custom-call(s32[3]{0:T(128)S(1)} %pad_add_fusion.place, bf16[4,128,1024]{2,1,0:T(8,128)(2,1)} %get-tuple-element.26.turned_ref, bf16[17,4,1024]{2,1,0:T(4,128)(2,1)S(1)} %copy-done, f32[4,128,1024]{2,1,0:T(8,128)} %begin_attended.1.total_u.total_l, f32[4,128,1024]{2,1,0:T(8,128)} %begin_attended.1.total_u.total_l, ...), custom_call_target="tpu_custom_call" | custom-call | flops 345000000 | bytes 1000 | tf_op jit(solution)/shard_map/end_attended/pallas_call | solution.py:502
  126.1 3.7 %all-to-all-done = bf16[8,32,512]{2,1,0:T(8,128)(2,1)S(1)} async-done(((bf16[8,32,512]{2,1,0:T(8,128)(2,1)}), bf16[8,32,512]{2,1,0:T(8,128)(2,1)S(1)}, u32[]{:S(2)}, u32[]{:S(2)}) %all-to-all-start) | async-done | bytes 262176 | tf_op jit(solution)/shard_map/all_to_all | solution.py:603
  (66 shorter events, 15.8 us)
Async XLA Ops:
  6.6 5.6 %copy-start.2 = (bf16[1024,512]{1,0:T(8,128)(2,1)S(1)}, bf16[1024,512]{1,0:T(8,128)(2,1)}, u32[]{:S(2)}) copy-start(bf16[1024,512]{1,0:T(8,128)(2,1)} %in_ref.2) | copy-start | bytes 3145732
  6.6 2.1 %collective-permute-start = (f32[5,2,128,128]{3,2,1,0:T(8,128)S(1)}, f32[5,2,128,128]{3,2,1,0:T(8,128)S(1)}, u32[]{:S(2)}, u32[]{:S(2)}) collective-permute-start(f32[5,2,128,128]{3,2,1,0:T(8,128)S(1)} %get-tuple-element.28), channel_id=1, source_target_pairs={{0,4},{4,0},{1,5},{5,1},{2,6},{6,2},{3,7},{7,3},{8,12},{12,8},{9,1... | collective-permute-start | bytes 1966088 | tf_op jit(solution)/shard_map/ppermute | solution.py:36
  8.8 7.2 %collective-permute-start.3 = (bf16[3,2,128,128]{3,2,1,0:T(8,128)(2,1)S(1)}, bf16[3,2,128,128]{3,2,1,0:T(8,128)(2,1)S(1)}, u32[]{:S(2)}, u32[]{:S(2)}) collective-permute-start(bf16[3,2,128,128]{3,2,1,0:T(8,128)(2,1)S(1)} %slice.139.rest_0_), channel_id=1, source_target_pairs={{0,32},{32,0},{64,96},{96,64},{128,160},{160,128},{192,224},{224,1... | collective-permute-start | bytes 589832 | tf_op jit(solution)/shard_map/ppermute | solution.py:36
  10.8 33.7 %collective-permute-start.16 = (f32[4,128,128]{2,1,0:T(8,128)S(1)}, f32[4,128,128]{2,1,0:T(8,128)S(1)}, u32[]{:S(2)}, u32[]{:S(2)}) collective-permute-start(f32[4,128,128]{2,1,0:T(8,128)S(1)} %get-tuple-element.40), channel_id=1, source_target_pairs={{4,0},{5,1},{6,2},{7,3},{12,8},{13,9},{14,10},{15,11},{20,16},{21,... | collective-permute-start | bytes 786440 | tf_op jit(solution)/shard_map/ppermute | solution.py:553
  12.2 7.3 %copy-start = (bf16[17,4,1024]{2,1,0:T(4,128)(2,1)S(1)}, bf16[17,4,1024]{2,1,0:T(4,128)(2,1)}, u32[]{:S(2)}) copy-start(bf16[17,4,1024]{2,1,0:T(4,128)(2,1)} %lw_ref.9) | copy-start | bytes 417796
  12.2 7.3 %copy-start.3 = (bf16[1024,512]{1,0:T(8,128)(2,1)S(1)}, bf16[1024,512]{1,0:T(8,128)(2,1)}, u32[]{:S(2)}) copy-start(bf16[1024,512]{1,0:T(8,128)(2,1)} %g_ref.3) | copy-start | bytes 3145732
  12.2 7.3 %copy-start.4 = (bf16[1024,512]{1,0:T(8,128)(2,1)S(1)}, bf16[1024,512]{1,0:T(8,128)(2,1)}, u32[]{:S(2)}) copy-start(bf16[1024,512]{1,0:T(8,128)(2,1)} %k_ref.7) | copy-start | bytes 3145732
  12.8 25.9 %collective-permute-start.1 = (bf16[512,1024]{1,0:T(8,128)(2,1)S(1)}, bf16[512,1024]{1,0:T(8,128)(2,1)S(1)}, u32[]{:S(2)}, u32[]{:S(2)}) collective-permute-start(bf16[512,1024]{1,0:T(8,128)(2,1)S(1)} %turn_features.1.own.rest_0_), channel_id=1, source_target_pairs={{0,1},{1,2},{2,3},{3,0},{4,5},{5,6},{6,7},{7,4},{8,9},{9,10},{10,1... | collective-permute-start | bytes 3145736 | tf_op jit(solution)/shard_map/ppermute | solution.py:32
  13.1 27.2 %collective-permute-start.2 = (bf16[512,1024]{1,0:T(8,128)(2,1)S(1)}, bf16[512,1024]{1,0:T(8,128)(2,1)S(1)}, u32[]{:S(2)}, u32[]{:S(2)}) collective-permute-start(bf16[512,1024]{1,0:T(8,128)(2,1)S(1)} %turn_features.1.own.rest_0_), channel_id=1, source_target_pairs={{0,3},{1,0},{2,1},{3,2},{4,7},{5,4},{6,5},{7,6},{8,11},{9,8},{10,9... | collective-permute-start | bytes 3145736 | tf_op jit(solution)/shard_map/ppermute | solution.py:32
  16.1 9.5 %collective-permute-start.4 = (bf16[2,2,128,128]{3,2,1,0:T(8,128)(2,1)S(1)}, bf16[2,2,128,128]{3,2,1,0:T(8,128)(2,1)S(1)}, u32[]{:S(2)}, u32[]{:S(2)}) collective-permute-start(bf16[2,2,128,128]{3,2,1,0:T(8,128)(2,1)S(1)} %pad_maximum_fusion.3.rest_0_), channel_id=1, source_target_pairs={{0,64},{32,96},{64,0},{96,32},{128,192},{160,224},{192,128},{224,1... | collective-permute-start | bytes 393224 | tf_op jit(solution)/shard_map/ppermute | solution.py:36
  19.4 5.2 %copy-start.1 = (bf16[2048,512]{1,0:T(8,128)(2,1)S(1)}, bf16[2048,512]{1,0:T(8,128)(2,1)}, u32[]{:S(2)}) copy-start(bf16[2048,512]{1,0:T(8,128)(2,1)} %in_ref.3) | copy-start | bytes 6291460
  25.6 10.1 %collective-permute-start.5 = (bf16[2,128,128]{2,1,0:T(8,128)(2,1)S(1)}, bf16[2,128,128]{2,1,0:T(8,128)(2,1)S(1)}, u32[]{:S(2)}, u32[]{:S(2)}) collective-permute-start(bf16[2,128,128]{2,1,0:T(8,128)(2,1)S(1)} %fusion.15.rest_0_), channel_id=1, source_target_pairs={{128,0},{160,32},{192,64},{224,96},{129,1},{161,33},{193,65},{225,... | collective-permute-start | bytes 196616 | tf_op jit(solution)/shard_map/ppermute | solution.py:558
  40.4 9.5 %collective-permute-start.13 = (bf16[2,128,128]{2,1,0:T(8,128)(2,1)S(1)}, bf16[2,128,128]{2,1,0:T(8,128)(2,1)S(1)}, u32[]{:S(2)}, u32[]{:S(2)}) collective-permute-start(bf16[2,128,128]{2,1,0:T(8,128)(2,1)S(1)} %get-tuple-element.54), channel_id=1, source_target_pairs={{0,8},{8,16},{16,24},{24,0},{1,9},{9,17},{17,25},{25,1},{2,10},{10... | collective-permute-start | bytes 196616 | tf_op jit(solution)/shard_map/ppermute | solution.py:32
  41.0 9.0 %collective-permute-start.14 = (bf16[2,128,128]{2,1,0:T(8,128)(2,1)S(1)}, bf16[2,128,128]{2,1,0:T(8,128)(2,1)S(1)}, u32[]{:S(2)}, u32[]{:S(2)}) collective-permute-start(bf16[2,128,128]{2,1,0:T(8,128)(2,1)S(1)} %get-tuple-element.55), channel_id=1, source_target_pairs={{0,24},{8,0},{16,8},{24,16},{1,25},{9,1},{17,9},{25,17},{2,26},{10... | collective-permute-start | bytes 196616 | tf_op jit(solution)/shard_map/ppermute | solution.py:32
  42.6 7.4 %collective-permute-start.15 = (bf16[2,128,128]{2,1,0:T(8,128)(2,1)S(1)}, bf16[2,128,128]{2,1,0:T(8,128)(2,1)S(1)}, u32[]{:S(2)}, u32[]{:S(2)}) collective-permute-start(bf16[2,128,128]{2,1,0:T(8,128)(2,1)S(1)} %fusion.12.rest_0_), channel_id=1, source_target_pairs={{0,16},{8,24},{16,0},{24,8},{1,17},{9,25},{17,1},{25,9},{2,18},{10... | collective-permute-start | bytes 196616 | tf_op jit(solution)/shard_map/ppermute | solution.py:32
  44.1 13.2 %collective-permute-start.6 = (bf16[256,1024]{1,0:T(8,128)(2,1)S(1)}, bf16[256,1024]{1,0:T(8,128)(2,1)S(1)}, u32[]{:S(2)}, u32[]{:S(2)}) collective-permute-start(bf16[256,1024]{1,0:T(8,128)(2,1)S(1)} %slice.79), channel_id=1, source_target_pairs={{0,1},{1,2},{2,3},{3,0},{4,5},{5,6},{6,7},{7,4},{8,9},{9,10},{10,1... | collective-permute-start | bytes 1572872 | tf_op jit(solution)/shard_map/ppermute | solution.py:32
  44.5 14.3 %collective-permute-start.7 = (bf16[256,1024]{1,0:T(8,128)(2,1)S(1)}, bf16[256,1024]{1,0:T(8,128)(2,1)S(1)}, u32[]{:S(2)}, u32[]{:S(2)}) collective-permute-start(bf16[256,1024]{1,0:T(8,128)(2,1)S(1)} %slice.80), channel_id=1, source_target_pairs={{0,3},{1,0},{2,1},{3,2},{4,7},{5,4},{6,5},{7,6},{8,11},{9,8},{10,9... | collective-permute-start | bytes 1572872 | tf_op jit(solution)/shard_map/ppermute | solution.py:32
  62.9 1.3 %collective-permute-start.17 = (f32[2,128,128]{2,1,0:T(8,128)S(1)}, f32[2,128,128]{2,1,0:T(8,128)S(1)}, u32[]{:S(2)}, u32[]{:S(2)}) collective-permute-start(f32[2,128,128]{2,1,0:T(8,128)S(1)} %get-tuple-element.41), channel_id=1, source_target_pairs={{0,4},{4,0},{1,5},{5,1},{2,6},{6,2},{3,7},{7,3},{8,12},{12,8},{9,1... | collective-permute-start | bytes 393224 | tf_op jit(solution)/shard_map/ppermute | solution.py:36
  62.9 1.7 %collective-permute-start.8 = (f32[4,128,128]{2,1,0:T(8,128)S(1)}, f32[4,128,128]{2,1,0:T(8,128)S(1)}, u32[]{:S(2)}, u32[]{:S(2)}) collective-permute-start(f32[4,128,128]{2,1,0:T(8,128)S(1)} %get-tuple-element.39), channel_id=1, source_target_pairs={{0,4},{4,0},{1,5},{5,1},{2,6},{6,2},{3,7},{7,3},{8,12},{12,8},{9,1... | collective-permute-start | bytes 786440 | tf_op jit(solution)/shard_map/ppermute | solution.py:36
  70.3 8.2 %collective-permute-start.18 = (f32[4,8,32,512]{3,2,1,0:T(8,128)}, f32[4,8,32,512]{3,2,1,0:T(8,128)S(1)}, u32[]{:S(2)}, u32[]{:S(2)}) collective-permute-start(f32[4,8,32,512]{3,2,1,0:T(8,128)} %get-tuple-element.43), channel_id=1, source_target_pairs={{0,4},{4,0},{1,5},{5,1},{2,6},{6,2},{3,7},{7,3},{8,12},{12,8},{9,1... | collective-permute-start | bytes 6291464 | tf_op jit(solution)/shard_map/ppermute | solution.py:36
  70.6 5.8 %collective-permute-start.10 = (bf16[2,128,128]{2,1,0:T(8,128)(2,1)S(1)}, bf16[2,128,128]{2,1,0:T(8,128)(2,1)S(1)}, u32[]{:S(2)}, u32[]{:S(2)}) collective-permute-start(bf16[2,128,128]{2,1,0:T(8,128)(2,1)S(1)} %fusion.20.rest_5_), channel_id=1, source_target_pairs={{0,16},{8,24},{16,0},{24,8},{1,17},{9,25},{17,1},{25,9},{2,18},{10... | collective-permute-start | bytes 196616 | tf_op jit(solution)/shard_map/ppermute | solution.py:32
  72.7 5.5 %collective-permute-start.11 = (bf16[2,128,128]{2,1,0:T(8,128)(2,1)S(1)}, bf16[2,128,128]{2,1,0:T(8,128)(2,1)S(1)}, u32[]{:S(2)}, u32[]{:S(2)}) collective-permute-start(bf16[2,128,128]{2,1,0:T(8,128)(2,1)S(1)} %fusion.20.rest_5_), channel_id=1, source_target_pairs={{0,24},{8,0},{16,8},{24,16},{1,25},{9,1},{17,9},{25,17},{2,26},{10... | collective-permute-start | bytes 196616 | tf_op jit(solution)/shard_map/ppermute | solution.py:32
  73.6 4.6 %collective-permute-start.9 = (bf16[2,128,128]{2,1,0:T(8,128)(2,1)S(1)}, bf16[2,128,128]{2,1,0:T(8,128)(2,1)S(1)}, u32[]{:S(2)}, u32[]{:S(2)}) collective-permute-start(bf16[2,128,128]{2,1,0:T(8,128)(2,1)S(1)} %fusion.20.rest_5_), channel_id=1, source_target_pairs={{0,8},{8,16},{16,24},{24,0},{1,9},{9,17},{17,25},{25,1},{2,10},{10... | collective-permute-start | bytes 196616 | tf_op jit(solution)/shard_map/ppermute | solution.py:32
  78.3 3.7 %collective-permute-start.12 = (bf16[2,2,128,128]{3,2,1,0:T(8,128)(2,1)S(1)}, bf16[2,2,128,128]{3,2,1,0:T(8,128)(2,1)S(1)}, u32[]{:S(2)}, u32[]{:S(2)}) collective-permute-start(bf16[2,2,128,128]{3,2,1,0:T(8,128)(2,1)S(1)} %pad_maximum_fusion.4), channel_id=1, source_target_pairs={{0,4},{4,0},{1,5},{5,1},{2,6},{6,2},{3,7},{7,3},{8,12},{12,8},{9,1... | collective-permute-start | bytes 393224 | tf_op jit(solution)/shard_map/ppermute | solution.py:36
  81.5 13.0 %collective-permute-start.19 = (bf16[2,128,128]{2,1,0:T(8,128)(2,1)S(1)}, bf16[2,128,128]{2,1,0:T(8,128)(2,1)S(1)}, u32[]{:S(2)}, u32[]{:S(2)}) collective-permute-start(bf16[2,128,128]{2,1,0:T(8,128)(2,1)S(1)} %get-tuple-element.45.rest_6_), channel_id=1, source_target_pairs={{0,32},{32,0},{64,96},{96,64},{128,160},{160,128},{192,224},{224,1... | collective-permute-start | bytes 196616 | tf_op jit(solution)/shard_map/ppermute | solution.py:36
  82.0 14.9 %collective-permute-start.20 = (bf16[8,32,512]{2,1,0:T(8,128)(2,1)S(1)}, bf16[8,32,512]{2,1,0:T(8,128)(2,1)S(1)}, u32[]{:S(2)}, u32[]{:S(2)}) collective-permute-start(bf16[8,32,512]{2,1,0:T(8,128)(2,1)S(1)} %get-tuple-element.46), channel_id=1, source_target_pairs={{0,8},{8,16},{16,24},{24,0},{1,9},{9,17},{17,25},{25,1},{2,10},{10... | collective-permute-start | bytes 786440 | tf_op jit(solution)/shard_map/ppermute | solution.py:32
  85.3 15.0 %collective-permute-start.21 = (bf16[8,32,512]{2,1,0:T(8,128)(2,1)S(1)}, bf16[8,32,512]{2,1,0:T(8,128)(2,1)S(1)}, u32[]{:S(2)}, u32[]{:S(2)}) collective-permute-start(bf16[8,32,512]{2,1,0:T(8,128)(2,1)S(1)} %get-tuple-element.47), channel_id=1, source_target_pairs={{0,24},{8,0},{16,8},{24,16},{1,25},{9,1},{17,9},{25,17},{2,26},{10... | collective-permute-start | bytes 786440 | tf_op jit(solution)/shard_map/ppermute | solution.py:32
  85.3 15.0 %collective-permute-start.22 = (bf16[8,32,512]{2,1,0:T(8,128)(2,1)S(1)}, bf16[8,32,512]{2,1,0:T(8,128)(2,1)S(1)}, u32[]{:S(2)}, u32[]{:S(2)}) collective-permute-start(bf16[8,32,512]{2,1,0:T(8,128)(2,1)S(1)} %get-tuple-element.48), channel_id=1, source_target_pairs={{0,16},{8,24},{16,0},{24,8},{1,17},{9,25},{17,1},{25,9},{2,18},{10... | collective-permute-start | bytes 786440 | tf_op jit(solution)/shard_map/ppermute | solution.py:32
  101.2 5.7 %collective-permute-start.23 = (bf16[2,128,128]{2,1,0:T(8,128)(2,1)S(1)}, bf16[2,128,128]{2,1,0:T(8,128)(2,1)S(1)}, u32[]{:S(2)}, u32[]{:S(2)}) collective-permute-start(bf16[2,128,128]{2,1,0:T(8,128)(2,1)S(1)} %fusion.13), channel_id=1, source_target_pairs={{0,64},{32,96},{64,0},{96,32},{128,192},{160,224},{192,128},{224,1... | collective-permute-start | bytes 196616 | tf_op jit(solution)/shard_map/ppermute | solution.py:36
  106.9 12.5 %collective-permute-start.24 = (bf16[2,128,128]{2,1,0:T(8,128)(2,1)S(1)}, bf16[2,128,128]{2,1,0:T(8,128)(2,1)S(1)}, u32[]{:S(2)}, u32[]{:S(2)}) collective-permute-start(bf16[2,128,128]{2,1,0:T(8,128)(2,1)S(1)} %get-tuple-element.60), channel_id=1, source_target_pairs={{0,128},{32,160},{64,192},{96,224},{1,129},{33,161},{65,193},{97,2... | collective-permute-start | bytes 196616 | tf_op jit(solution)/shard_map/ppermute | solution.py:602
  115.9 13.8 %all-to-all-start = ((bf16[8,32,512]{2,1,0:T(8,128)(2,1)}), bf16[8,32,512]{2,1,0:T(8,128)(2,1)S(1)}, u32[]{:S(2)}, u32[]{:S(2)}) async-start(bf16[8,32,512]{2,1,0:T(8,128)(2,1)} %add_convert_fusion), calls=%async_computation | async-start | bytes 524288 | tf_op jit(solution)/shard_map/all_to_all | solution.py:603
  119.4 1.5 %collective-permute-start.25 = (bf16[3,2,128,128]{3,2,1,0:T(8,128)(2,1)S(1)}, bf16[3,2,128,128]{3,2,1,0:T(8,128)(2,1)S(1)}, u32[]{:S(2)}, u32[]{:S(2)}) collective-permute-start(bf16[3,2,128,128]{3,2,1,0:T(8,128)(2,1)S(1)} %pad_maximum_fusion.2), channel_id=1, source_target_pairs={{0,4},{4,0},{1,5},{5,1},{2,6},{6,2},{3,7},{7,3},{8,12},{12,8},{9,1... | collective-permute-start | bytes 589832 | tf_op jit(solution)/shard_map/ppermute | solution.py:36

commit v4 on v3

--- a/solution.py
+++ b/solution.py
@@ -566,7 +566,7 @@
         summed = summed + shift(message, "x", distance, NX).astype(F32)
     begun = begin_values(place, (own, left, right), turned_weight, message)
     values, state = end_values(place, begun, (fu, fl), turned_weight, keys, message)
-    other = swap(behind(summed, state), "core", 1, 2)
+    other = swap(summed, "core", 1, 2)
     mine = (summed + first_got[:2]).astype(BF)
     other = (other + first_got[2:]).astype(BF)
 
@@ -594,7 +594,7 @@
     level_3 = jnp.where(z & 1 == 1, got, 0.0)
     running = running + got
     rows = rows.astype(BF)
-    message = behind(running.astype(BF), begun, rows)
+    message = behind(running.astype(BF), begun, first)
     got = swap(message, "z", 2, NZ).astype(F32)
     level_4 = jnp.where(z & 2 == 2, got, 0.0)
     running = running + got
@@ -603,6 +603,7 @@
     rows = lax.all_to_all(rows, "z", 0, 0, tiled=True)
     weight_grad = rows.astype(F32).sum(axis=0)
     upper_levels = jnp.stack([level_3.astype(BF), level_4.astype(BF), level_5])
+    upper_levels = behind(upper_levels, rows)
     attended = end_attended(place, turned_queries, level_weights, begun, both(upper_levels))
     return attended, weight_grad
 

time: 131 us -> 130 us (level)
  the two profiles are of different devices: /device:TPU:30 before, /device:TPU:1 now
where the time goes in v4:
time: 130 us
  starting transfers between devices  53 us (41%)
  Pallas kernels  46.2 us (36%)
  waiting for transfers between devices  27.1 us (21%)
  other arithmetic  2.26 us (2%)
    ppermute x10, starting transfers between devices, swap(): return lax.ppermute(value, axis, [(i, i ^ distance) for i in range(size)])  20.2 us
    ppermute x13, waiting for transfers between devices, shift(): lax.ppermute(value, axis, [(i, (i + distance) % size) for i in range(size)])  18.8 us
    ppermute x13, starting transfers between devices, shift(): lax.ppermute(value, axis, [(i, (i + distance) % size) for i in range(size)])  15.9 us
    pallas_call x2, Pallas kernels, near(): pl.pallas_call(functools.partial(near_kernel, base), grid=(2,), in_specs=...  10.3 us
    ppermute x1, starting transfers between devices, local(): level_5 = lax.ppermute(message, 'z', [(i, i + 4) for i in range(4)])  7.27 us
    pallas_call x1, Pallas kernels, begin_attended(): pl.pallas_call(begin_attended_kernel, grid_spec=pltpu.PrefetchScalarGridS...  7.2 us
    all_to_all x1, starting transfers between devices, local(): rows = lax.all_to_all(rows, 'z', 0, 0, tiled=True)  5.92 us
    pallas_call x1, Pallas kernels, query_states(): pl.pallas_call(query_state_kernel, grid_spec=pltpu.PrefetchScalarGridSpec...  5.86 us
  transfers between devices with their start and end apart: 27, of which 13 were waited for; matrix products, arithmetic and copies ran while one was open for 2% of the time, Pallas kernels for 23%

profile of v4, /device:TPU:1, one launch (start us, length us, event | category | flops | bytes accessed | tf_op | source)
XLA Modules:
  0.0 129.6 jit_solution(520113703813197200)
XLA Ops:
  0.7 5.9 %query_states.1 = (f32[4,128,128]{2,1,0:T(8,128)S(1)}, f32[5,2,128,128]{3,2,1,0:T(8,128)S(1)}, f32[5,2,128,128]{3,2,1,0:T(8,128)S(1)}, bf16[4,128,1024]{2,1,0:T(8,128)(2,1)}) custom-call(s32[3]{0:T(128)S(1)} %pad_add_fusion.place, bf16[1024,512]{1,0:T(8,128)(2,1)} %q_l.1, bf16[1024,512]{1,0:T(8,128)(2,1)} %q_l.1, bf16[1024,512]{1,0:T(8,128)(2,1)} %g_ref.3, ...), custom_call_target="tpu_custom_call" | custom-call | flops 4600000000 | bytes 1000 | tf_op jit(solution)/shard_map/query_states/pallas_call | solution.py:122
  6.6 3.2 %collective-permute-start = (f32[5,2,128,128]{3,2,1,0:T(8,128)S(1)}, f32[5,2,128,128]{3,2,1,0:T(8,128)S(1)}, u32[]{:S(2)}, u32[]{:S(2)}) collective-permute-start(f32[5,2,128,128]{3,2,1,0:T(8,128)S(1)} %get-tuple-element.28), channel_id=1, source_target_pairs={{0,4},{4,0},{1,5},{5,1},{2,6},{6,2},{3,7},{7,3},{8,12},{12,8},{9,1... | collective-permute-start | bytes 1966088 | tf_op jit(solution)/shard_map/ppermute | solution.py:36
  9.8 1.7 %collective-permute-done = f32[5,2,128,128]{3,2,1,0:T(8,128)S(1)} collective-permute-done((f32[5,2,128,128]{3,2,1,0:T(8,128)S(1)}, f32[5,2,128,128]{3,2,1,0:T(8,128)S(1)}, u32[]{:S(2)}, u32[]{:S(2)}) %collective-permute-start) | collective-permute-done | bytes 655392 | tf_op jit(solution)/shard_map/ppermute | solution.py:36
  11.8 2.4 %collective-permute-start.16 = (f32[4,128,128]{2,1,0:T(8,128)S(1)}, f32[4,128,128]{2,1,0:T(8,128)S(1)}, u32[]{:S(2)}, u32[]{:S(2)}) collective-permute-start(f32[4,128,128]{2,1,0:T(8,128)S(1)} %get-tuple-element.40), channel_id=1, source_target_pairs={{4,0},{5,1},{6,2},{7,3},{12,8},{13,9},{14,10},{15,11},{20,16},{21,... | collective-permute-start | bytes 786440 | tf_op jit(solution)/shard_map/ppermute | solution.py:553
  16.3 1.5 %collective-permute-start.2 = (bf16[512,1024]{1,0:T(8,128)(2,1)S(1)}, bf16[512,1024]{1,0:T(8,128)(2,1)S(1)}, u32[]{:S(2)}, u32[]{:S(2)}) collective-permute-start(bf16[512,1024]{1,0:T(8,128)(2,1)S(1)} %turn_features.1.own.rest_0_), channel_id=1, source_target_pairs={{0,3},{1,0},{2,1},{3,2},{4,7},{5,4},{6,5},{7,6},{8,11},{9,8},{10,9... | collective-permute-start | bytes 3145736 | tf_op jit(solution)/shard_map/ppermute | solution.py:32
  17.9 3.1 %collective-permute-start.4 = (bf16[2,2,128,128]{3,2,1,0:T(8,128)(2,1)S(1)}, bf16[2,2,128,128]{3,2,1,0:T(8,128)(2,1)S(1)}, u32[]{:S(2)}, u32[]{:S(2)}) collective-permute-start(bf16[2,2,128,128]{3,2,1,0:T(8,128)(2,1)S(1)} %pad_maximum_fusion.3.rest_0_), channel_id=1, source_target_pairs={{0,64},{32,96},{64,0},{96,32},{128,192},{160,224},{192,128},{224,1... | collective-permute-start | bytes 393224 | tf_op jit(solution)/shard_map/ppermute | solution.py:36
  21.0 5.2 %near.2 = (f32[1024,256]{1,0:T(8,128)S(1)}, bf16[2,5,256,256]{3,2,1,0:T(8,128)(2,1)}, bf16[2,5,256,256]{3,2,1,0:T(8,128)(2,1)}) custom-call(bf16[1024,512]{1,0:T(8,128)(2,1)S(1)} %copy-done.4, bf16[4,128,1024]{2,1,0:T(8,128)(2,1)} %get-tuple-element.26.turned_ref, bf16[1024,512]{1,0:T(8,128)(2,1)S(1)} %copy-done.3, bf16[17,4,1024]{2,1,0:T(4,128)(2,1)S(1)} %copy-done, ...), custom_call_target="tpu_custom_call" | custom-call | flops 3680000000 | bytes 1000 | tf_op jit(solution)/shard_map/near/pallas_call | solution.py:200
  28.6 5.1 %near.3 = (f32[1024,256]{1,0:T(8,128)S(1)}, bf16[2,5,256,256]{3,2,1,0:T(8,128)(2,1)}, bf16[2,5,256,256]{3,2,1,0:T(8,128)(2,1)}) custom-call(bf16[1024,512]{1,0:T(8,128)(2,1)S(1)} %copy-done.4, bf16[4,128,1024]{2,1,0:T(8,128)(2,1)} %get-tuple-element.26.turned_ref, bf16[1024,512]{1,0:T(8,128)(2,1)S(1)} %copy-done.3, bf16[17,4,1024]{2,1,0:T(4,128)(2,1)S(1)} %copy-done, ...), custom_call_target="tpu_custom_call" | custom-call | flops 3680000000 | bytes 1000 | tf_op jit(solution)/shard_map/near/pallas_call | solution.py:200
  33.7 2.5 %collective-permute-done.5 = bf16[2,128,128]{2,1,0:T(8,128)(2,1)S(1)} collective-permute-done((bf16[2,128,128]{2,1,0:T(8,128)(2,1)S(1)}, bf16[2,128,128]{2,1,0:T(8,128)(2,1)S(1)}, u32[]{:S(2)}, u32[]{:S(2)}) %collective-permute-start.5) | collective-permute-done | bytes 65568 | tf_op jit(solution)/shard_map/ppermute | solution.py:558
  36.2 4.8 %collective-permute-done.1.left.rest_1_ = bf16[512,1024]{1,0:T(8,128)(2,1)S(1)} collective-permute-done((bf16[512,1024]{1,0:T(8,128)(2,1)S(1)}, bf16[512,1024]{1,0:T(8,128)(2,1)S(1)}, u32[]{:S(2)}, u32[]{:S(2)}) %collective-permute-start.1) | collective-permute-done | bytes 1048608 | tf_op jit(solution)/shard_map/ppermute | solution.py:32
  42.8 1.5 %collective-permute-start.14 = (bf16[2,128,128]{2,1,0:T(8,128)(2,1)S(1)}, bf16[2,128,128]{2,1,0:T(8,128)(2,1)S(1)}, u32[]{:S(2)}, u32[]{:S(2)}) collective-permute-start(bf16[2,128,128]{2,1,0:T(8,128)(2,1)S(1)} %get-tuple-element.55), channel_id=1, source_target_pairs={{0,24},{8,0},{16,8},{24,16},{1,25},{9,1},{17,9},{25,17},{2,26},{10... | collective-permute-start | bytes 196616 | tf_op jit(solution)/shard_map/ppermute | solution.py:32
  44.3 1.6 %collective-permute-start.15 = (bf16[2,128,128]{2,1,0:T(8,128)(2,1)S(1)}, bf16[2,128,128]{2,1,0:T(8,128)(2,1)S(1)}, u32[]{:S(2)}, u32[]{:S(2)}) collective-permute-start(bf16[2,128,128]{2,1,0:T(8,128)(2,1)S(1)} %fusion.12.rest_0_), channel_id=1, source_target_pairs={{0,16},{8,24},{16,0},{24,8},{1,17},{9,25},{17,1},{25,9},{2,18},{10... | collective-permute-start | bytes 196616 | tf_op jit(solution)/shard_map/ppermute | solution.py:32
  47.4 1.6 %collective-permute-start.7 = (bf16[256,1024]{1,0:T(8,128)(2,1)S(1)}, bf16[256,1024]{1,0:T(8,128)(2,1)S(1)}, u32[]{:S(2)}, u32[]{:S(2)}) collective-permute-start(bf16[256,1024]{1,0:T(8,128)(2,1)S(1)} %slice.80), channel_id=1, source_target_pairs={{0,3},{1,0},{2,1},{3,2},{4,7},{5,4},{6,5},{7,6},{8,11},{9,8},{10,9... | collective-permute-start | bytes 1572872 | tf_op jit(solution)/shard_map/ppermute | solution.py:32
  48.9 3.4 %begin_values.1.total_ref = f32[512,1024]{1,0:T(8,128)S(1)} custom-call(s32[3]{0:T(128)S(1)} %pad_add_fusion.place, bf16[512,1024]{1,0:T(8,128)(2,1)S(1)} %turn_features.1.own.rest_0_, bf16[512,1024]{1,0:T(8,128)(2,1)S(1)} %collective-permute-done.1.left.rest_1_, bf16[512,1024]{1,0:T(8,128)(2,1)S(1)} %collective-permute-done.2.right.rest_2_, ...), custom_call_target="tpu_custom_call" | custom-call | flops 4024999936 | bytes 1000 | tf_op jit(solution)/shard_map/begin_values/pallas_call | solution.py:252
  52.5 2.1 %collective-permute-start.17 = (f32[2,128,128]{2,1,0:T(8,128)S(1)}, f32[2,128,128]{2,1,0:T(8,128)S(1)}, u32[]{:S(2)}, u32[]{:S(2)}) collective-permute-start(f32[2,128,128]{2,1,0:T(8,128)S(1)} %get-tuple-element.51), channel_id=1, source_target_pairs={{0,4},{4,0},{1,5},{5,1},{2,6},{6,2},{3,7},{7,3},{8,12},{12,8},{9,1... | collective-permute-start | bytes 393224 | tf_op jit(solution)/shard_map/ppermute | solution.py:36
  54.6 5.0 %collective-permute-done.6.fu.rest_3_ = bf16[256,1024]{1,0:T(8,128)(2,1)S(1)} collective-permute-done((bf16[256,1024]{1,0:T(8,128)(2,1)S(1)}, bf16[256,1024]{1,0:T(8,128)(2,1)S(1)}, u32[]{:S(2)}, u32[]{:S(2)}) %collective-permute-start.6) | collective-permute-done | bytes 524320 | tf_op jit(solution)/shard_map/ppermute | solution.py:32
  59.5 4.1 %end_values.1 = (bf16[512,1024]{1,0:T(8,128)(2,1)}, f32[4,128,128]{2,1,0:T(8,128)S(1)}) custom-call(s32[3]{0:T(128)S(1)} %pad_add_fusion.place, f32[512,1024]{1,0:T(8,128)S(1)} %begin_values.1.total_ref, bf16[256,1024]{1,0:T(8,128)(2,1)S(1)} %collective-permute-done.6.fu.rest_3_, bf16[256,1024]{1,0:T(8,128)(2,1)S(1)} %collective-permute-done.7.fl.rest_4_, ...), custom_call_target="tpu_custom_call" | custom-call | flops 4255000064 | bytes 1000 | tf_op jit(solution)/shard_map/end_values/pallas_call | solution.py:274
  63.6 2.3 %collective-permute-start.8 = (f32[4,128,128]{2,1,0:T(8,128)S(1)}, f32[4,128,128]{2,1,0:T(8,128)S(1)}, u32[]{:S(2)}, u32[]{:S(2)}) collective-permute-start(f32[4,128,128]{2,1,0:T(8,128)S(1)} %get-tuple-element.39), channel_id=1, source_target_pairs={{0,4},{4,0},{1,5},{5,1},{2,6},{6,2},{3,7},{7,3},{8,12},{12,8},{9,1... | collective-permute-start | bytes 786440 | tf_op jit(solution)/shard_map/ppermute | solution.py:36
  67.1 5.6 %weight_terms.1 = (f32[4,8,32,512]{3,2,1,0:T(8,128)}, f32[4,8,32,512]{3,2,1,0:T(8,128)}) custom-call(s32[3]{0:T(128)S(1)} %pad_add_fusion.place, f32[1024,256]{1,0:T(8,128)S(1)} %get-tuple-element.30.near_a, f32[1024,256]{1,0:T(8,128)S(1)} %get-tuple-element.32.near_b, bf16[1024,512]{1,0:T(8,128)(2,1)S(1)} %copy-done.4, ...), custom_call_target="tpu_custom_call" | custom-call | flops 5750000128 | bytes 1000 | tf_op jit(solution)/shard_map/weight_terms/pallas_call | solution.py:348
  73.0 1.4 %collective-permute-start.10 = (bf16[2,128,128]{2,1,0:T(8,128)(2,1)S(1)}, bf16[2,128,128]{2,1,0:T(8,128)(2,1)S(1)}, u32[]{:S(2)}, u32[]{:S(2)}) collective-permute-start(bf16[2,128,128]{2,1,0:T(8,128)(2,1)S(1)} %fusion.20.rest_5_), channel_id=1, source_target_pairs={{0,16},{8,24},{16,0},{24,8},{1,17},{9,25},{17,1},{25,9},{2,18},{10... | collective-permute-start | bytes 196616 | tf_op jit(solution)/shard_map/ppermute | solution.py:32
  75.9 2.1 %collective-permute-done.10 = bf16[2,128,128]{2,1,0:T(8,128)(2,1)S(1)} collective-permute-done((bf16[2,128,128]{2,1,0:T(8,128)(2,1)S(1)}, bf16[2,128,128]{2,1,0:T(8,128)(2,1)S(1)}, u32[]{:S(2)}, u32[]{:S(2)}) %collective-permute-start.10) | collective-permute-done | bytes 65568 | tf_op jit(solution)/shard_map/ppermute | solution.py:32
  78.1 2.0 %collective-permute-done.9 = bf16[2,128,128]{2,1,0:T(8,128)(2,1)S(1)} collective-permute-done((bf16[2,128,128]{2,1,0:T(8,128)(2,1)S(1)}, bf16[2,128,128]{2,1,0:T(8,128)(2,1)S(1)}, u32[]{:S(2)}, u32[]{:S(2)}) %collective-permute-start.9) | collective-permute-done | bytes 65568 | tf_op jit(solution)/shard_map/ppermute | solution.py:32
  80.2 2.0 %collective-permute-start.12 = (bf16[2,2,128,128]{3,2,1,0:T(8,128)(2,1)S(1)}, bf16[2,2,128,128]{3,2,1,0:T(8,128)(2,1)S(1)}, u32[]{:S(2)}, u32[]{:S(2)}) collective-permute-start(bf16[2,2,128,128]{3,2,1,0:T(8,128)(2,1)S(1)} %pad_maximum_fusion.4), channel_id=1, source_target_pairs={{0,4},{4,0},{1,5},{5,1},{2,6},{6,2},{3,7},{7,3},{8,12},{12,8},{9,1... | collective-permute-start | bytes 393224 | tf_op jit(solution)/shard_map/ppermute | solution.py:36
  82.2 3.0 %pair_sums.1 = (f32[8,32,512]{2,1,0:T(8,128)S(1)}, bf16[8,32,512]{2,1,0:T(8,128)(2,1)S(1)}, bf16[8,32,512]{2,1,0:T(8,128)(2,1)S(1)}, bf16[8,32,512]{2,1,0:T(8,128)(2,1)S(1)}) custom-call(s32[3]{0:T(128)S(1)} %pad_add_fusion.place, f32[4,8,32,512]{3,2,1,0:T(8,128)} %get-tuple-element.41.kept_u.kept_l, f32[4,8,32,512]{3,2,1,0:T(8,128)} %get-tuple-element.41.kept_u.kept_l, ...), custom_call_target="tpu_custom_call" | custom-call | flops 1264999936 | bytes 1000 | tf_op jit(solution)/shard_map/pair_sums/pallas_call | solution.py:393
  85.7 2.4 %collective-permute-start.23 = (bf16[8,32,512]{2,1,0:T(8,128)(2,1)S(1)}, bf16[8,32,512]{2,1,0:T(8,128)(2,1)S(1)}, u32[]{:S(2)}, u32[]{:S(2)}) collective-permute-start(bf16[8,32,512]{2,1,0:T(8,128)(2,1)S(1)} %get-tuple-element.47), channel_id=1, source_target_pairs={{0,24},{8,0},{16,8},{24,16},{1,25},{9,1},{17,9},{25,17},{2,26},{10... | collective-permute-start | bytes 786440 | tf_op jit(solution)/shard_map/ppermute | solution.py:32
  88.1 7.2 %begin_attended.1.total_u.total_l = f32[4,128,1024]{2,1,0:T(8,128)} custom-call(s32[3]{0:T(128)S(1)} %pad_add_fusion.place, bf16[4,128,1024]{2,1,0:T(8,128)(2,1)} %get-tuple-element.26.turned_ref, bf16[17,4,1024]{2,1,0:T(4,128)(2,1)S(1)} %copy-done, bf16[512,1024]{1,0:T(8,128)(2,1)} %get-tuple-element.34.v_ref, ...), custom_call_target="tpu_custom_call" | custom-call | flops 345000000 | bytes 1000 | tf_op jit(solution)/shard_map/begin_attended/pallas_call | solution.py:463
  95.3 4.5 %collective-permute-done.20 = bf16[8,32,512]{2,1,0:T(8,128)(2,1)S(1)} collective-permute-done((bf16[8,32,512]{2,1,0:T(8,128)(2,1)S(1)}, bf16[8,32,512]{2,1,0:T(8,128)(2,1)S(1)}, u32[]{:S(2)}, u32[]{:S(2)}) %collective-permute-start.20) | collective-permute-done | bytes 262176 | tf_op jit(solution)/shard_map/ppermute | solution.py:32
  99.9 3.2 %collective-permute-start.21 = (bf16[2,128,128]{2,1,0:T(8,128)(2,1)S(1)}, bf16[2,128,128]{2,1,0:T(8,128)(2,1)S(1)}, u32[]{:S(2)}, u32[]{:S(2)}) collective-permute-start(bf16[2,128,128]{2,1,0:T(8,128)(2,1)S(1)} %fusion.13), channel_id=1, source_target_pairs={{0,64},{32,96},{64,0},{96,32},{128,192},{160,224},{192,128},{224,1... | collective-permute-start | bytes 196616 | tf_op jit(solution)/shard_map/ppermute | solution.py:36
  104.0 5.9 %all-to-all-start = ((bf16[8,32,512]{2,1,0:T(8,128)(2,1)}), bf16[8,32,512]{2,1,0:T(8,128)(2,1)S(1)}, u32[]{:S(2)}, u32[]{:S(2)}) async-start(bf16[8,32,512]{2,1,0:T(8,128)(2,1)} %add_convert_fusion), calls=%async_computation | async-start | bytes 524288 | tf_op jit(solution)/shard_map/all_to_all | solution.py:603
  109.9 7.3 %collective-permute-start.22 = (bf16[2,128,128]{2,1,0:T(8,128)(2,1)S(1)}, bf16[2,128,128]{2,1,0:T(8,128)(2,1)S(1)}, u32[]{:S(2)}, u32[]{:S(2)}) collective-permute-start(bf16[2,128,128]{2,1,0:T(8,128)(2,1)S(1)} %get-tuple-element.60), channel_id=1, source_target_pairs={{0,128},{32,160},{64,192},{96,224},{1,129},{33,161},{65,193},{97,2... | collective-permute-start | bytes 196616 | tf_op jit(solution)/shard_map/ppermute | solution.py:602
  119.6 3.8 %collective-permute-start.25 = (bf16[3,2,128,128]{3,2,1,0:T(8,128)(2,1)S(1)}, bf16[3,2,128,128]{3,2,1,0:T(8,128)(2,1)S(1)}, u32[]{:S(2)}, u32[]{:S(2)}) collective-permute-start(bf16[3,2,128,128]{3,2,1,0:T(8,128)(2,1)S(1)} %pad_maximum_fusion.2), channel_id=1, source_target_pairs={{0,4},{4,0},{1,5},{5,1},{2,6},{6,2},{3,7},{7,3},{8,12},{12,8},{9,1... | collective-permute-start | bytes 589832 | tf_op jit(solution)/shard_map/ppermute | solution.py:36
  124.5 5.1 %end_attended.1 = bf16[1024,512]{1,0:T(8,128)(2,1)} custom-call(s32[3]{0:T(128)S(1)} %pad_add_fusion.place, bf16[4,128,1024]{2,1,0:T(8,128)(2,1)} %get-tuple-element.26.turned_ref, bf16[17,4,1024]{2,1,0:T(4,128)(2,1)S(1)} %copy-done, f32[4,128,1024]{2,1,0:T(8,128)} %begin_attended.1.total_u.total_l, f32[4,128,1024]{2,1,0:T(8,128)} %begin_attended.1.total_u.total_l, ...), custom_call_target="tpu_custom_call" | custom-call | flops 345000000 | bytes 1000 | tf_op jit(solution)/shard_map/end_attended/pallas_call | solution.py:502
  (66 shorter events, 16.0 us)
Async XLA Ops:
  6.6 7.7 %copy-start.2 = (bf16[1024,512]{1,0:T(8,128)(2,1)S(1)}, bf16[1024,512]{1,0:T(8,128)(2,1)}, u32[]{:S(2)}) copy-start(bf16[1024,512]{1,0:T(8,128)(2,1)} %in_ref.2) | copy-start | bytes 3145732
  6.6 5.0 %collective-permute-start = (f32[5,2,128,128]{3,2,1,0:T(8,128)S(1)}, f32[5,2,128,128]{3,2,1,0:T(8,128)S(1)}, u32[]{:S(2)}, u32[]{:S(2)}) collective-permute-start(f32[5,2,128,128]{3,2,1,0:T(8,128)S(1)} %get-tuple-element.28), channel_id=1, source_target_pairs={{0,4},{4,0},{1,5},{5,1},{2,6},{6,2},{3,7},{7,3},{8,12},{12,8},{9,1... | collective-permute-start | bytes 1966088 | tf_op jit(solution)/shard_map/ppermute | solution.py:36
  11.7 6.2 %collective-permute-start.3 = (bf16[3,2,128,128]{3,2,1,0:T(8,128)(2,1)S(1)}, bf16[3,2,128,128]{3,2,1,0:T(8,128)(2,1)S(1)}, u32[]{:S(2)}, u32[]{:S(2)}) collective-permute-start(bf16[3,2,128,128]{3,2,1,0:T(8,128)(2,1)S(1)} %slice.139.rest_0_), channel_id=1, source_target_pairs={{0,32},{32,0},{64,96},{96,64},{128,160},{160,128},{192,224},{224,1... | collective-permute-start | bytes 589832 | tf_op jit(solution)/shard_map/ppermute | solution.py:36
  11.8 35.6 %collective-permute-start.16 = (f32[4,128,128]{2,1,0:T(8,128)S(1)}, f32[4,128,128]{2,1,0:T(8,128)S(1)}, u32[]{:S(2)}, u32[]{:S(2)}) collective-permute-start(f32[4,128,128]{2,1,0:T(8,128)S(1)} %get-tuple-element.40), channel_id=1, source_target_pairs={{4,0},{5,1},{6,2},{7,3},{12,8},{13,9},{14,10},{15,11},{20,16},{21,... | collective-permute-start | bytes 786440 | tf_op jit(solution)/shard_map/ppermute | solution.py:553
  14.3 6.7 %copy-start = (bf16[17,4,1024]{2,1,0:T(4,128)(2,1)S(1)}, bf16[17,4,1024]{2,1,0:T(4,128)(2,1)}, u32[]{:S(2)}) copy-start(bf16[17,4,1024]{2,1,0:T(4,128)(2,1)} %lw_ref.9) | copy-start | bytes 417796
  14.3 6.7 %copy-start.3 = (bf16[1024,512]{1,0:T(8,128)(2,1)S(1)}, bf16[1024,512]{1,0:T(8,128)(2,1)}, u32[]{:S(2)}) copy-start(bf16[1024,512]{1,0:T(8,128)(2,1)} %g_ref.3) | copy-start | bytes 3145732
  14.3 6.7 %copy-start.4 = (bf16[1024,512]{1,0:T(8,128)(2,1)S(1)}, bf16[1024,512]{1,0:T(8,128)(2,1)}, u32[]{:S(2)}) copy-start(bf16[1024,512]{1,0:T(8,128)(2,1)} %k_ref.7) | copy-start | bytes 3145732
  14.9 26.1 %collective-permute-start.1 = (bf16[512,1024]{1,0:T(8,128)(2,1)S(1)}, bf16[512,1024]{1,0:T(8,128)(2,1)S(1)}, u32[]{:S(2)}, u32[]{:S(2)}) collective-permute-start(bf16[512,1024]{1,0:T(8,128)(2,1)S(1)} %turn_features.1.own.rest_0_), channel_id=1, source_target_pairs={{0,1},{1,2},{2,3},{3,0},{4,5},{5,6},{6,7},{7,4},{8,9},{9,10},{10,1... | collective-permute-start | bytes 3145736 | tf_op jit(solution)/shard_map/ppermute | solution.py:32
  16.3 25.1 %collective-permute-start.2 = (bf16[512,1024]{1,0:T(8,128)(2,1)S(1)}, bf16[512,1024]{1,0:T(8,128)(2,1)S(1)}, u32[]{:S(2)}, u32[]{:S(2)}) collective-permute-start(bf16[512,1024]{1,0:T(8,128)(2,1)S(1)} %turn_features.1.own.rest_0_), channel_id=1, source_target_pairs={{0,3},{1,0},{2,1},{3,2},{4,7},{5,4},{6,5},{7,6},{8,11},{9,8},{10,9... | collective-permute-start | bytes 3145736 | tf_op jit(solution)/shard_map/ppermute | solution.py:32
  17.9 9.3 %collective-permute-start.4 = (bf16[2,2,128,128]{3,2,1,0:T(8,128)(2,1)S(1)}, bf16[2,2,128,128]{3,2,1,0:T(8,128)(2,1)S(1)}, u32[]{:S(2)}, u32[]{:S(2)}) collective-permute-start(bf16[2,2,128,128]{3,2,1,0:T(8,128)(2,1)S(1)} %pad_maximum_fusion.3.rest_0_), channel_id=1, source_target_pairs={{0,64},{32,96},{64,0},{96,32},{128,192},{160,224},{192,128},{224,1... | collective-permute-start | bytes 393224 | tf_op jit(solution)/shard_map/ppermute | solution.py:36
  21.0 5.2 %copy-start.1 = (bf16[2048,512]{1,0:T(8,128)(2,1)S(1)}, bf16[2048,512]{1,0:T(8,128)(2,1)}, u32[]{:S(2)}) copy-start(bf16[2048,512]{1,0:T(8,128)(2,1)} %in_ref.3) | copy-start | bytes 6291460
  27.3 8.9 %collective-permute-start.5 = (bf16[2,128,128]{2,1,0:T(8,128)(2,1)S(1)}, bf16[2,128,128]{2,1,0:T(8,128)(2,1)S(1)}, u32[]{:S(2)}, u32[]{:S(2)}) collective-permute-start(bf16[2,128,128]{2,1,0:T(8,128)(2,1)S(1)} %fusion.15.rest_0_), channel_id=1, source_target_pairs={{128,0},{160,32},{192,64},{224,96},{129,1},{161,33},{193,65},{225,... | collective-permute-start | bytes 196616 | tf_op jit(solution)/shard_map/ppermute | solution.py:558
  41.5 10.9 %collective-permute-start.13 = (bf16[2,128,128]{2,1,0:T(8,128)(2,1)S(1)}, bf16[2,128,128]{2,1,0:T(8,128)(2,1)S(1)}, u32[]{:S(2)}, u32[]{:S(2)}) collective-permute-start(bf16[2,128,128]{2,1,0:T(8,128)(2,1)S(1)} %get-tuple-element.54), channel_id=1, source_target_pairs={{0,8},{8,16},{16,24},{24,0},{1,9},{9,17},{17,25},{25,1},{2,10},{10... | collective-permute-start | bytes 196616 | tf_op jit(solution)/shard_map/ppermute | solution.py:32
  42.8 9.7 %collective-permute-start.14 = (bf16[2,128,128]{2,1,0:T(8,128)(2,1)S(1)}, bf16[2,128,128]{2,1,0:T(8,128)(2,1)S(1)}, u32[]{:S(2)}, u32[]{:S(2)}) collective-permute-start(bf16[2,128,128]{2,1,0:T(8,128)(2,1)S(1)} %get-tuple-element.55), channel_id=1, source_target_pairs={{0,24},{8,0},{16,8},{24,16},{1,25},{9,1},{17,9},{25,17},{2,26},{10... | collective-permute-start | bytes 196616 | tf_op jit(solution)/shard_map/ppermute | solution.py:32
  44.3 8.1 %collective-permute-start.15 = (bf16[2,128,128]{2,1,0:T(8,128)(2,1)S(1)}, bf16[2,128,128]{2,1,0:T(8,128)(2,1)S(1)}, u32[]{:S(2)}, u32[]{:S(2)}) collective-permute-start(bf16[2,128,128]{2,1,0:T(8,128)(2,1)S(1)} %fusion.12.rest_0_), channel_id=1, source_target_pairs={{0,16},{8,24},{16,0},{24,8},{1,17},{9,25},{17,1},{25,9},{2,18},{10... | collective-permute-start | bytes 196616 | tf_op jit(solution)/shard_map/ppermute | solution.py:32
  45.9 13.6 %collective-permute-start.6 = (bf16[256,1024]{1,0:T(8,128)(2,1)S(1)}, bf16[256,1024]{1,0:T(8,128)(2,1)S(1)}, u32[]{:S(2)}, u32[]{:S(2)}) collective-permute-start(bf16[256,1024]{1,0:T(8,128)(2,1)S(1)} %slice.79), channel_id=1, source_target_pairs={{0,1},{1,2},{2,3},{3,0},{4,5},{5,6},{6,7},{7,4},{8,9},{9,10},{10,1... | collective-permute-start | bytes 1572872 | tf_op jit(solution)/shard_map/ppermute | solution.py:32
  47.4 12.2 %collective-permute-start.7 = (bf16[256,1024]{1,0:T(8,128)(2,1)S(1)}, bf16[256,1024]{1,0:T(8,128)(2,1)S(1)}, u32[]{:S(2)}, u32[]{:S(2)}) collective-permute-start(bf16[256,1024]{1,0:T(8,128)(2,1)S(1)} %slice.80), channel_id=1, source_target_pairs={{0,3},{1,0},{2,1},{3,2},{4,7},{5,4},{6,5},{7,6},{8,11},{9,8},{10,9... | collective-permute-start | bytes 1572872 | tf_op jit(solution)/shard_map/ppermute | solution.py:32
  52.5 13.4 %collective-permute-start.17 = (f32[2,128,128]{2,1,0:T(8,128)S(1)}, f32[2,128,128]{2,1,0:T(8,128)S(1)}, u32[]{:S(2)}, u32[]{:S(2)}) collective-permute-start(f32[2,128,128]{2,1,0:T(8,128)S(1)} %get-tuple-element.51), channel_id=1, source_target_pairs={{0,4},{4,0},{1,5},{5,1},{2,6},{6,2},{3,7},{7,3},{8,12},{12,8},{9,1... | collective-permute-start | bytes 393224 | tf_op jit(solution)/shard_map/ppermute | solution.py:36
  63.6 3.4 %collective-permute-start.8 = (f32[4,128,128]{2,1,0:T(8,128)S(1)}, f32[4,128,128]{2,1,0:T(8,128)S(1)}, u32[]{:S(2)}, u32[]{:S(2)}) collective-permute-start(f32[4,128,128]{2,1,0:T(8,128)S(1)} %get-tuple-element.39), channel_id=1, source_target_pairs={{0,4},{4,0},{1,5},{5,1},{2,6},{6,2},{3,7},{7,3},{8,12},{12,8},{9,1... | collective-permute-start | bytes 786440 | tf_op jit(solution)/shard_map/ppermute | solution.py:36
  72.7 9.5 %collective-permute-start.18 = (f32[4,8,32,512]{3,2,1,0:T(8,128)}, f32[4,8,32,512]{3,2,1,0:T(8,128)S(1)}, u32[]{:S(2)}, u32[]{:S(2)}) collective-permute-start(f32[4,8,32,512]{3,2,1,0:T(8,128)} %get-tuple-element.42), channel_id=1, source_target_pairs={{0,4},{4,0},{1,5},{5,1},{2,6},{6,2},{3,7},{7,3},{8,12},{12,8},{9,1... | collective-permute-start | bytes 6291464 | tf_op jit(solution)/shard_map/ppermute | solution.py:36
  73.0 5.0 %collective-permute-start.10 = (bf16[2,128,128]{2,1,0:T(8,128)(2,1)S(1)}, bf16[2,128,128]{2,1,0:T(8,128)(2,1)S(1)}, u32[]{:S(2)}, u32[]{:S(2)}) collective-permute-start(bf16[2,128,128]{2,1,0:T(8,128)(2,1)S(1)} %fusion.20.rest_5_), channel_id=1, source_target_pairs={{0,16},{8,24},{16,0},{24,8},{1,17},{9,25},{17,1},{25,9},{2,18},{10... | collective-permute-start | bytes 196616 | tf_op jit(solution)/shard_map/ppermute | solution.py:32
  74.5 3.6 %collective-permute-start.11 = (bf16[2,128,128]{2,1,0:T(8,128)(2,1)S(1)}, bf16[2,128,128]{2,1,0:T(8,128)(2,1)S(1)}, u32[]{:S(2)}, u32[]{:S(2)}) collective-permute-start(bf16[2,128,128]{2,1,0:T(8,128)(2,1)S(1)} %fusion.20.rest_5_), channel_id=1, source_target_pairs={{0,24},{8,0},{16,8},{24,16},{1,25},{9,1},{17,9},{25,17},{2,26},{10... | collective-permute-start | bytes 196616 | tf_op jit(solution)/shard_map/ppermute | solution.py:32
  75.7 4.3 %collective-permute-start.9 = (bf16[2,128,128]{2,1,0:T(8,128)(2,1)S(1)}, bf16[2,128,128]{2,1,0:T(8,128)(2,1)S(1)}, u32[]{:S(2)}, u32[]{:S(2)}) collective-permute-start(bf16[2,128,128]{2,1,0:T(8,128)(2,1)S(1)} %fusion.20.rest_5_), channel_id=1, source_target_pairs={{0,8},{8,16},{16,24},{24,0},{1,9},{9,17},{17,25},{25,1},{2,10},{10... | collective-permute-start | bytes 196616 | tf_op jit(solution)/shard_map/ppermute | solution.py:32
  80.2 5.1 %collective-permute-start.12 = (bf16[2,2,128,128]{3,2,1,0:T(8,128)(2,1)S(1)}, bf16[2,2,128,128]{3,2,1,0:T(8,128)(2,1)S(1)}, u32[]{:S(2)}, u32[]{:S(2)}) collective-permute-start(bf16[2,2,128,128]{3,2,1,0:T(8,128)(2,1)S(1)} %pad_maximum_fusion.4), channel_id=1, source_target_pairs={{0,4},{4,0},{1,5},{5,1},{2,6},{6,2},{3,7},{7,3},{8,12},{12,8},{9,1... | collective-permute-start | bytes 393224 | tf_op jit(solution)/shard_map/ppermute | solution.py:36
  85.2 10.1 %collective-permute-start.19 = (bf16[2,128,128]{2,1,0:T(8,128)(2,1)S(1)}, bf16[2,128,128]{2,1,0:T(8,128)(2,1)S(1)}, u32[]{:S(2)}, u32[]{:S(2)}) collective-permute-start(bf16[2,128,128]{2,1,0:T(8,128)(2,1)S(1)} %get-tuple-element.44.rest_6_), channel_id=1, source_target_pairs={{0,32},{32,0},{64,96},{96,64},{128,160},{160,128},{192,224},{224,1... | collective-permute-start | bytes 196616 | tf_op jit(solution)/shard_map/ppermute | solution.py:36
  85.3 14.5 %collective-permute-start.20 = (bf16[8,32,512]{2,1,0:T(8,128)(2,1)S(1)}, bf16[8,32,512]{2,1,0:T(8,128)(2,1)S(1)}, u32[]{:S(2)}, u32[]{:S(2)}) collective-permute-start(bf16[8,32,512]{2,1,0:T(8,128)(2,1)S(1)} %get-tuple-element.45), channel_id=1, source_target_pairs={{0,8},{8,16},{16,24},{24,0},{1,9},{9,17},{17,25},{25,1},{2,10},{10... | collective-permute-start | bytes 786440 | tf_op jit(solution)/shard_map/ppermute | solution.py:32
  85.7 17.4 %collective-permute-start.23 = (bf16[8,32,512]{2,1,0:T(8,128)(2,1)S(1)}, bf16[8,32,512]{2,1,0:T(8,128)(2,1)S(1)}, u32[]{:S(2)}, u32[]{:S(2)}) collective-permute-start(bf16[8,32,512]{2,1,0:T(8,128)(2,1)S(1)} %get-tuple-element.47), channel_id=1, source_target_pairs={{0,24},{8,0},{16,8},{24,16},{1,25},{9,1},{17,9},{25,17},{2,26},{10... | collective-permute-start | bytes 786440 | tf_op jit(solution)/shard_map/ppermute | solution.py:32
  88.1 15.0 %collective-permute-start.24 = (bf16[8,32,512]{2,1,0:T(8,128)(2,1)S(1)}, bf16[8,32,512]{2,1,0:T(8,128)(2,1)S(1)}, u32[]{:S(2)}, u32[]{:S(2)}) collective-permute-start(bf16[8,32,512]{2,1,0:T(8,128)(2,1)S(1)} %get-tuple-element.48), channel_id=1, source_target_pairs={{0,16},{8,24},{16,0},{24,8},{1,17},{9,25},{17,1},{25,9},{2,18},{10... | collective-permute-start | bytes 786440 | tf_op jit(solution)/shard_map/ppermute | solution.py:32
  99.9 10.0 %collective-permute-start.21 = (bf16[2,128,128]{2,1,0:T(8,128)(2,1)S(1)}, bf16[2,128,128]{2,1,0:T(8,128)(2,1)S(1)}, u32[]{:S(2)}, u32[]{:S(2)}) collective-permute-start(bf16[2,128,128]{2,1,0:T(8,128)(2,1)S(1)} %fusion.13), channel_id=1, source_target_pairs={{0,64},{32,96},{64,0},{96,32},{128,192},{160,224},{192,128},{224,1... | collective-permute-start | bytes 196616 | tf_op jit(solution)/shard_map/ppermute | solution.py:36
  104.0 15.7 %all-to-all-start = ((bf16[8,32,512]{2,1,0:T(8,128)(2,1)}), bf16[8,32,512]{2,1,0:T(8,128)(2,1)S(1)}, u32[]{:S(2)}, u32[]{:S(2)}) async-start(bf16[8,32,512]{2,1,0:T(8,128)(2,1)} %add_convert_fusion), calls=%async_computation | async-start | bytes 524288 | tf_op jit(solution)/shard_map/all_to_all | solution.py:603
  109.9 8.6 %collective-permute-start.22 = (bf16[2,128,128]{2,1,0:T(8,128)(2,1)S(1)}, bf16[2,128,128]{2,1,0:T(8,128)(2,1)S(1)}, u32[]{:S(2)}, u32[]{:S(2)}) collective-permute-start(bf16[2,128,128]{2,1,0:T(8,128)(2,1)S(1)} %get-tuple-element.60), channel_id=1, source_target_pairs={{0,128},{32,160},{64,192},{96,224},{1,129},{33,161},{65,193},{97,2... | collective-permute-start | bytes 196616 | tf_op jit(solution)/shard_map/ppermute | solution.py:602
  119.6 4.9 %collective-permute-start.25 = (bf16[3,2,128,128]{3,2,1,0:T(8,128)(2,1)S(1)}, bf16[3,2,128,128]{3,2,1,0:T(8,128)(2,1)S(1)}, u32[]{:S(2)}, u32[]{:S(2)}) collective-permute-start(bf16[3,2,128,128]{3,2,1,0:T(8,128)(2,1)S(1)} %pad_maximum_fusion.2), channel_id=1, source_target_pairs={{0,4},{4,0},{1,5},{5,1},{2,6},{6,2},{3,7},{7,3},{8,12},{12,8},{9,1... | collective-permute-start | bytes 589832 | tf_op jit(solution)/shard_map/ppermute | solution.py:36

commit v5 on v2

--- a/solution.py
+++ b/solution.py
@@ -602,7 +602,7 @@
     level_5 = lax.ppermute(message, "z", [(i, i + 4) for i in range(4)])
     rows = lax.all_to_all(rows, "z", 0, 0, tiled=True)
     weight_grad = rows.astype(F32).sum(axis=0)
-    upper_levels = behind(jnp.stack([level_3.astype(BF), level_4.astype(BF), level_5]), rows)
+    upper_levels = jnp.stack([level_3.astype(BF), level_4.astype(BF), level_5])
     attended = end_attended(place, turned_queries, level_weights, begun, both(upper_levels))
     return attended, weight_grad
 

time: 132 us -> 127 us (0.962)
  waiting for transfers between devices: 37 us -> 32.5 us
    ppermute x13, waiting for transfers between devices: 23 us -> 15.6 us  [shift(): lax.ppermute(value, axis, [(i, (i + distance) % size) for i in range(size)])]
    all_to_all x1, starting transfers between devices: 7.58 us -> 3.41 us  [local(): rows = lax.all_to_all(rows, 'z', 0, 0, tiled=True)]
    all_to_all x1, waiting for transfers between devices: 0.01 us -> 3.66 us  [local(): rows = lax.all_to_all(rows, 'z', 0, 0, tiled=True)]
    ppermute x13, starting transfers between devices: 18.3 us -> 21.8 us  [shift(): lax.ppermute(value, axis, [(i, (i + distance) % size) for i in range(size)])]
    ppermute x1, waiting for transfers between devices: 1.88 us -> 0.01 us  [local(): level_5 = lax.ppermute(message, 'z', [(i, i + 4) for i in range(4)])]
  transfers between devices with their start and end apart: 27 -> 27, of which waited for: 16 -> 14; matrix products, arithmetic and copies ran while one was open for 2% -> 1% of each run, Pallas kernels for 17% -> 22%
where the time goes in v5:
time: 127 us; the launch traced here: 126 us
  Pallas kernels  46.2 us (36%)
  starting transfers between devices  44.3 us (35%)
  waiting for transfers between devices  32.5 us (26%)
  other arithmetic  2.28 us (2%)
    ppermute x13, starting transfers between devices, shift(): lax.ppermute(value, axis, [(i, (i + distance) % size) for i in range(size)])  21.8 us
    ppermute x13, waiting for transfers between devices, shift(): lax.ppermute(value, axis, [(i, (i + distance) % size) for i in range(size)])  15.6 us
    pallas_call x2, Pallas kernels, near(): pl.pallas_call(functools.partial(near_kernel, base), grid=(2,), in_specs=...  10.3 us
    ppermute x10, starting transfers between devices, swap(): return lax.ppermute(value, axis, [(i, i ^ distance) for i in range(size)])  10.1 us
    ppermute x10, waiting for transfers between devices, swap(): return lax.ppermute(value, axis, [(i, i ^ distance) for i in range(size)])  9.55 us
    pallas_call x1, Pallas kernels, begin_attended(): pl.pallas_call(begin_attended_kernel, grid_spec=pltpu.PrefetchScalarGridS...  7.21 us
    ppermute x1, starting transfers between devices, local(): level_5 = lax.ppermute(message, 'z', [(i, i + 4) for i in range(4)])  6.4 us
    pallas_call x1, Pallas kernels, query_states(): pl.pallas_call(query_state_kernel, grid_spec=pltpu.PrefetchScalarGridSpec...  5.85 us
  transfers between devices with their start and end apart: 27, of which 14 were waited for; matrix products, arithmetic and copies ran while one was open for 1% of the time, Pallas kernels for 22%

profile of v5, /device:TPU:30, one launch (start us, length us, event | category | flops | bytes accessed | tf_op | source)
XLA Modules:
  0.0 126.4 jit_solution(8872313338925611085)
XLA Ops:
  0.7 5.9 %query_states.1 = (f32[4,128,128]{2,1,0:T(8,128)S(1)}, f32[5,2,128,128]{3,2,1,0:T(8,128)S(1)}, f32[5,2,128,128]{3,2,1,0:T(8,128)S(1)}, bf16[4,128,1024]{2,1,0:T(8,128)(2,1)}) custom-call(s32[3]{0:T(128)S(1)} %pad_add_fusion.place, bf16[1024,512]{1,0:T(8,128)(2,1)} %q_l.1, bf16[1024,512]{1,0:T(8,128)(2,1)} %q_l.1, bf16[1024,512]{1,0:T(8,128)(2,1)} %g_ref.3, ...), custom_call_target="tpu_custom_call" | custom-call | flops 4600000000 | bytes 1000 | tf_op jit(solution)/shard_map/query_states/pallas_call | solution.py:122
  6.6 2.1 %collective-permute-done = f32[5,2,128,128]{3,2,1,0:T(8,128)S(1)} collective-permute-done((f32[5,2,128,128]{3,2,1,0:T(8,128)S(1)}, f32[5,2,128,128]{3,2,1,0:T(8,128)S(1)}, u32[]{:S(2)}, u32[]{:S(2)}) %collective-permute-start) | collective-permute-done | bytes 655392 | tf_op jit(solution)/shard_map/ppermute | solution.py:36
  8.8 2.0 %collective-permute-start.3 = (bf16[3,2,128,128]{3,2,1,0:T(8,128)(2,1)S(1)}, bf16[3,2,128,128]{3,2,1,0:T(8,128)(2,1)S(1)}, u32[]{:S(2)}, u32[]{:S(2)}) collective-permute-start(bf16[3,2,128,128]{3,2,1,0:T(8,128)(2,1)S(1)} %slice.139.rest_0_), channel_id=1, source_target_pairs={{0,32},{32,0},{64,96},{96,64},{128,160},{160,128},{192,224},{224,1... | collective-permute-start | bytes 589832 | tf_op jit(solution)/shard_map/ppermute | solution.py:36
  13.1 1.8 %collective-permute-start.2 = (bf16[512,1024]{1,0:T(8,128)(2,1)S(1)}, bf16[512,1024]{1,0:T(8,128)(2,1)S(1)}, u32[]{:S(2)}, u32[]{:S(2)}) collective-permute-start(bf16[512,1024]{1,0:T(8,128)(2,1)S(1)} %turn_features.1.own.rest_0_), channel_id=1, source_target_pairs={{0,3},{1,0},{2,1},{3,2},{4,7},{5,4},{6,5},{7,6},{8,11},{9,8},{10,9... | collective-permute-start | bytes 3145736 | tf_op jit(solution)/shard_map/ppermute | solution.py:32
  16.1 3.4 %collective-permute-start.4 = (bf16[2,2,128,128]{3,2,1,0:T(8,128)(2,1)S(1)}, bf16[2,2,128,128]{3,2,1,0:T(8,128)(2,1)S(1)}, u32[]{:S(2)}, u32[]{:S(2)}) collective-permute-start(bf16[2,2,128,128]{3,2,1,0:T(8,128)(2,1)S(1)} %pad_maximum_fusion.3.rest_0_), channel_id=1, source_target_pairs={{0,64},{32,96},{64,0},{96,32},{128,192},{160,224},{192,128},{224,1... | collective-permute-start | bytes 393224 | tf_op jit(solution)/shard_map/ppermute | solution.py:36
  19.4 5.2 %near.2 = (f32[1024,256]{1,0:T(8,128)S(1)}, bf16[2,5,256,256]{3,2,1,0:T(8,128)(2,1)}, bf16[2,5,256,256]{3,2,1,0:T(8,128)(2,1)}) custom-call(bf16[1024,512]{1,0:T(8,128)(2,1)S(1)} %copy-done.4, bf16[4,128,1024]{2,1,0:T(8,128)(2,1)} %get-tuple-element.27.turned_ref, bf16[1024,512]{1,0:T(8,128)(2,1)S(1)} %copy-done.3, bf16[17,4,1024]{2,1,0:T(4,128)(2,1)S(1)} %copy-done, ...), custom_call_target="tpu_custom_call" | custom-call | flops 3680000000 | bytes 1000 | tf_op jit(solution)/shard_map/near/pallas_call | solution.py:200
  26.9 5.1 %near.3 = (f32[1024,256]{1,0:T(8,128)S(1)}, bf16[2,5,256,256]{3,2,1,0:T(8,128)(2,1)}, bf16[2,5,256,256]{3,2,1,0:T(8,128)(2,1)}) custom-call(bf16[1024,512]{1,0:T(8,128)(2,1)S(1)} %copy-done.4, bf16[4,128,1024]{2,1,0:T(8,128)(2,1)} %get-tuple-element.27.turned_ref, bf16[1024,512]{1,0:T(8,128)(2,1)S(1)} %copy-done.3, bf16[17,4,1024]{2,1,0:T(4,128)(2,1)S(1)} %copy-done, ...), custom_call_target="tpu_custom_call" | custom-call | flops 3680000000 | bytes 1000 | tf_op jit(solution)/shard_map/near/pallas_call | solution.py:200
  32.1 3.6 %collective-permute-done.5 = bf16[2,128,128]{2,1,0:T(8,128)(2,1)S(1)} collective-permute-done((bf16[2,128,128]{2,1,0:T(8,128)(2,1)S(1)}, bf16[2,128,128]{2,1,0:T(8,128)(2,1)S(1)}, u32[]{:S(2)}, u32[]{:S(2)}) %collective-permute-start.5) | collective-permute-done | bytes 65568 | tf_op jit(solution)/shard_map/ppermute | solution.py:558
  35.7 3.1 %collective-permute-done.1.left.rest_1_ = bf16[512,1024]{1,0:T(8,128)(2,1)S(1)} collective-permute-done((bf16[512,1024]{1,0:T(8,128)(2,1)S(1)}, bf16[512,1024]{1,0:T(8,128)(2,1)S(1)}, u32[]{:S(2)}, u32[]{:S(2)}) %collective-permute-start.1) | collective-permute-done | bytes 1048608 | tf_op jit(solution)/shard_map/ppermute | solution.py:32
  38.8 1.6 %collective-permute-done.2.right.rest_2_ = bf16[512,1024]{1,0:T(8,128)(2,1)S(1)} collective-permute-done((bf16[512,1024]{1,0:T(8,128)(2,1)S(1)}, bf16[512,1024]{1,0:T(8,128)(2,1)S(1)}, u32[]{:S(2)}, u32[]{:S(2)}) %collective-permute-start.2) | collective-permute-done | bytes 1048608 | tf_op jit(solution)/shard_map/ppermute | solution.py:32
  41.0 1.5 %collective-permute-start.14 = (bf16[2,128,128]{2,1,0:T(8,128)(2,1)S(1)}, bf16[2,128,128]{2,1,0:T(8,128)(2,1)S(1)}, u32[]{:S(2)}, u32[]{:S(2)}) collective-permute-start(bf16[2,128,128]{2,1,0:T(8,128)(2,1)S(1)} %get-tuple-element.57), channel_id=1, source_target_pairs={{0,24},{8,0},{16,8},{24,16},{1,25},{9,1},{17,9},{25,17},{2,26},{10... | collective-permute-start | bytes 196616 | tf_op jit(solution)/shard_map/ppermute | solution.py:32
  42.6 1.5 %collective-permute-start.15 = (bf16[2,128,128]{2,1,0:T(8,128)(2,1)S(1)}, bf16[2,128,128]{2,1,0:T(8,128)(2,1)S(1)}, u32[]{:S(2)}, u32[]{:S(2)}) collective-permute-start(bf16[2,128,128]{2,1,0:T(8,128)(2,1)S(1)} %fusion.12.rest_0_), channel_id=1, source_target_pairs={{0,16},{8,24},{16,0},{24,8},{1,17},{9,25},{17,1},{25,9},{2,18},{10... | collective-permute-start | bytes 196616 | tf_op jit(solution)/shard_map/ppermute | solution.py:32
  44.5 2.0 %collective-permute-start.7 = (bf16[256,1024]{1,0:T(8,128)(2,1)S(1)}, bf16[256,1024]{1,0:T(8,128)(2,1)S(1)}, u32[]{:S(2)}, u32[]{:S(2)}) collective-permute-start(bf16[256,1024]{1,0:T(8,128)(2,1)S(1)} %slice.80), channel_id=1, source_target_pairs={{0,3},{1,0},{2,1},{3,2},{4,7},{5,4},{6,5},{7,6},{8,11},{9,8},{10,9... | collective-permute-start | bytes 1572872 | tf_op jit(solution)/shard_map/ppermute | solution.py:32
  46.5 3.4 %begin_values.1.total_ref = f32[512,1024]{1,0:T(8,128)S(1)} custom-call(s32[3]{0:T(128)S(1)} %pad_add_fusion.place, bf16[512,1024]{1,0:T(8,128)(2,1)S(1)} %turn_features.1.own.rest_0_, bf16[512,1024]{1,0:T(8,128)(2,1)S(1)} %collective-permute-done.1.left.rest_1_, bf16[512,1024]{1,0:T(8,128)(2,1)S(1)} %collective-permute-done.2.right.rest_2_, ...), custom_call_target="tpu_custom_call" | custom-call | flops 4024999936 | bytes 1000 | tf_op jit(solution)/shard_map/begin_values/pallas_call | solution.py:252
  50.0 7.2 %collective-permute-done.6.fu.rest_3_ = bf16[256,1024]{1,0:T(8,128)(2,1)S(1)} collective-permute-done((bf16[256,1024]{1,0:T(8,128)(2,1)S(1)}, bf16[256,1024]{1,0:T(8,128)(2,1)S(1)}, u32[]{:S(2)}, u32[]{:S(2)}) %collective-permute-start.6) | collective-permute-done | bytes 524320 | tf_op jit(solution)/shard_map/ppermute | solution.py:32
  57.3 1.5 %collective-permute-done.7.fl.rest_4_ = bf16[256,1024]{1,0:T(8,128)(2,1)S(1)} collective-permute-done((bf16[256,1024]{1,0:T(8,128)(2,1)S(1)}, bf16[256,1024]{1,0:T(8,128)(2,1)S(1)}, u32[]{:S(2)}, u32[]{:S(2)}) %collective-permute-start.7) | collective-permute-done | bytes 524320 | tf_op jit(solution)/shard_map/ppermute | solution.py:32
  58.8 4.1 %end_values.1 = (bf16[512,1024]{1,0:T(8,128)(2,1)}, f32[4,128,128]{2,1,0:T(8,128)S(1)}) custom-call(s32[3]{0:T(128)S(1)} %pad_add_fusion.place, f32[512,1024]{1,0:T(8,128)S(1)} %begin_values.1.total_ref, bf16[256,1024]{1,0:T(8,128)(2,1)S(1)} %collective-permute-done.6.fu.rest_3_, bf16[256,1024]{1,0:T(8,128)(2,1)S(1)} %collective-permute-done.7.fl.rest_4_, ...), custom_call_target="tpu_custom_call" | custom-call | flops 4255000064 | bytes 1000 | tf_op jit(solution)/shard_map/end_values/pallas_call | solution.py:274
  64.7 5.6 %weight_terms.1 = (f32[4,8,32,512]{3,2,1,0:T(8,128)}, f32[4,8,32,512]{3,2,1,0:T(8,128)}) custom-call(s32[3]{0:T(128)S(1)} %pad_add_fusion.place, f32[1024,256]{1,0:T(8,128)S(1)} %get-tuple-element.31.near_a, f32[1024,256]{1,0:T(8,128)S(1)} %get-tuple-element.33.near_b, bf16[1024,512]{1,0:T(8,128)(2,1)S(1)} %copy-done.4, ...), custom_call_target="tpu_custom_call" | custom-call | flops 5750000128 | bytes 1000 | tf_op jit(solution)/shard_map/weight_terms/pallas_call | solution.py:348
  70.6 2.1 %collective-permute-start.10 = (bf16[2,128,128]{2,1,0:T(8,128)(2,1)S(1)}, bf16[2,128,128]{2,1,0:T(8,128)(2,1)S(1)}, u32[]{:S(2)}, u32[]{:S(2)}) collective-permute-start(bf16[2,128,128]{2,1,0:T(8,128)(2,1)S(1)} %fusion.20.rest_5_), channel_id=1, source_target_pairs={{0,16},{8,24},{16,0},{24,8},{1,17},{9,25},{17,1},{25,9},{2,18},{10... | collective-permute-start | bytes 196616 | tf_op jit(solution)/shard_map/ppermute | solution.py:32
  73.6 2.4 %collective-permute-start.9 = (bf16[2,128,128]{2,1,0:T(8,128)(2,1)S(1)}, bf16[2,128,128]{2,1,0:T(8,128)(2,1)S(1)}, u32[]{:S(2)}, u32[]{:S(2)}) collective-permute-start(bf16[2,128,128]{2,1,0:T(8,128)(2,1)S(1)} %fusion.20.rest_5_), channel_id=1, source_target_pairs={{0,8},{8,16},{16,24},{24,0},{1,9},{9,17},{17,25},{25,1},{2,10},{10... | collective-permute-start | bytes 196616 | tf_op jit(solution)/shard_map/ppermute | solution.py:32
  76.5 1.8 %collective-permute-done.11 = bf16[2,128,128]{2,1,0:T(8,128)(2,1)S(1)} collective-permute-done((bf16[2,128,128]{2,1,0:T(8,128)(2,1)S(1)}, bf16[2,128,128]{2,1,0:T(8,128)(2,1)S(1)}, u32[]{:S(2)}, u32[]{:S(2)}) %collective-permute-start.11) | collective-permute-done | bytes 65568 | tf_op jit(solution)/shard_map/ppermute | solution.py:32
  78.3 3.0 %pair_sums.1 = (f32[8,32,512]{2,1,0:T(8,128)S(1)}, bf16[8,32,512]{2,1,0:T(8,128)(2,1)S(1)}, bf16[8,32,512]{2,1,0:T(8,128)(2,1)S(1)}, bf16[8,32,512]{2,1,0:T(8,128)(2,1)S(1)}) custom-call(s32[3]{0:T(128)S(1)} %pad_add_fusion.place, f32[4,8,32,512]{3,2,1,0:T(8,128)} %get-tuple-element.43.kept_u.kept_l, f32[4,8,32,512]{3,2,1,0:T(8,128)} %get-tuple-element.43.kept_u.kept_l, ...), custom_call_target="tpu_custom_call" | custom-call | flops 1264999936 | bytes 1000 | tf_op jit(solution)/shard_map/pair_sums/pallas_call | solution.py:393
  81.3 3.3 %collective-permute-start.20 = (bf16[8,32,512]{2,1,0:T(8,128)(2,1)S(1)}, bf16[8,32,512]{2,1,0:T(8,128)(2,1)S(1)}, u32[]{:S(2)}, u32[]{:S(2)}) collective-permute-start(bf16[8,32,512]{2,1,0:T(8,128)(2,1)S(1)} %get-tuple-element.47), channel_id=1, source_target_pairs={{0,8},{8,16},{16,24},{24,0},{1,9},{9,17},{17,25},{25,1},{2,10},{10... | collective-permute-start | bytes 786440 | tf_op jit(solution)/shard_map/ppermute | solution.py:32
  85.2 3.8 %collective-permute-done.19 = bf16[2,128,128]{2,1,0:T(8,128)(2,1)S(1)} collective-permute-done((bf16[2,128,128]{2,1,0:T(8,128)(2,1)S(1)}, bf16[2,128,128]{2,1,0:T(8,128)(2,1)S(1)}, u32[]{:S(2)}, u32[]{:S(2)}) %collective-permute-start.19) | collective-permute-done | bytes 65568 | tf_op jit(solution)/shard_map/ppermute | solution.py:36
  89.0 3.4 %collective-permute-start.21 = (bf16[2,128,128]{2,1,0:T(8,128)(2,1)S(1)}, bf16[2,128,128]{2,1,0:T(8,128)(2,1)S(1)}, u32[]{:S(2)}, u32[]{:S(2)}) collective-permute-start(bf16[2,128,128]{2,1,0:T(8,128)(2,1)S(1)} %fusion.13.rest_6_), channel_id=1, source_target_pairs={{0,64},{32,96},{64,0},{96,32},{128,192},{160,224},{192,128},{224,1... | collective-permute-start | bytes 196616 | tf_op jit(solution)/shard_map/ppermute | solution.py:36
  93.5 3.9 %collective-permute-start.25 = (bf16[8,32,512]{2,1,0:T(8,128)(2,1)S(1)}, bf16[8,32,512]{2,1,0:T(8,128)(2,1)S(1)}, u32[]{:S(2)}, u32[]{:S(2)}) collective-permute-start(bf16[8,32,512]{2,1,0:T(8,128)(2,1)S(1)} %get-tuple-element.51), channel_id=1, source_target_pairs={{0,16},{8,24},{16,0},{24,8},{1,17},{9,25},{17,1},{25,9},{2,18},{10... | collective-permute-start | bytes 786440 | tf_op jit(solution)/shard_map/ppermute | solution.py:32
  97.4 7.2 %begin_attended.1.total_u.total_l = f32[4,128,1024]{2,1,0:T(8,128)} custom-call(s32[3]{0:T(128)S(1)} %pad_add_fusion.place, bf16[4,128,1024]{2,1,0:T(8,128)(2,1)} %get-tuple-element.27.turned_ref, bf16[17,4,1024]{2,1,0:T(4,128)(2,1)S(1)} %copy-done, bf16[512,1024]{1,0:T(8,128)(2,1)} %get-tuple-element.35.v_ref, ...), custom_call_target="tpu_custom_call" | custom-call | flops 345000000 | bytes 1000 | tf_op jit(solution)/shard_map/begin_attended/pallas_call | solution.py:463
  104.7 6.4 %collective-permute-start.22 = (bf16[2,128,128]{2,1,0:T(8,128)(2,1)S(1)}, bf16[2,128,128]{2,1,0:T(8,128)(2,1)S(1)}, u32[]{:S(2)}, u32[]{:S(2)}) collective-permute-start(bf16[2,128,128]{2,1,0:T(8,128)(2,1)S(1)} %get-tuple-element.49), channel_id=1, source_target_pairs={{0,128},{32,160},{64,192},{96,224},{1,129},{33,161},{65,193},{97,2... | collective-permute-start | bytes 196616 | tf_op jit(solution)/shard_map/ppermute | solution.py:602
  111.9 3.4 %all-to-all-start = ((bf16[8,32,512]{2,1,0:T(8,128)(2,1)}), bf16[8,32,512]{2,1,0:T(8,128)(2,1)S(1)}, u32[]{:S(2)}, u32[]{:S(2)}) async-start(bf16[8,32,512]{2,1,0:T(8,128)(2,1)} %add_convert_fusion), calls=%async_computation | async-start | bytes 524288 | tf_op jit(solution)/shard_map/all_to_all | solution.py:603
  115.5 1.4 %collective-permute-done.23 = bf16[3,2,128,128]{3,2,1,0:T(8,128)(2,1)S(1)} collective-permute-done((bf16[3,2,128,128]{3,2,1,0:T(8,128)(2,1)S(1)}, bf16[3,2,128,128]{3,2,1,0:T(8,128)(2,1)S(1)}, u32[]{:S(2)}, u32[]{:S(2)}) %collective-permute-start.23) | collective-permute-done | bytes 196640 | tf_op jit(solution)/shard_map/ppermute | solution.py:36
  117.0 5.1 %end_attended.1 = bf16[1024,512]{1,0:T(8,128)(2,1)} custom-call(s32[3]{0:T(128)S(1)} %pad_add_fusion.place, bf16[4,128,1024]{2,1,0:T(8,128)(2,1)} %get-tuple-element.27.turned_ref, bf16[17,4,1024]{2,1,0:T(4,128)(2,1)S(1)} %copy-done, f32[4,128,1024]{2,1,0:T(8,128)} %begin_attended.1.total_u.total_l, f32[4,128,1024]{2,1,0:T(8,128)} %begin_attended.1.total_u.total_l, ...), custom_call_target="tpu_custom_call" | custom-call | flops 345000000 | bytes 1000 | tf_op jit(solution)/shard_map/end_attended/pallas_call | solution.py:502
  122.1 3.7 %all-to-all-done = bf16[8,32,512]{2,1,0:T(8,128)(2,1)S(1)} async-done(((bf16[8,32,512]{2,1,0:T(8,128)(2,1)}), bf16[8,32,512]{2,1,0:T(8,128)(2,1)S(1)}, u32[]{:S(2)}, u32[]{:S(2)}) %all-to-all-start) | async-done | bytes 262176 | tf_op jit(solution)/shard_map/all_to_all | solution.py:603
  (66 shorter events, 13.9 us)
Async XLA Ops:
  6.6 5.6 %copy-start.2 = (bf16[1024,512]{1,0:T(8,128)(2,1)S(1)}, bf16[1024,512]{1,0:T(8,128)(2,1)}, u32[]{:S(2)}) copy-start(bf16[1024,512]{1,0:T(8,128)(2,1)} %in_ref.2) | copy-start | bytes 3145732
  6.6 2.1 %collective-permute-start = (f32[5,2,128,128]{3,2,1,0:T(8,128)S(1)}, f32[5,2,128,128]{3,2,1,0:T(8,128)S(1)}, u32[]{:S(2)}, u32[]{:S(2)}) collective-permute-start(f32[5,2,128,128]{3,2,1,0:T(8,128)S(1)} %get-tuple-element.29), channel_id=1, source_target_pairs={{0,4},{4,0},{1,5},{5,1},{2,6},{6,2},{3,7},{7,3},{8,12},{12,8},{9,1... | collective-permute-start | bytes 1966088 | tf_op jit(solution)/shard_map/ppermute | solution.py:36
  8.8 7.2 %collective-permute-start.3 = (bf16[3,2,128,128]{3,2,1,0:T(8,128)(2,1)S(1)}, bf16[3,2,128,128]{3,2,1,0:T(8,128)(2,1)S(1)}, u32[]{:S(2)}, u32[]{:S(2)}) collective-permute-start(bf16[3,2,128,128]{3,2,1,0:T(8,128)(2,1)S(1)} %slice.139.rest_0_), channel_id=1, source_target_pairs={{0,32},{32,0},{64,96},{96,64},{128,160},{160,128},{192,224},{224,1... | collective-permute-start | bytes 589832 | tf_op jit(solution)/shard_map/ppermute | solution.py:36
  10.8 33.7 %collective-permute-start.16 = (f32[4,128,128]{2,1,0:T(8,128)S(1)}, f32[4,128,128]{2,1,0:T(8,128)S(1)}, u32[]{:S(2)}, u32[]{:S(2)}) collective-permute-start(f32[4,128,128]{2,1,0:T(8,128)S(1)} %get-tuple-element.41), channel_id=1, source_target_pairs={{4,0},{5,1},{6,2},{7,3},{12,8},{13,9},{14,10},{15,11},{20,16},{21,... | collective-permute-start | bytes 786440 | tf_op jit(solution)/shard_map/ppermute | solution.py:553
  12.2 7.3 %copy-start = (bf16[17,4,1024]{2,1,0:T(4,128)(2,1)S(1)}, bf16[17,4,1024]{2,1,0:T(4,128)(2,1)}, u32[]{:S(2)}) copy-start(bf16[17,4,1024]{2,1,0:T(4,128)(2,1)} %lw_ref.9) | copy-start | bytes 417796
  12.2 7.3 %copy-start.3 = (bf16[1024,512]{1,0:T(8,128)(2,1)S(1)}, bf16[1024,512]{1,0:T(8,128)(2,1)}, u32[]{:S(2)}) copy-start(bf16[1024,512]{1,0:T(8,128)(2,1)} %g_ref.3) | copy-start | bytes 3145732
  12.2 7.3 %copy-start.4 = (bf16[1024,512]{1,0:T(8,128)(2,1)S(1)}, bf16[1024,512]{1,0:T(8,128)(2,1)}, u32[]{:S(2)}) copy-start(bf16[1024,512]{1,0:T(8,128)(2,1)} %k_ref.7) | copy-start | bytes 3145732
  12.8 25.9 %collective-permute-start.1 = (bf16[512,1024]{1,0:T(8,128)(2,1)S(1)}, bf16[512,1024]{1,0:T(8,128)(2,1)S(1)}, u32[]{:S(2)}, u32[]{:S(2)}) collective-permute-start(bf16[512,1024]{1,0:T(8,128)(2,1)S(1)} %turn_features.1.own.rest_0_), channel_id=1, source_target_pairs={{0,1},{1,2},{2,3},{3,0},{4,5},{5,6},{6,7},{7,4},{8,9},{9,10},{10,1... | collective-permute-start | bytes 3145736 | tf_op jit(solution)/shard_map/ppermute | solution.py:32
  13.1 27.2 %collective-permute-start.2 = (bf16[512,1024]{1,0:T(8,128)(2,1)S(1)}, bf16[512,1024]{1,0:T(8,128)(2,1)S(1)}, u32[]{:S(2)}, u32[]{:S(2)}) collective-permute-start(bf16[512,1024]{1,0:T(8,128)(2,1)S(1)} %turn_features.1.own.rest_0_), channel_id=1, source_target_pairs={{0,3},{1,0},{2,1},{3,2},{4,7},{5,4},{6,5},{7,6},{8,11},{9,8},{10,9... | collective-permute-start | bytes 3145736 | tf_op jit(solution)/shard_map/ppermute | solution.py:32
  16.1 9.5 %collective-permute-start.4 = (bf16[2,2,128,128]{3,2,1,0:T(8,128)(2,1)S(1)}, bf16[2,2,128,128]{3,2,1,0:T(8,128)(2,1)S(1)}, u32[]{:S(2)}, u32[]{:S(2)}) collective-permute-start(bf16[2,2,128,128]{3,2,1,0:T(8,128)(2,1)S(1)} %pad_maximum_fusion.3.rest_0_), channel_id=1, source_target_pairs={{0,64},{32,96},{64,0},{96,32},{128,192},{160,224},{192,128},{224,1... | collective-permute-start | bytes 393224 | tf_op jit(solution)/shard_map/ppermute | solution.py:36
  19.4 5.2 %copy-start.1 = (bf16[2048,512]{1,0:T(8,128)(2,1)S(1)}, bf16[2048,512]{1,0:T(8,128)(2,1)}, u32[]{:S(2)}) copy-start(bf16[2048,512]{1,0:T(8,128)(2,1)} %in_ref.3) | copy-start | bytes 6291460
  25.6 10.1 %collective-permute-start.5 = (bf16[2,128,128]{2,1,0:T(8,128)(2,1)S(1)}, bf16[2,128,128]{2,1,0:T(8,128)(2,1)S(1)}, u32[]{:S(2)}, u32[]{:S(2)}) collective-permute-start(bf16[2,128,128]{2,1,0:T(8,128)(2,1)S(1)} %fusion.15.rest_0_), channel_id=1, source_target_pairs={{128,0},{160,32},{192,64},{224,96},{129,1},{161,33},{193,65},{225,... | collective-permute-start | bytes 196616 | tf_op jit(solution)/shard_map/ppermute | solution.py:558
  40.4 9.5 %collective-permute-start.13 = (bf16[2,128,128]{2,1,0:T(8,128)(2,1)S(1)}, bf16[2,128,128]{2,1,0:T(8,128)(2,1)S(1)}, u32[]{:S(2)}, u32[]{:S(2)}) collective-permute-start(bf16[2,128,128]{2,1,0:T(8,128)(2,1)S(1)} %get-tuple-element.56), channel_id=1, source_target_pairs={{0,8},{8,16},{16,24},{24,0},{1,9},{9,17},{17,25},{25,1},{2,10},{10... | collective-permute-start | bytes 196616 | tf_op jit(solution)/shard_map/ppermute | solution.py:32
  41.0 9.0 %collective-permute-start.14 = (bf16[2,128,128]{2,1,0:T(8,128)(2,1)S(1)}, bf16[2,128,128]{2,1,0:T(8,128)(2,1)S(1)}, u32[]{:S(2)}, u32[]{:S(2)}) collective-permute-start(bf16[2,128,128]{2,1,0:T(8,128)(2,1)S(1)} %get-tuple-element.57), channel_id=1, source_target_pairs={{0,24},{8,0},{16,8},{24,16},{1,25},{9,1},{17,9},{25,17},{2,26},{10... | collective-permute-start | bytes 196616 | tf_op jit(solution)/shard_map/ppermute | solution.py:32
  42.6 7.4 %collective-permute-start.15 = (bf16[2,128,128]{2,1,0:T(8,128)(2,1)S(1)}, bf16[2,128,128]{2,1,0:T(8,128)(2,1)S(1)}, u32[]{:S(2)}, u32[]{:S(2)}) collective-permute-start(bf16[2,128,128]{2,1,0:T(8,128)(2,1)S(1)} %fusion.12.rest_0_), channel_id=1, source_target_pairs={{0,16},{8,24},{16,0},{24,8},{1,17},{9,25},{17,1},{25,9},{2,18},{10... | collective-permute-start | bytes 196616 | tf_op jit(solution)/shard_map/ppermute | solution.py:32
  44.1 13.2 %collective-permute-start.6 = (bf16[256,1024]{1,0:T(8,128)(2,1)S(1)}, bf16[256,1024]{1,0:T(8,128)(2,1)S(1)}, u32[]{:S(2)}, u32[]{:S(2)}) collective-permute-start(bf16[256,1024]{1,0:T(8,128)(2,1)S(1)} %slice.79), channel_id=1, source_target_pairs={{0,1},{1,2},{2,3},{3,0},{4,5},{5,6},{6,7},{7,4},{8,9},{9,10},{10,1... | collective-permute-start | bytes 1572872 | tf_op jit(solution)/shard_map/ppermute | solution.py:32
  44.5 14.3 %collective-permute-start.7 = (bf16[256,1024]{1,0:T(8,128)(2,1)S(1)}, bf16[256,1024]{1,0:T(8,128)(2,1)S(1)}, u32[]{:S(2)}, u32[]{:S(2)}) collective-permute-start(bf16[256,1024]{1,0:T(8,128)(2,1)S(1)} %slice.80), channel_id=1, source_target_pairs={{0,3},{1,0},{2,1},{3,2},{4,7},{5,4},{6,5},{7,6},{8,11},{9,8},{10,9... | collective-permute-start | bytes 1572872 | tf_op jit(solution)/shard_map/ppermute | solution.py:32
  62.9 1.3 %collective-permute-start.17 = (f32[2,128,128]{2,1,0:T(8,128)S(1)}, f32[2,128,128]{2,1,0:T(8,128)S(1)}, u32[]{:S(2)}, u32[]{:S(2)}) collective-permute-start(f32[2,128,128]{2,1,0:T(8,128)S(1)} %get-tuple-element.42), channel_id=1, source_target_pairs={{0,4},{4,0},{1,5},{5,1},{2,6},{6,2},{3,7},{7,3},{8,12},{12,8},{9,1... | collective-permute-start | bytes 393224 | tf_op jit(solution)/shard_map/ppermute | solution.py:36
  62.9 1.7 %collective-permute-start.8 = (f32[4,128,128]{2,1,0:T(8,128)S(1)}, f32[4,128,128]{2,1,0:T(8,128)S(1)}, u32[]{:S(2)}, u32[]{:S(2)}) collective-permute-start(f32[4,128,128]{2,1,0:T(8,128)S(1)} %get-tuple-element.40), channel_id=1, source_target_pairs={{0,4},{4,0},{1,5},{5,1},{2,6},{6,2},{3,7},{7,3},{8,12},{12,8},{9,1... | collective-permute-start | bytes 786440 | tf_op jit(solution)/shard_map/ppermute | solution.py:36
  70.3 8.0 %collective-permute-start.18 = (f32[4,8,32,512]{3,2,1,0:T(8,128)}, f32[4,8,32,512]{3,2,1,0:T(8,128)S(1)}, u32[]{:S(2)}, u32[]{:S(2)}) collective-permute-start(f32[4,8,32,512]{3,2,1,0:T(8,128)} %get-tuple-element.44), channel_id=1, source_target_pairs={{0,4},{4,0},{1,5},{5,1},{2,6},{6,2},{3,7},{7,3},{8,12},{12,8},{9,1... | collective-permute-start | bytes 6291464 | tf_op jit(solution)/shard_map/ppermute | solution.py:36
  70.6 5.8 %collective-permute-start.10 = (bf16[2,128,128]{2,1,0:T(8,128)(2,1)S(1)}, bf16[2,128,128]{2,1,0:T(8,128)(2,1)S(1)}, u32[]{:S(2)}, u32[]{:S(2)}) collective-permute-start(bf16[2,128,128]{2,1,0:T(8,128)(2,1)S(1)} %fusion.20.rest_5_), channel_id=1, source_target_pairs={{0,16},{8,24},{16,0},{24,8},{1,17},{9,25},{17,1},{25,9},{2,18},{10... | collective-permute-start | bytes 196616 | tf_op jit(solution)/shard_map/ppermute | solution.py:32
  72.7 5.5 %collective-permute-start.11 = (bf16[2,128,128]{2,1,0:T(8,128)(2,1)S(1)}, bf16[2,128,128]{2,1,0:T(8,128)(2,1)S(1)}, u32[]{:S(2)}, u32[]{:S(2)}) collective-permute-start(bf16[2,128,128]{2,1,0:T(8,128)(2,1)S(1)} %fusion.20.rest_5_), channel_id=1, source_target_pairs={{0,24},{8,0},{16,8},{24,16},{1,25},{9,1},{17,9},{25,17},{2,26},{10... | collective-permute-start | bytes 196616 | tf_op jit(solution)/shard_map/ppermute | solution.py:32
  73.6 4.6 %collective-permute-start.9 = (bf16[2,128,128]{2,1,0:T(8,128)(2,1)S(1)}, bf16[2,128,128]{2,1,0:T(8,128)(2,1)S(1)}, u32[]{:S(2)}, u32[]{:S(2)}) collective-permute-start(bf16[2,128,128]{2,1,0:T(8,128)(2,1)S(1)} %fusion.20.rest_5_), channel_id=1, source_target_pairs={{0,8},{8,16},{16,24},{24,0},{1,9},{9,17},{17,25},{25,1},{2,10},{10... | collective-permute-start | bytes 196616 | tf_op jit(solution)/shard_map/ppermute | solution.py:32
  81.3 7.6 %collective-permute-start.20 = (bf16[8,32,512]{2,1,0:T(8,128)(2,1)S(1)}, bf16[8,32,512]{2,1,0:T(8,128)(2,1)S(1)}, u32[]{:S(2)}, u32[]{:S(2)}) collective-permute-start(bf16[8,32,512]{2,1,0:T(8,128)(2,1)S(1)} %get-tuple-element.47), channel_id=1, source_target_pairs={{0,8},{8,16},{16,24},{24,0},{1,9},{9,17},{17,25},{25,1},{2,10},{10... | collective-permute-start | bytes 786440 | tf_op jit(solution)/shard_map/ppermute | solution.py:32
  84.7 4.3 %collective-permute-start.19 = (bf16[2,128,128]{2,1,0:T(8,128)(2,1)S(1)}, bf16[2,128,128]{2,1,0:T(8,128)(2,1)S(1)}, u32[]{:S(2)}, u32[]{:S(2)}) collective-permute-start(bf16[2,128,128]{2,1,0:T(8,128)(2,1)S(1)} %get-tuple-element.46), channel_id=1, source_target_pairs={{0,32},{32,0},{64,96},{96,64},{128,160},{160,128},{192,224},{224,1... | collective-permute-start | bytes 196616 | tf_op jit(solution)/shard_map/ppermute | solution.py:36
  85.1 7.3 %collective-permute-start.12 = (bf16[2,2,128,128]{3,2,1,0:T(8,128)(2,1)S(1)}, bf16[2,2,128,128]{3,2,1,0:T(8,128)(2,1)S(1)}, u32[]{:S(2)}, u32[]{:S(2)}) collective-permute-start(bf16[2,2,128,128]{3,2,1,0:T(8,128)(2,1)S(1)} %pad_maximum_fusion.4), channel_id=1, source_target_pairs={{0,4},{4,0},{1,5},{5,1},{2,6},{6,2},{3,7},{7,3},{8,12},{12,8},{9,1... | collective-permute-start | bytes 393224 | tf_op jit(solution)/shard_map/ppermute | solution.py:36
  89.0 15.7 %collective-permute-start.21 = (bf16[2,128,128]{2,1,0:T(8,128)(2,1)S(1)}, bf16[2,128,128]{2,1,0:T(8,128)(2,1)S(1)}, u32[]{:S(2)}, u32[]{:S(2)}) collective-permute-start(bf16[2,128,128]{2,1,0:T(8,128)(2,1)S(1)} %fusion.13.rest_6_), channel_id=1, source_target_pairs={{0,64},{32,96},{64,0},{96,32},{128,192},{160,224},{192,128},{224,1... | collective-permute-start | bytes 196616 | tf_op jit(solution)/shard_map/ppermute | solution.py:36
  92.3 18.7 %collective-permute-start.24 = (bf16[8,32,512]{2,1,0:T(8,128)(2,1)S(1)}, bf16[8,32,512]{2,1,0:T(8,128)(2,1)S(1)}, u32[]{:S(2)}, u32[]{:S(2)}) collective-permute-start(bf16[8,32,512]{2,1,0:T(8,128)(2,1)S(1)} %get-tuple-element.50), channel_id=1, source_target_pairs={{0,24},{8,0},{16,8},{24,16},{1,25},{9,1},{17,9},{25,17},{2,26},{10... | collective-permute-start | bytes 786440 | tf_op jit(solution)/shard_map/ppermute | solution.py:32
  93.5 17.6 %collective-permute-start.25 = (bf16[8,32,512]{2,1,0:T(8,128)(2,1)S(1)}, bf16[8,32,512]{2,1,0:T(8,128)(2,1)S(1)}, u32[]{:S(2)}, u32[]{:S(2)}) collective-permute-start(bf16[8,32,512]{2,1,0:T(8,128)(2,1)S(1)} %get-tuple-element.51), channel_id=1, source_target_pairs={{0,16},{8,24},{16,0},{24,8},{1,17},{9,25},{17,1},{25,9},{2,18},{10... | collective-permute-start | bytes 786440 | tf_op jit(solution)/shard_map/ppermute | solution.py:32
  104.7 10.7 %collective-permute-start.22 = (bf16[2,128,128]{2,1,0:T(8,128)(2,1)S(1)}, bf16[2,128,128]{2,1,0:T(8,128)(2,1)S(1)}, u32[]{:S(2)}, u32[]{:S(2)}) collective-permute-start(bf16[2,128,128]{2,1,0:T(8,128)(2,1)S(1)} %get-tuple-element.49), channel_id=1, source_target_pairs={{0,128},{32,160},{64,192},{96,224},{1,129},{33,161},{65,193},{97,2... | collective-permute-start | bytes 196616 | tf_op jit(solution)/shard_map/ppermute | solution.py:602
  111.9 13.8 %all-to-all-start = ((bf16[8,32,512]{2,1,0:T(8,128)(2,1)}), bf16[8,32,512]{2,1,0:T(8,128)(2,1)S(1)}, u32[]{:S(2)}, u32[]{:S(2)}) async-start(bf16[8,32,512]{2,1,0:T(8,128)(2,1)} %add_convert_fusion), calls=%async_computation | async-start | bytes 524288 | tf_op jit(solution)/shard_map/all_to_all | solution.py:603
  115.4 1.5 %collective-permute-start.23 = (bf16[3,2,128,128]{3,2,1,0:T(8,128)(2,1)S(1)}, bf16[3,2,128,128]{3,2,1,0:T(8,128)(2,1)S(1)}, u32[]{:S(2)}, u32[]{:S(2)}) collective-permute-start(bf16[3,2,128,128]{3,2,1,0:T(8,128)(2,1)S(1)} %pad_maximum_fusion.2), channel_id=1, source_target_pairs={{0,4},{4,0},{1,5},{5,1},{2,6},{6,2},{3,7},{7,3},{8,12},{12,8},{9,1... | collective-permute-start | bytes 589832 | tf_op jit(solution)/shard_map/ppermute | solution.py:36
